TPU v7x, 32 devices: a whole 2x2x4 slice. The times are simulated.
32 devices in a mesh: wide: 4 (over z), narrow: 8 (over y, x, core).
Axes of the slice: x: 2, y: 2, z: 4, core: 2. Of those that a mesh axis runs over, the one named last changes fastest.
Arguments:
- layer_in: bfloat16 [8, 1024, 1536], P('wide', 'narrow'), may hold values from -6 to 6
- seg_ids: int32 [8, 1024], P('wide', 'narrow'), may hold values from 1 to 1025, as said below
- pad_mask: int32 [8, 1024], P('wide', 'narrow'), may hold values from 0 to 1, as said below
- gain_attn: bfloat16 [1536], P(('wide', 'narrow')), may hold values from 0.5 to 1.5
- w_query: bfloat16 [1536, 1536], P(('wide', 'narrow')), may hold values from -0.15625 to 0.15625
- b_query: bfloat16 [1536], P(('wide', 'narrow')), may hold values from -3 to 3
- w_key: bfloat16 [1536, 256], P(('wide', 'narrow')), may hold values from -0.15625 to 0.15625
- b_key: bfloat16 [256], P(('wide', 'narrow')), may hold values from -3 to 3
- w_value: bfloat16 [1536, 256], P(('wide', 'narrow')), may hold values from -0.15625 to 0.15625
- b_value: bfloat16 [256], P(('wide', 'narrow')), may hold values from -3 to 3
- w_out: bfloat16 [1536, 1536], P(('wide', 'narrow')), may hold values from -1.25 to 1.25
- gain_mlp: bfloat16 [1536], P(('wide', 'narrow')), may hold values from 0.5 to 1.5
- w_gate: bfloat16 [1536, 8960], P('wide', 'narrow'), may hold values from -0.15625 to 0.15625
- w_up: bfloat16 [1536, 8960], P('wide', 'narrow'), may hold values from -0.15625 to 0.15625
- w_down: bfloat16 [8960, 1536], P('narrow', 'wide'), may hold values from -0.09375 to 0.09375
- grad_out: bfloat16 [8, 1024, 1536], P('wide', 'narrow'), may hold values from -6 to 6
Outputs:
- layer_out: bfloat16 [8, 1024, 1536], P('wide', 'narrow')
- grad_in: bfloat16 [8, 1024, 1536], P('wide', 'narrow')
- grad_gain_attn: float32 [1536], P(('wide', 'narrow'))
- grad_w_query: float32 [1536, 1536], P(('wide', 'narrow'))
- grad_b_query: float32 [1536], P(('wide', 'narrow'))
- grad_w_key: float32 [1536, 256], P(('wide', 'narrow'))
- grad_b_key: float32 [256], P(('wide', 'narrow'))
- grad_w_value: float32 [1536, 256], P(('wide', 'narrow'))
- grad_b_value: float32 [256], P(('wide', 'narrow'))
- grad_w_out: float32 [1536, 1536], P(('wide', 'narrow'))
- grad_gain_mlp: float32 [1536], P(('wide', 'narrow'))
- grad_w_gate: float32 [1536, 8960], P('wide', 'narrow')
- grad_w_up: float32 [1536, 8960], P('wide', 'narrow')
- grad_w_down: float32 [8960, 1536], P('narrow', 'wide')
Inputs may be any that keep to these rules, and one draw needn't show every extreme that they name: `seg_ids`: along each row the numbers start at 1 and never fall; padding tokens carry the number 1024 + 1, above every real document. Among the 2 rows of each index of wide, one row is a single document covering all but 1 to 127 of its tokens. `pad_mask`: each row is 1 up to its valid length and 0 after it.
All inputs are finite; a program needn't handle non-finite values.
Results may differ from a plain program's by a relative error of at most 0.023.
Values may be sent and summed in bfloat16 or wider, within the bound.
No kernel may reach another device: no remote copies, remote signals or barrier semaphores. Data moves between devices by JAX's collectives and lax.ppermute only.
A program may use at most 384 MiB of HBM per device.

v0:
```python
import math

import jax
import jax.numpy as jnp
from jax import lax
from jax.sharding import PartitionSpec as P

Q_HEADS = 12
KV_HEADS = 2
HEAD = 128
HQ = 1536
HK = 256


EPS = 1e-06
THETA = 10000.0


def norm_parts(value):
    factor = lax.rsqrt(jnp.mean(value * value, axis=-1, keepdims=True) + EPS)
    return (value * factor, factor)


def norm_back(grad, unit, factor, gain):
    scaled = grad * gain
    return factor * (scaled - unit * jnp.mean(scaled * unit, axis=-1, keepdims=True))


def rotate(value, cosine, sine):
    half = value.shape[-1] // 2
    first = value[..., :half]
    second = value[..., half:]
    return jnp.concatenate(
        [first * cosine - second * sine, second * cosine + first * sine], axis=-1
    )


def angles(places, head_size):
    freq = jnp.exp(
        jnp.arange(head_size // 2, dtype=jnp.float32) * (-2.0 * math.log(THETA) / head_size)
    )
    turn = places.astype(jnp.float32)[..., None] * freq
    return (jnp.cos(turn), jnp.sin(turn))


def row_probs(query, keys, allowed, scale):
    scores = jnp.einsum("qhgd,khd->hgqk", query, keys, preferred_element_type=jnp.float32) * scale
    scores = jnp.where(allowed[None, None], scores, -1e30)
    top = jnp.max(scores, axis=-1, keepdims=True)
    expo = jnp.exp(scores - top)
    return expo / jnp.sum(expo, axis=-1, keepdims=True)


def swiglu_back(d_hidden, gate, up):
    sigma = jax.nn.sigmoid(gate)
    active = gate * sigma
    d_gate = (d_hidden * up * sigma * (1.0 + gate * (1.0 - sigma))).astype(jnp.bfloat16)
    d_up = (d_hidden * active).astype(jnp.bfloat16)
    return (d_gate, d_up)


def on_device(
    layer_in,
    seg_ids,
    pad_mask,
    gain_attn,
    w_query,
    b_query,
    w_key,
    b_key,
    w_value,
    b_value,
    w_out,
    gain_mlp,
    w_gate,
    w_up,
    w_down,
    grad_out,
):
    rows, seg_len, width = layer_in.shape
    parts = lax.axis_size("narrow")
    row_len = seg_len * parts
    me = lax.axis_index("narrow")
    group = Q_HEADS // KV_HEADS
    scale = 1.0 / math.sqrt(HEAD)
    f32 = jnp.float32
    bf16 = jnp.bfloat16
    ids_all, pads_all = (
        lax.all_gather(seg_ids, "narrow", axis=1, tiled=True),
        lax.all_gather(pad_mask, "narrow", axis=1, tiled=True),
    )
    wq, wk, wv, wo, g_one, g_two, bq, bk, bv = (
        lax.all_gather(w_query, ("wide", "narrow"), axis=0, tiled=True),
        lax.all_gather(w_key, ("wide", "narrow"), axis=0, tiled=True),
        lax.all_gather(w_value, ("wide", "narrow"), axis=0, tiled=True),
        lax.all_gather(w_out, ("wide", "narrow"), axis=0, tiled=True),
        lax.all_gather(gain_attn, ("wide", "narrow"), axis=0, tiled=True),
        lax.all_gather(gain_mlp, ("wide", "narrow"), axis=0, tiled=True),
        lax.all_gather(b_query, ("wide", "narrow"), axis=0, tiled=True),
        lax.all_gather(b_key, ("wide", "narrow"), axis=0, tiled=True),
        lax.all_gather(b_value, ("wide", "narrow"), axis=0, tiled=True),
    )
    wg, wu, wd = (
        lax.all_gather(w_gate, "wide", axis=0, tiled=True),
        lax.all_gather(w_up, "wide", axis=0, tiled=True),
        lax.all_gather(w_down, "wide", axis=1, tiled=True),
    )
    g_one = g_one.astype(f32)
    g_two = g_two.astype(f32)
    global_idx = me * seg_len + jnp.arange(seg_len, dtype=jnp.int32)
    begins = jnp.sum((ids_all[:, None, :] < seg_ids[:, :, None]).astype(jnp.int32), axis=-1)
    cosine, sine = angles(global_idx[None, :] - begins, HEAD)
    cosine = cosine[:, :, None, :]
    sine = sine[:, :, None, :]
    key_idx = jnp.arange(row_len, dtype=jnp.int32)
    allowed = (ids_all[:, None, :] == seg_ids[:, :, None]) & (
        key_idx[None, None, :] < global_idx[None, :, None]
    ) & (pads_all[:, None, :] == 1) | (key_idx[None, None, :] == global_idx[None, :, None])
    x_in = layer_in.astype(f32)
    unit_one, factor_one = norm_parts(x_in)
    h_one = (unit_one * g_one).astype(bf16)
    q_lin = jnp.dot(h_one, wq, preferred_element_type=f32) + bq.astype(f32)
    k_lin = jnp.dot(h_one, wk, preferred_element_type=f32) + bk.astype(f32)
    v_lin = jnp.dot(h_one, wv, preferred_element_type=f32) + bv.astype(f32)
    q_rot = rotate(q_lin.reshape(rows, seg_len, Q_HEADS, HEAD), cosine, sine).astype(bf16)
    k_rot = rotate(k_lin.reshape(rows, seg_len, KV_HEADS, HEAD), cosine, sine).astype(bf16)
    v_low = v_lin.astype(bf16)
    keys_all, values_all = (
        lax.all_gather(k_rot.reshape(rows, seg_len, HK), "narrow", axis=1, tiled=True),
        lax.all_gather(v_low, "narrow", axis=1, tiled=True),
    )
    keys_all = keys_all.reshape(rows, row_len, KV_HEADS, HEAD)
    values_all = values_all.reshape(rows, row_len, KV_HEADS, HEAD)
    queries = q_rot.reshape(rows, seg_len, KV_HEADS, group, HEAD)
    outputs = []
    for row in range(rows):
        probs = row_probs(queries[row], keys_all[row], allowed[row], scale)
        outputs.append(
            jnp.einsum(
                "hgqk,khd->qhgd", probs.astype(bf16), values_all[row], preferred_element_type=f32
            )
        )
    attended = jnp.stack(outputs).reshape(rows, seg_len, HQ).astype(bf16)
    x_mid = x_in + jnp.dot(attended, wo, preferred_element_type=f32)
    unit_two, factor_two = norm_parts(x_mid)
    h_two = (unit_two * g_two).astype(bf16)
    h_all = lax.all_gather(h_two, "narrow", axis=1, tiled=True)
    gate = jnp.dot(h_all, wg, preferred_element_type=f32)
    up = jnp.dot(h_all, wu, preferred_element_type=f32)
    hidden = (jax.nn.silu(gate) * up).astype(bf16)
    partial_value = jnp.dot(hidden, wd, preferred_element_type=f32)
    mixed = lax.psum_scatter(partial_value, "narrow", scatter_dimension=1, tiled=True)
    layer_out = (x_mid + mixed).astype(bf16)
    grad_all = lax.all_gather(grad_out, "narrow", axis=1, tiled=True)
    d_hidden = jnp.einsum("rtd,fd->rtf", grad_all, wd, preferred_element_type=f32)
    d_wd = jnp.einsum("rtf,rtd->fd", hidden, grad_all, preferred_element_type=f32)
    d_gate, d_up = swiglu_back(d_hidden, gate, up)
    d_wg = jnp.einsum("rtd,rtf->df", h_all, d_gate, preferred_element_type=f32)
    d_wu = jnp.einsum("rtd,rtf->df", h_all, d_up, preferred_element_type=f32)
    grad_w_gate, grad_w_up, grad_w_down = (
        lax.psum_scatter(d_wg, "wide", scatter_dimension=0, tiled=True),
        lax.psum_scatter(d_wu, "wide", scatter_dimension=0, tiled=True),
        lax.psum_scatter(d_wd, "wide", scatter_dimension=1, tiled=True),
    )
    d_h_part = jnp.einsum("rtf,df->rtd", d_gate, wg, preferred_element_type=f32) + jnp.einsum(
        "rtf,df->rtd", d_up, wu, preferred_element_type=f32
    )
    d_h_two = lax.psum_scatter(d_h_part, "narrow", scatter_dimension=1, tiled=True)
    d_g_two = jnp.sum(d_h_two * unit_two, axis=(0, 1))
    d_mid = grad_out.astype(f32) + norm_back(d_h_two, unit_two, factor_two, g_two)
    d_branch = d_mid.astype(bf16)
    d_wo = jnp.einsum("rsh,rsd->hd", attended, d_branch, preferred_element_type=f32)
    d_attended = jnp.einsum("rsd,hd->rsh", d_branch, wo, preferred_element_type=f32).astype(bf16)
    d_att_heads = d_attended.reshape(rows, seg_len, KV_HEADS, group, HEAD)
    query_grads = []
    key_grads = []
    value_grads = []
    for row in range(rows):
        probs = row_probs(queries[row], keys_all[row], allowed[row], scale)
        d_prob = jnp.einsum(
            "qhgd,khd->hgqk", d_att_heads[row], values_all[row], preferred_element_type=f32
        )
        delta = jnp.sum(probs * d_prob, axis=-1, keepdims=True)
        d_score = (scale * probs * (d_prob - delta)).astype(bf16)
        query_grads.append(
            jnp.einsum("hgqk,khd->qhgd", d_score, keys_all[row], preferred_element_type=f32)
        )
        key_grads.append(
            jnp.einsum("hgqk,qhgd->khd", d_score, queries[row], preferred_element_type=f32)
        )
        value_grads.append(
            jnp.einsum(
                "hgqk,qhgd->khd", probs.astype(bf16), d_att_heads[row], preferred_element_type=f32
            )
        )
    d_query = jnp.stack(query_grads).reshape(rows, seg_len, Q_HEADS, HEAD)
    d_keys_all = jnp.stack(key_grads).reshape(rows, row_len, HK)
    d_values_all = jnp.stack(value_grads).reshape(rows, row_len, HK)
    d_keys, d_values = (
        lax.psum_scatter(d_keys_all, "narrow", scatter_dimension=1, tiled=True),
        lax.psum_scatter(d_values_all, "narrow", scatter_dimension=1, tiled=True),
    )
    dq_lin = rotate(d_query, cosine, -sine).reshape(rows, seg_len, HQ).astype(bf16)
    dk_lin = (
        rotate(d_keys.reshape(rows, seg_len, KV_HEADS, HEAD), cosine, -sine)
        .reshape(rows, seg_len, HK)
        .astype(bf16)
    )
    dv_lin = d_values.astype(bf16)
    d_wq = jnp.einsum("rsd,rsh->dh", h_one, dq_lin, preferred_element_type=f32)
    d_wk = jnp.einsum("rsd,rsh->dh", h_one, dk_lin, preferred_element_type=f32)
    d_wv = jnp.einsum("rsd,rsh->dh", h_one, dv_lin, preferred_element_type=f32)
    d_bq = jnp.sum(dq_lin.astype(f32), axis=(0, 1))
    d_bk = jnp.sum(dk_lin.astype(f32), axis=(0, 1))
    d_bv = jnp.sum(dv_lin.astype(f32), axis=(0, 1))
    d_h_one = jnp.einsum("rsh,dh->rsd", dq_lin, wq, preferred_element_type=f32)
    d_h_one = d_h_one + jnp.einsum("rsh,dh->rsd", dk_lin, wk, preferred_element_type=f32)
    d_h_one = d_h_one + jnp.einsum("rsh,dh->rsd", dv_lin, wv, preferred_element_type=f32)
    d_g_one = jnp.sum(d_h_one * unit_one, axis=(0, 1))
    grad_in = (d_mid + norm_back(d_h_one, unit_one, factor_one, g_one)).astype(bf16)
    (
        grad_w_query,
        grad_w_key,
        grad_w_value,
        grad_w_out,
        grad_gain_attn,
        grad_gain_mlp,
        grad_b_query,
        grad_b_key,
        grad_b_value,
    ) = (
        lax.psum_scatter(d_wq, ("wide", "narrow"), scatter_dimension=0, tiled=True),
        lax.psum_scatter(d_wk, ("wide", "narrow"), scatter_dimension=0, tiled=True),
        lax.psum_scatter(d_wv, ("wide", "narrow"), scatter_dimension=0, tiled=True),
        lax.psum_scatter(d_wo, ("wide", "narrow"), scatter_dimension=0, tiled=True),
        lax.psum_scatter(d_g_one, ("wide", "narrow"), scatter_dimension=0, tiled=True),
        lax.psum_scatter(d_g_two, ("wide", "narrow"), scatter_dimension=0, tiled=True),
        lax.psum_scatter(d_bq, ("wide", "narrow"), scatter_dimension=0, tiled=True),
        lax.psum_scatter(d_bk, ("wide", "narrow"), scatter_dimension=0, tiled=True),
        lax.psum_scatter(d_bv, ("wide", "narrow"), scatter_dimension=0, tiled=True),
    )
    return (
        layer_out,
        grad_in,
        grad_gain_attn,
        grad_w_query,
        grad_b_query,
        grad_w_key,
        grad_b_key,
        grad_w_value,
        grad_b_value,
        grad_w_out,
        grad_gain_mlp,
        grad_w_gate,
        grad_w_up,
        grad_w_down,
    )


def solution(mesh):
    return jax.shard_map(
        on_device,
        mesh=mesh,
        in_specs=(
            P("wide", "narrow", None),
            P("wide", "narrow"),
            P("wide", "narrow"),
            P(("wide", "narrow")),
            P(("wide", "narrow"), None),
            P(("wide", "narrow")),
            P(("wide", "narrow"), None),
            P(("wide", "narrow")),
            P(("wide", "narrow"), None),
            P(("wide", "narrow")),
            P(("wide", "narrow"), None),
            P(("wide", "narrow")),
            P("wide", "narrow"),
            P("wide", "narrow"),
            P("narrow", "wide"),
            P("wide", "narrow", None),
        ),
        out_specs=(
            P("wide", "narrow", None),
            P("wide", "narrow", None),
            P(("wide", "narrow")),
            P(("wide", "narrow"), None),
            P(("wide", "narrow")),
            P(("wide", "narrow"), None),
            P(("wide", "narrow")),
            P(("wide", "narrow"), None),
            P(("wide", "narrow")),
            P(("wide", "narrow"), None),
            P(("wide", "narrow")),
            P("wide", "narrow"),
            P("wide", "narrow"),
            P("narrow", "wide"),
        ),
        check_vma=False,
    )
```

profile of v0, /device:TPU:0, one launch (start us, length us, event | category | flops | bytes accessed | tf_op | source)
XLA Modules:
  0.0 1824.1 jit_solution(10996955170616263083)
XLA Ops:
  11.5 42.2 %all-reduce.11 = (bf16[256]{0:T(256)(128)(2,1)S(1)}, bf16[1536]{0:T(1024)(128)(2,1)S(1)}, bf16[256]{0:T(256)(128)(2,1)S(1)}, bf16[1536]{0:T(1024)(128)(2,1)S(1)}, bf16[1536]{0:T(1024)(128)(2,1)S(1)}) all-reduce(bf16[256]{0:T(256)(128)(2,1)S(1)} %dynamic-update-slice.1, ...), channel_id=1, replica_groups=mesh['wide'=4,'narrow'=8] {'wide','narrow'}, use_global_device_ids=true, to_apply=%add.1 | all-reduce | flops 5120 | bytes 20480
  55.2 42.7 %all_gather.55 = bf16[1536,256]{1,0:T(8,128)(2,1)S(1)} all-gather(bf16[48,256]{1,0:T(8,128)(2,1)} %param.24), channel_id=1, replica_groups=mesh['wide'=4,'narrow'=8] {'wide','narrow'}, dimensions={0}, use_global_device_ids=true | all-gather | bytes 811008 | tf_op jit(solution)/shard_map/all_gather | solution.py:95
  101.2 39.0 %all_gather.60 = bf16[1536,256]{1,0:T(8,128)(2,1)S(1)} all-gather(bf16[48,256]{1,0:T(8,128)(2,1)S(1)} %copy-done.43), channel_id=1, replica_groups=mesh['wide'=4,'narrow'=8] {'wide','narrow'}, dimensions={0}, use_global_device_ids=true | all-gather | bytes 811008 | tf_op jit(solution)/shard_map/all_gather | solution.py:94
  176.1 65.3 %all-gather.14.cloned.1.call-done = bf16[1536,1536]{1,0:T(8,128)(2,1)} async-done(((bf16[48,1536]{1,0:T(8,128)(2,1)}), bf16[1536,1536]{1,0:T(8,128)(2,1)}) %all-gather.14.cloned.1.call-update) | async-done | bytes 4718608 | tf_op jit(solution)/shard_map/all_gather | solution.py:93
  266.8 39.8 %all-gather.16.cloned.1.call-done = bf16[1536,1536]{1,0:T(8,128)(2,1)} async-done(((bf16[48,1536]{1,0:T(8,128)(2,1)}), bf16[1536,1536]{1,0:T(8,128)(2,1)}) %all-gather.16.cloned.1.call-update) | async-done | bytes 4718608 | tf_op jit(solution)/shard_map/all_gather | solution.py:96
  314.1 61.1 %all-gather.22.cloned.1.call-done = bf16[1536,1120]{0,1:T(8,128)(2,1)} async-done(((bf16[384,1120]{0,1:T(8,128)(2,1)}), bf16[1536,1120]{0,1:T(8,128)(2,1)}) %all-gather.22.cloned.1.call-update) | async-done | bytes 3440656 | tf_op jit(solution)/shard_map/all_gather | solution.py:105
  375.2 46.6 %all-gather.18.cloned.1.call-done = bf16[2,1024,1536]{2,1,0:T(8,128)(2,1)} async-done(((bf16[2,128,1536]{2,1,0:T(8,128)(2,1)}), bf16[2,1024,1536]{2,1,0:T(8,128)(2,1)}) %all-gather.18.cloned.1.call-update) | async-done | bytes 6291472 | tf_op jit(solution)/shard_map/all_gather | solution.py:147
  434.7 56.9 %all-gather.20.cloned.1.call-done = bf16[1536,1120]{0,1:T(8,128)(2,1)} async-done(((bf16[384,1120]{0,1:T(8,128)(2,1)}), bf16[1536,1120]{0,1:T(8,128)(2,1)}) %all-gather.20.cloned.1.call-update) | async-done | bytes 3440656 | tf_op jit(solution)/shard_map/all_gather | solution.py:104
  504.6 55.7 %all-gather.24.cloned.1.call-done = bf16[1120,1536]{1,0:T(8,128)(2,1)} async-done(((bf16[1120,384]{1,0:T(8,128)(2,1)}), bf16[1120,1536]{1,0:T(8,128)(2,1)}) %all-gather.24.cloned.1.call-update) | async-done | bytes 3440656 | tf_op jit(solution)/shard_map/all_gather | solution.py:106
  560.3 46.2 %all-gather.26.cloned.1.call-done = bf16[2,1024,1536]{2,1,0:T(8,128)(2,1)} async-done(((bf16[2,128,1536]{2,1,0:T(8,128)(2,1)}), bf16[2,1024,1536]{2,1,0:T(8,128)(2,1)}) %all-gather.26.cloned.1.call-update) | async-done | bytes 6291472 | tf_op jit(solution)/shard_map/all_gather | solution.py:154
  606.4 19.4 %multiply_convert_fusion = (bf16[2,1024,1120]{1,2,0:T(8,128)(2,1)}, bf16[2,1024,1120]{1,2,0:T(8,128)(2,1)}, bf16[2,1024,1120]{1,2,0:T(8,128)(2,1)}) fusion(f32[2,1024,1120]{1,2,0:T(8,128)} %fusion.28, f32[2,1024,1120]{1,2,0:T(8,128)} %fusion.24, bf16[2,1024,1536]{2,1,0:T(8,128)(2,1)} %all-gather.26.cloned.1.call-done, ...), kind=kOutput, calls=%fused_computation.2 | convolution fusion | flops 7080837120 | bytes 41844736 | tf_op jit(solution)/shard_map/rtd,fd->rtf/dot_general | solution.py:155
  639.5 14.0 convolution_add_fusion
  653.5 15.0 fusion.21
  668.8 77.2 %reduce-scatter.14.cloned.1.call-done = f32[2,128,1536]{2,1,0:T(8,128)} async-done(((f32[2,1024,1536]{2,1,0:T(8,128)}), f32[2,128,1536]{2,1,0:T(8,128)}) %reduce-scatter.14.cloned.1.call-update) | async-done | bytes 1572880 | tf_op jit(solution)/shard_map/reduce_scatter | solution.py:168
  748.5 93.5 %reduce-scatter.12.cloned.1.call-done = f32[2,128,1536]{2,1,0:T(8,128)} async-done(((f32[2,1024,1536]{2,1,0:T(8,128)}), f32[2,128,1536]{2,1,0:T(8,128)}) %reduce-scatter.12.cloned.1.call-update) | async-done | bytes 1572880 | tf_op jit(solution)/shard_map/reduce_scatter | solution.py:152
  926.6 29.0 %reduce-scatter.16.cloned.1.call-done = f32[2,128,256]{1,2,0:T(8,128)} async-done(((f32[2,1024,256]{1,2,0:T(8,128)}), f32[2,128,256]{1,2,0:T(8,128)}) %reduce-scatter.16.cloned.1.call-update) | async-done | bytes 262160 | tf_op jit(solution)/shard_map/reduce_scatter | solution.py:200
  986.2 45.8 %all-reduce.10 = (f32[1536]{0:T(1024)S(1)}, f32[1536]{0:T(1024)S(1)}, f32[256]{0:T(256)S(1)}, f32[256]{0:T(256)S(1)}, f32[1536]{0:T(1024)S(1)}) all-reduce(f32[1536]{0:T(1024)S(1)} %get-tuple-element.16, f32[1536]{0:T(1024)S(1)} %bitcast.244, f32[256]{0:T(256)S(1)} %bitcast.245, ...), channel_id=6, replica_groups=mesh['wide'=4,'narrow'=8] {'wide','narrow'}, use_global_device_ids=true, to_apply=%region_16.17.clone | all-reduce | flops 5120 | bytes 40960
  1037.7 42.1 %reduce-scatter.28.cloned.1.call-done = f32[384,1120]{0,1:T(8,128)} async-done(((f32[1536,1120]{0,1:T(8,128)}), f32[384,1120]{0,1:T(8,128)}) %reduce-scatter.28.cloned.1.call-update) | async-done | bytes 1720336 | tf_op jit(solution)/shard_map/reduce_scatter | solution.py:161
  1079.8 123.7 %reduce-scatter.30.cloned.1.call-done = f32[384,1120]{0,1:T(8,128)} async-done(((f32[1536,1120]{0,1:T(8,128)}), f32[384,1120]{0,1:T(8,128)}) %reduce-scatter.30.cloned.1.call-update) | async-done | bytes 1720336 | tf_op jit(solution)/shard_map/reduce_scatter | solution.py:162
  1203.4 123.6 %reduce-scatter.32.cloned.1.call-done = f32[1120,384]{1,0:T(8,128)} async-done(((f32[1120,1536]{1,0:T(8,128)}), f32[1120,384]{1,0:T(8,128)}) %reduce-scatter.32.cloned.1.call-update) | async-done | bytes 1720336 | tf_op jit(solution)/shard_map/reduce_scatter | solution.py:163
  1327.0 104.1 %reduce-scatter.24.cloned.1.call-done = f32[48,256]{1,0:T(8,128)} async-done(((f32[1536,256]{1,0:T(8,128)}), f32[48,256]{1,0:T(8,128)}) %reduce-scatter.24.cloned.1.call-update) | async-done | bytes 49168 | tf_op jit(solution)/shard_map/reduce_scatter | solution.py:234
  1431.1 102.6 %reduce-scatter.22.cloned.1.call-done = f32[48,256]{1,0:T(8,128)} async-done(((f32[1536,256]{1,0:T(8,128)}), f32[48,256]{1,0:T(8,128)}) %reduce-scatter.22.cloned.1.call-update) | async-done | bytes 49168 | tf_op jit(solution)/shard_map/reduce_scatter | solution.py:233
  1533.7 142.1 %reduce-scatter.26.cloned.1.call-done = f32[48,1536]{1,0:T(8,128)} async-done(((f32[1536,1536]{1,0:T(8,128)}), f32[48,1536]{1,0:T(8,128)}) %reduce-scatter.26.cloned.1.call-update) | async-done | bytes 294928 | tf_op jit(solution)/shard_map/reduce_scatter | solution.py:235
  1675.9 141.0 %reduce-scatter.20.cloned.1.call-done = f32[48,1536]{1,0:T(8,128)} async-done(((f32[1536,1536]{1,0:T(8,128)}), f32[48,1536]{1,0:T(8,128)}) %reduce-scatter.20.cloned.1.call-update) | async-done | bytes 294928 | tf_op jit(solution)/shard_map/reduce_scatter | solution.py:232
  (261 shorter events, 239.9 us)
Async XLA Ops:
  7.2 133.9 %copy-start = (bf16[2,128,1536]{2,1,0:T(8,128)(2,1)S(1)}, bf16[2,128,1536]{2,1,0:T(8,128)(2,1)}, u32[]{:S(2)}) copy-start(bf16[2,128,1536]{2,1,0:T(8,128)(2,1)} %param.16) | copy-start | bytes 2359300
  7.2 158.3 %all-gather.10.cloned.1.call-start = ((), (), s32[]{:S(2)}) async-start(), calls=%async_computation.11 | async-start | bytes 1179648 | tf_op jit(solution)/shard_map/all_gather | solution.py:130
  53.8 187.6 %copy-start.37 = (f32[1536]{0:T(1024)}, f32[1536]{0:T(1024)S(1)}, u32[]{:S(2)}) copy-start(f32[1536]{0:T(1024)S(1)} %convert_element_type.111) | copy-start | bytes 18436
  55.1 186.2 %copy-start.40 = (f32[2,128]{1,0:T(2,128)}, f32[2,128]{1,0:T(2,128)S(1)}, u32[]{:S(2)}) copy-start(f32[2,128]{1,0:T(2,128)S(1)} %add_rsqrt_fusion.1) | copy-start | bytes 3076
  101.1 73.7 %all-gather.12.cloned.1.call-start = ((), (), s32[]{:S(2)}) async-start(), calls=%async_computation.12 | async-start | bytes 1179648 | tf_op jit(solution)/shard_map/all_gather | solution.py:129
  153.8 87.6 %all-gather.14.cloned.1.call-start = ((), (), s32[]{:S(2)}) async-start(), calls=%async_computation.13 | async-start | bytes 4866048 | tf_op jit(solution)/shard_map/all_gather | solution.py:93
  154.5 152.1 %all-gather.16.cloned.1.call-start = ((), (), s32[]{:S(2)}) async-start(), calls=%async_computation.14 | async-start | bytes 4866048 | tf_op jit(solution)/shard_map/all_gather | solution.py:96
  155.1 220.1 %all-gather.22.cloned.1.call-start = ((), (), s32[]{:S(2)}) async-start(), calls=%async_computation.17 | async-start | bytes 4300800 | tf_op jit(solution)/shard_map/all_gather | solution.py:105
  155.7 266.1 %all-gather.18.cloned.1.call-start = ((), (), s32[]{:S(2)}) async-start(), calls=%async_computation.15 | async-start | bytes 7077888 | tf_op jit(solution)/shard_map/all_gather | solution.py:147
  311.6 180.1 %all-gather.20.cloned.1.call-start = ((), (), s32[]{:S(2)}) async-start(), calls=%async_computation.16 | async-start | bytes 4300800 | tf_op jit(solution)/shard_map/all_gather | solution.py:104
  312.3 248.0 %all-gather.24.cloned.1.call-start = ((), (), s32[]{:S(2)}) async-start(), calls=%async_computation.18 | async-start | bytes 4300800 | tf_op jit(solution)/shard_map/all_gather | solution.py:106
  313.1 293.4 %all-gather.26.cloned.1.call-start = ((), (), s32[]{:S(2)}) async-start(), calls=%async_computation.20 | async-start | bytes 7077888 | tf_op jit(solution)/shard_map/all_gather | solution.py:154
  313.8 432.3 %reduce-scatter.14.cloned.1.call-start = ((), (), s32[]{:S(2)}) async-start(), calls=%async_computation.21 | async-start | bytes 14155776 | tf_op jit(solution)/shard_map/reduce_scatter | solution.py:168
  653.5 188.5 %reduce-scatter.12.cloned.1.call-start = ((), (), s32[]{:S(2)}) async-start(), calls=%async_computation.19 | async-start | bytes 14155776 | tf_op jit(solution)/shard_map/reduce_scatter | solution.py:152
  668.6 173.4 %copy-start.7 = (bf16[2,128,1536]{2,1,0:T(8,128)(2,1)S(1)}, bf16[2,128,1536]{2,1,0:T(8,128)(2,1)}, u32[]{:S(2)}) copy-start(bf16[2,128,1536]{2,1,0:T(8,128)(2,1)} %param.31) | copy-start | bytes 2359300
  668.6 253.5 %reduce-scatter.18.cloned.1.call-start = ((), (), s32[]{:S(2)}) async-start(), calls=%async_computation.23 | async-start | bytes 2359296 | tf_op jit(solution)/shard_map/reduce_scatter | solution.py:201
  869.3 86.3 %reduce-scatter.16.cloned.1.call-start = ((), (), s32[]{:S(2)}) async-start(), calls=%async_computation.22 | async-start | bytes 2359296 | tf_op jit(solution)/shard_map/reduce_scatter | solution.py:200
  883.7 196.1 %reduce-scatter.28.cloned.1.call-start = ((), (), s32[]{:S(2)}) async-start(), calls=%async_computation.28 | async-start | bytes 8601600 | tf_op jit(solution)/shard_map/reduce_scatter | solution.py:161
  896.6 306.9 %reduce-scatter.30.cloned.1.call-start = ((), (), s32[]{:S(2)}) async-start(), calls=%async_computation.29 | async-start | bytes 8601600 | tf_op jit(solution)/shard_map/reduce_scatter | solution.py:162
  909.3 417.7 %reduce-scatter.32.cloned.1.call-start = ((), (), s32[]{:S(2)}) async-start(), calls=%async_computation.30 | async-start | bytes 8601600 | tf_op jit(solution)/shard_map/reduce_scatter | solution.py:163
  922.0 509.1 %reduce-scatter.24.cloned.1.call-start = ((), (), s32[]{:S(2)}) async-start(), calls=%async_computation.26 | async-start | bytes 1622016 | tf_op jit(solution)/shard_map/reduce_scatter | solution.py:234
  925.8 607.9 %reduce-scatter.22.cloned.1.call-start = ((), (), s32[]{:S(2)}) async-start(), calls=%async_computation.25 | async-start | bytes 1622016 | tf_op jit(solution)/shard_map/reduce_scatter | solution.py:233
  963.7 712.1 %reduce-scatter.26.cloned.1.call-start = ((), (), s32[]{:S(2)}) async-start(), calls=%async_computation.27 | async-start | bytes 9732096 | tf_op jit(solution)/shard_map/reduce_scatter | solution.py:235
  969.2 847.7 %reduce-scatter.20.cloned.1.call-start = ((), (), s32[]{:S(2)}) async-start(), calls=%async_computation.24 | async-start | bytes 9732096 | tf_op jit(solution)/shard_map/reduce_scatter | solution.py:232
  (52 other events, 800.2 us)
Sparse Core Ops, SparseCore 0:
  101.2 21.4 all-gather.9
  153.9 20.8 all-gather.11
  177.7 63.6 all-gather.13
  244.1 62.4 all-gather.15
  308.1 67.0 all-gather.21
  377.5 44.2 all-gather.17
  423.4 68.2 all-gather.19
  493.3 66.9 all-gather.23
  562.2 44.2 all-gather.25
  653.6 92.3 reduce-scatter.13
  749.6 92.3 reduce-scatter.11
  869.4 41.2 reduce-scatter.17
  914.4 41.2 reduce-scatter.15
  958.4 121.3 reduce-scatter.27
  1082.6 120.7 reduce-scatter.29
  1206.2 120.8 reduce-scatter.31
  1333.5 97.5 reduce-scatter.23
  1437.6 96.0 reduce-scatter.21
  1541.2 134.6 reduce-scatter.25
  1682.2 134.6 reduce-scatter.19
where the time goes:
time: 1830 us; the launch traced here: 1820 us
  waiting for transfers between devices  1360 us (74%)
  matrix products  200 us (11%)
  blocking collectives  187 us (10%)
  local copies, waits for them, and re-layouts  31.7 us (2%)
  other arithmetic  27.8 us (2%)
    reduce_scatter x1, waiting for transfers between devices, on_device(): lax.psum_scatter(d_wo, ('wide', 'narrow'), scatter_dimension=0, tiled=True)  142 us
    reduce_scatter x1, waiting for transfers between devices, on_device(): lax.psum_scatter(d_wq, ('wide', 'narrow'), scatter_dimension=0, tiled=True)  141 us
    reduce_scatter x1, waiting for transfers between devices, on_device(): lax.psum_scatter(d_wu, 'wide', scatter_dimension=0, tiled=True)  124 us
    reduce_scatter x1, waiting for transfers between devices, on_device(): lax.psum_scatter(d_wd, 'wide', scatter_dimension=1, tiled=True)  124 us
    reduce_scatter x1, waiting for transfers between devices, on_device(): lax.psum_scatter(d_wv, ('wide', 'narrow'), scatter_dimension=0, tiled=True)  104 us
    reduce_scatter x1, waiting for transfers between devices, on_device(): lax.psum_scatter(d_wk, ('wide', 'narrow'), scatter_dimension=0, tiled=True)  103 us
    reduce_scatter x1, waiting for transfers between devices, on_device(): lax.psum_scatter(partial_value, 'narrow', scatter_dimension=1, tiled=True)  93.5 us
    unnamed x2, blocking collectives  88 us
  transfers between devices with their start and end apart: 20, of which 18 were waited for; matrix products, arithmetic and copies ran while one was open for 9% of the time, Pallas kernels for 0%

commit v1 on v0

v1 whole, which is shorter than its diff:
```python
import math

import jax
import jax.numpy as jnp
from jax import lax
from jax.sharding import PartitionSpec as P

Q_HEADS = 12
KV_HEADS = 2
HEAD = 128
HQ = 1536
HK = 256

EPS = 1e-06
THETA = 10000.0

F32 = jnp.float32
BF16 = jnp.bfloat16


def norm_parts(value):
    factor = lax.rsqrt(jnp.mean(value * value, axis=-1, keepdims=True) + EPS)
    return (value * factor, factor)


def norm_back(grad, unit, factor, gain):
    scaled = grad * gain
    return factor * (scaled - unit * jnp.mean(scaled * unit, axis=-1, keepdims=True))


def rotate(value, cosine, sine):
    half = value.shape[-1] // 2
    first = value[..., :half]
    second = value[..., half:]
    return jnp.concatenate(
        [first * cosine - second * sine, second * cosine + first * sine], axis=-1
    )


def angles(places, head_size):
    freq = jnp.exp(
        jnp.arange(head_size // 2, dtype=jnp.float32) * (-2.0 * math.log(THETA) / head_size)
    )
    turn = places.astype(jnp.float32)[..., None] * freq
    return (jnp.cos(turn), jnp.sin(turn))


def row_probs(query, keys, allowed, scale):
    scores = jnp.einsum("qhgd,khd->hgqk", query, keys, preferred_element_type=F32) * scale
    scores = jnp.where(allowed[None, None], scores, -1e30)
    top = jnp.max(scores, axis=-1, keepdims=True)
    expo = jnp.exp(scores - top)
    return expo / jnp.sum(expo, axis=-1, keepdims=True)


def mm(left, right):
    return jnp.dot(left, right, preferred_element_type=F32)


def mm_t(left, right):
    return lax.dot_general(
        left, right, (((left.ndim - 1,), (1,)), ((), ())), preferred_element_type=F32
    )


def t_mm(left, right):
    return lax.dot_general(left, right, (((0,), (0,)), ((), ())), preferred_element_type=F32)


class Links:
    def __init__(self, wide, narrow):
        self.wide, self.narrow = wide, narrow
        bits = [1 << i for i in range(1, (narrow - 1).bit_length())]
        half = len(bits) // 2
        core = [1] if narrow > 1 else []
        self.orders = (bits + core, bits[half:] + bits[:half] + core)
        self.ring = [(i, (i + 1) % wide) for i in range(wide)]

    def hop(self, value, bit):
        return lax.ppermute(value, "narrow", [(i, i ^ bit) for i in range(self.narrow)])

    def offsets(self, which):
        found = [0]
        for bit in self.orders[which]:
            found = found + [o ^ bit for o in found]
        return found

    def gather(self, value, which):
        held = value[None]
        for bit in self.orders[which]:
            held = jnp.concatenate([held, self.hop(held, bit)], axis=0)
        return held

    def scatter(self, blocks, which, bits=None):
        for bit in reversed(self.orders[which] if bits is None else bits):
            half = blocks.shape[0] // 2
            got = self.hop(blocks[half:], bit)
            blocks = (blocks[:half].astype(F32) + got.astype(F32)).astype(blocks.dtype)
        return blocks[0]

    def ring_gather(self, value):
        slots = [value]
        for _ in range(self.wide - 1):
            slots.append(lax.ppermute(slots[-1], "wide", self.ring))
        return slots

    def ring_scatter(self, slots):
        got = None
        for k in range(1, self.wide):
            send = slots[k] if got is None else (slots[k].astype(F32) + got.astype(F32)).astype(BF16)
            got = lax.ppermute(send, "wide", self.ring)
        if got is None:
            return slots[0].astype(F32)
        return slots[0].astype(F32) + got.astype(F32)

    def direct_gather(self, value):
        return [value] + [
            lax.ppermute(value, "wide", [(i, (i + k) % self.wide) for i in range(self.wide)])
            for k in range(1, self.wide)
        ]

    def direct_scatter(self, slots):
        total = slots[0].astype(F32)
        for k in range(1, self.wide):
            total = total + lax.ppermute(
                slots[k], "wide", [(i, (i - k) % self.wide) for i in range(self.wide)]
            ).astype(F32)
        return total


def on_device(
    layer_in,
    seg_ids,
    pad_mask,
    gain_attn,
    w_query,
    b_query,
    w_key,
    b_key,
    w_value,
    b_value,
    w_out,
    gain_mlp,
    w_gate,
    w_up,
    w_down,
    grad_out,
):
    rows, seg_len, width = layer_in.shape
    wide = lax.axis_size("wide")
    parts = lax.axis_size("narrow")
    links = Links(wide, parts)
    here = lax.axis_index("wide")
    me = lax.axis_index("narrow")
    row_len = seg_len * parts
    tokens = rows * seg_len
    group = Q_HEADS // KV_HEADS
    scale = 1.0 / math.sqrt(HEAD)
    share = w_query.shape[0]
    small = b_key.shape[0]
    slot = width // wide
    which = [row % 2 for row in range(rows)]

    vectors = jnp.concatenate([gain_attn, gain_mlp, b_query, b_key, b_value])
    vectors = jnp.pad(vectors, (0, 2 * HK - vectors.shape[0]))[None]
    kv_own = jnp.concatenate([jnp.concatenate([w_key, w_value], axis=1), vectors], axis=0)

    def gather_weight(own, order):
        held = links.gather(jnp.stack(links.direct_gather(own)), order)
        if order == 0:
            return held
        at = {offset: i for i, offset in enumerate(links.offsets(order))}
        return jnp.concatenate([held[at[o]][None] for o in links.offsets(0)], axis=0)

    def scatter_weight(grad, order):
        if order != 0:
            at = {offset: i for i, offset in enumerate(links.offsets(0))}
            grad = jnp.concatenate([grad[at[o]][None] for o in links.offsets(order)], axis=0)
        held = links.scatter(grad, order)
        return links.direct_scatter([held[k] for k in range(wide)])

    kv_all = gather_weight(kv_own, 1)
    wq = gather_weight(w_query, 0).reshape(width, HQ)
    wo = gather_weight(w_out, 1).reshape(HQ, width)
    wkv = kv_all[:, :, :share].reshape(width, 2 * HK)
    packed = kv_all[:, :, share]
    g_one_rel = packed[:, :, :share].reshape(width).astype(F32)
    g_two_rel = packed[:, :, share : 2 * share].reshape(width)
    bq_rel = packed[:, :, 2 * share : 3 * share].reshape(HQ)
    bk_rel = packed[:, :, 3 * share : 3 * share + small].reshape(HK)
    bv_rel = packed[:, :, 3 * share + small : 3 * share + 2 * small].reshape(HK)

    def placing(block):
        offs = jnp.array(links.offsets(0), jnp.int32) ^ me
        from_wide = (here - jnp.arange(wide, dtype=jnp.int32)) % wide
        source = (
            (from_wide[None, :, None] * parts + offs[:, None, None]) * block
            + jnp.arange(block, dtype=jnp.int32)[None, None, :]
        ).reshape(-1)
        count = block * parts * wide
        return (jnp.arange(count, dtype=jnp.int32)[:, None] == source[None, :]).astype(BF16)

    place = placing(share)
    place_small = placing(small)

    def to_rel(value):
        return mm(value, place).astype(BF16)

    def from_rel(value):
        return mm_t(value, place).astype(BF16)

    two = mm_t(jnp.stack([g_two_rel, bq_rel]), place)
    g_two, bq = two[0], two[1]
    two = mm_t(jnp.stack([bk_rel, bv_rel]), place_small)
    bkv = two.reshape(2 * HK)

    wg_slots = links.ring_gather(w_gate)
    wu_slots = links.ring_gather(w_up)
    wd_slots = links.ring_gather(w_down)
    wg = jnp.concatenate(wg_slots, axis=0)
    wu = jnp.concatenate(wu_slots, axis=0)
    wd = jnp.concatenate(wd_slots, axis=1)

    def rolled(value):
        return jnp.concatenate(
            [
                lax.dynamic_slice_in_dim(value, ((here - k) % wide) * slot, slot, value.ndim - 1)
                for k in range(wide)
            ],
            axis=-1,
        )

    def unrolled(value):
        return jnp.concatenate(
            [
                lax.dynamic_slice_in_dim(value, ((here - k) % wide) * slot, slot, value.ndim - 1)
                for k in range(wide)
            ],
            axis=-1,
        )

    def gather_tokens(value):
        return jnp.stack([links.gather(value[r], which[r]) for r in range(rows)])

    def scatter_tokens(value):
        return jnp.stack([links.scatter(value[r], which[r]) for r in range(rows)])

    marks = gather_tokens(jnp.stack([seg_ids, pad_mask], axis=1))
    ids_all = marks[:, :, 0].reshape(rows, row_len)
    pads_all = marks[:, :, 1].reshape(rows, row_len)
    sources = jnp.array([links.offsets(which[r]) for r in range(rows)], jnp.int32) ^ me
    key_idx = (
        sources[:, :, None] * seg_len + jnp.arange(seg_len, dtype=jnp.int32)[None, None, :]
    ).reshape(rows, row_len)
    global_idx = me * seg_len + jnp.arange(seg_len, dtype=jnp.int32)
    begins = jnp.sum((ids_all[:, None, :] < seg_ids[:, :, None]).astype(jnp.int32), axis=-1)
    cosine, sine = angles(global_idx[None, :] - begins, HEAD)
    cosine = cosine[:, :, None, :]
    sine = sine[:, :, None, :]
    allowed = (ids_all[:, None, :] == seg_ids[:, :, None]) & (
        key_idx[:, None, :] < global_idx[None, :, None]
    ) & (pads_all[:, None, :] == 1) | (key_idx[:, None, :] == global_idx[None, :, None])

    x_in = layer_in.reshape(tokens, width).astype(F32)
    x_rel = mm(layer_in.reshape(tokens, width), place)
    unit_one, factor_one = norm_parts(x_rel)
    h_one = (unit_one * g_one_rel).astype(BF16)
    kv_lin = mm(h_one, wkv) + bkv
    k_rot = rotate(kv_lin[:, :HK].reshape(rows, seg_len, KV_HEADS, HEAD), cosine, sine)
    k_rot = k_rot.astype(BF16).reshape(rows, seg_len, HK)
    v_low = kv_lin[:, HK:].astype(BF16).reshape(rows, seg_len, HK)
    kv_rows = gather_tokens(jnp.concatenate([k_rot, v_low], axis=-1))
    kv_rows = kv_rows.reshape(rows, row_len, 2, KV_HEADS, HEAD)
    keys_all = kv_rows[:, :, 0]
    values_all = kv_rows[:, :, 1]
    q_lin = mm(h_one, wq) + bq
    q_rot = rotate(q_lin.reshape(rows, seg_len, Q_HEADS, HEAD), cosine, sine).astype(BF16)
    queries = q_rot.reshape(rows, seg_len, KV_HEADS, group, HEAD)
    outputs = []
    for row in range(rows):
        probs = row_probs(queries[row], keys_all[row], allowed[row], scale)
        outputs.append(
            jnp.einsum(
                "hgqk,khd->qhgd", probs.astype(BF16), values_all[row], preferred_element_type=F32
            )
        )
    attended = to_rel(jnp.stack(outputs).reshape(tokens, HQ).astype(BF16))
    x_mid = x_in + mm(attended, wo)
    unit_two, factor_two = norm_parts(x_mid)
    h_two = rolled((unit_two * g_two).astype(BF16))

    all_tokens = rows * row_len
    grad_all = gather_tokens(rolled(grad_out)).reshape(all_tokens, width)
    h_all = gather_tokens(h_two.reshape(rows, seg_len, width)).reshape(all_tokens, width)
    d_hidden = mm_t(grad_all, wd)
    gate = mm(h_all, wg)
    up = mm(h_all, wu)
    sigma = jax.nn.sigmoid(gate)
    active = gate * sigma
    hidden = (active * up).astype(BF16)
    d_gate = (d_hidden * up * sigma * (1.0 + gate * (1.0 - sigma))).astype(BF16)
    d_up = (d_hidden * active).astype(BF16)

    def by_token(value):
        return value.astype(BF16).reshape(rows, parts, seg_len, width)

    d_h_two = scatter_tokens(by_token(mm_t(d_gate, wg) + mm_t(d_up, wu)))
    mixed = scatter_tokens(by_token(mm(hidden, wd)))
    layer_out = (x_mid + unrolled(mixed.reshape(tokens, width)).astype(F32)).astype(BF16)

    def row_slots(grad):
        return [grad[k * slot : (k + 1) * slot].astype(BF16) for k in range(wide)]

    grad_w_down = links.ring_scatter(
        [
            t_mm(hidden, grad_all[:, k * slot : (k + 1) * slot]).astype(BF16)
            for k in range(wide)
        ]
    )
    grad_w_gate = links.ring_scatter(row_slots(t_mm(h_all, d_gate)))
    grad_w_up = links.ring_scatter(row_slots(t_mm(h_all, d_up)))

    d_h_two = unrolled(d_h_two.reshape(tokens, width)).astype(F32)
    d_g_two = jnp.sum(d_h_two * unit_two, axis=0)
    d_mid = grad_out.reshape(tokens, width).astype(F32) + norm_back(
        d_h_two, unit_two, factor_two, g_two
    )
    d_branch = d_mid.astype(BF16)
    d_wo = t_mm(attended, d_branch)
    grad_w_out = scatter_weight(d_wo.astype(BF16).reshape(parts, wide, share, width), 1)
    d_attended = from_rel(mm_t(d_branch, wo).astype(BF16))
    d_att_heads = d_attended.reshape(rows, seg_len, KV_HEADS, group, HEAD)
    query_grads = []
    kv_grads = []
    for row in range(rows):
        probs = row_probs(queries[row], keys_all[row], allowed[row], scale)
        d_prob = jnp.einsum(
            "qhgd,khd->hgqk", d_att_heads[row], values_all[row], preferred_element_type=F32
        )
        delta = jnp.sum(probs * d_prob, axis=-1, keepdims=True)
        d_score = (scale * probs * (d_prob - delta)).astype(BF16)
        query_grads.append(
            jnp.einsum("hgqk,khd->qhgd", d_score, keys_all[row], preferred_element_type=F32)
        )
        d_key = jnp.einsum("hgqk,qhgd->khd", d_score, queries[row], preferred_element_type=F32)
        d_value = jnp.einsum(
            "hgqk,qhgd->khd", probs.astype(BF16), d_att_heads[row], preferred_element_type=F32
        )
        kv_grads.append(
            jnp.concatenate(
                [d_key.reshape(row_len, HK), d_value.reshape(row_len, HK)], axis=-1
            ).astype(BF16)
        )
    d_kv = jnp.stack(kv_grads).reshape(rows, parts, seg_len, 2 * HK)
    d_kv = scatter_tokens(d_kv).reshape(rows, seg_len, 2 * HK).astype(F32)
    d_query = jnp.stack(query_grads).reshape(rows, seg_len, Q_HEADS, HEAD)
    dq_lin = rotate(d_query, cosine, -sine).reshape(tokens, HQ).astype(BF16)
    d_wq = t_mm(h_one, dq_lin)
    grad_w_query = scatter_weight(d_wq.astype(BF16).reshape(parts, wide, share, HQ), 0)
    dk_lin = rotate(d_kv[..., :HK].reshape(rows, seg_len, KV_HEADS, HEAD), cosine, -sine)
    dk_lin = dk_lin.reshape(tokens, HK).astype(BF16)
    dv_lin = d_kv[..., HK:].reshape(tokens, HK).astype(BF16)
    dkv_lin = jnp.concatenate([dk_lin, dv_lin], axis=-1)
    d_wkv = t_mm(h_one, dkv_lin)
    d_bq = jnp.sum(dq_lin.astype(F32), axis=0)
    d_bkv = jnp.sum(dkv_lin.astype(F32), axis=0).reshape(2, HK)
    d_h_one = mm_t(dq_lin, wq) + mm_t(dkv_lin, wkv)
    d_g_one = jnp.sum(d_h_one * unit_one, axis=0)
    back = norm_back(d_h_one, unit_one, factor_one, g_one_rel).astype(BF16)
    grad_in = (d_mid + mm_t(back, place)).astype(BF16)

    two = mm(jnp.stack([d_g_two, d_bq]).astype(BF16), place)
    two = two.reshape(2, parts, wide, share)
    small_two = mm(d_bkv.astype(BF16), place_small).reshape(2, parts, wide, small)
    vec = jnp.concatenate(
        [
            d_g_one.reshape(parts, wide, share),
            two[0],
            two[1],
            small_two[0],
            small_two[1],
        ],
        axis=-1,
    )
    vec = jnp.pad(vec, ((0, 0), (0, 0), (0, 2 * HK - vec.shape[-1])))[:, :, None]
    kv_block = jnp.concatenate([d_wkv.reshape(parts, wide, share, 2 * HK), vec], axis=2)
    kv_sum = scatter_weight(kv_block.astype(BF16), 1)
    grad_w_key = kv_sum[:share, :HK]
    grad_w_value = kv_sum[:share, HK:]
    last = kv_sum[share]
    grad_gain_attn = last[:share]
    grad_gain_mlp = last[share : 2 * share]
    grad_b_query = last[2 * share : 3 * share]
    grad_b_key = last[3 * share : 3 * share + small]
    grad_b_value = last[3 * share + small : 3 * share + 2 * small]
    return (
        layer_out.reshape(rows, seg_len, width),
        grad_in.reshape(rows, seg_len, width),
        grad_gain_attn,
        grad_w_query,
        grad_b_query,
        grad_w_key,
        grad_b_key,
        grad_w_value,
        grad_b_value,
        grad_w_out,
        grad_gain_mlp,
        grad_w_gate,
        grad_w_up,
        grad_w_down,
    )


def solution(mesh):
    return jax.shard_map(
        on_device,
        mesh=mesh,
        in_specs=(
            P("wide", "narrow", None),
            P("wide", "narrow"),
            P("wide", "narrow"),
            P(("wide", "narrow")),
            P(("wide", "narrow"), None),
            P(("wide", "narrow")),
            P(("wide", "narrow"), None),
            P(("wide", "narrow")),
            P(("wide", "narrow"), None),
            P(("wide", "narrow")),
            P(("wide", "narrow"), None),
            P(("wide", "narrow")),
            P("wide", "narrow"),
            P("wide", "narrow"),
            P("narrow", "wide"),
            P("wide", "narrow", None),
        ),
        out_specs=(
            P("wide", "narrow", None),
            P("wide", "narrow", None),
            P(("wide", "narrow")),
            P(("wide", "narrow"), None),
            P(("wide", "narrow")),
            P(("wide", "narrow"), None),
            P(("wide", "narrow")),
            P(("wide", "narrow"), None),
            P(("wide", "narrow")),
            P(("wide", "narrow"), None),
            P(("wide", "narrow")),
            P("wide", "narrow"),
            P("wide", "narrow"),
            P("narrow", "wide"),
        ),
        check_vma=False,
    )
```

time: 1830 us -> 745 us (0.41)
  waiting for transfers between devices: 1360 us -> 304 us
  blocking collectives: 187 us -> 0 us
  starting transfers between devices: 1.7 us -> 82.1 us
  other arithmetic: 27.8 us -> 84.4 us
  local copies, waits for them, and re-layouts: 31.7 us -> 83.3 us
  matrix products: 200 us -> 180 us
    reduce_scatter x11 -> x0, waiting for transfers between devices: 979 us -> none  [the longest x1 142 us: on_device(): lax.psum_scatter(d_wo, ('wide', 'narrow'), scatter_dimension=0, tiled=True)]
    all_gather x9 -> x0, waiting for transfers between devices: 378 us -> none  [the longest x1 65.3 us: on_device(): lax.all_gather(w_query, ('wide', 'narrow'), axis=0, tiled=True)]
    ppermute x0 -> x96, waiting for transfers between devices: none -> 304 us  [the longest x60 138 us: hop(): lax.ppermute(value, 'narrow', [(i, i ^ bit) for i in range(self.narrow)])]
    all_gather x4 -> x0, blocking collectives: 98.7 us -> none  [the longest x1 42.7 us: on_device(): lax.all_gather(w_value, ('wide', 'narrow'), axis=0, tiled=True)]
    unnamed x2 -> x0, blocking collectives: 88 us -> none
    ppermute x0 -> x96, starting transfers between devices: none -> 82.1 us  [the longest x60 36.6 us: hop(): lax.ppermute(value, 'narrow', [(i, i ^ bit) for i in range(self.narrow)])]
    concatenate x0 -> x35, other arithmetic: none -> 25.9 us  [the longest x25 22.5 us: gather(): held = jnp.concatenate([held, self.hop(held, bit)], axis=0)]
    dot_general x25 -> x32, matrix products: 178 us -> 157 us  [the longest x10 54.6 us: mm(): return jnp.dot(left, right, preferred_element_type=F32)]
  transfers between devices with their start and end apart: 20 -> 96, of which waited for: 18 -> 44; matrix products, arithmetic and copies ran while one was open for 9% -> 35% of each run, Pallas kernels for 0% -> 0%
where the time goes in v1:
time: 745 us; the launch traced here: 737 us
  waiting for transfers between devices  304 us (41%)
  matrix products  180 us (24%)
  other arithmetic  84.4 us (11%)
  local copies, waits for them, and re-layouts  83.3 us (11%)
  starting transfers between devices  82.1 us (11%)
    ppermute x60, waiting for transfers between devices, hop(): lax.ppermute(value, 'narrow', [(i, i ^ bit) for i in range(self.narrow)])  138 us
    ppermute x9, waiting for transfers between devices, ring_scatter(): got = lax.ppermute(send, 'wide', self.ring)  101 us
    dot_general x10, matrix products, mm(): return jnp.dot(left, right, preferred_element_type=F32)  54.6 us
    dot_general x9, matrix products, mm_t(): lax.dot_general(left, right, (((left.ndim - 1,), (1,)), ((), ())), prefer...  53 us
    ppermute x9, waiting for transfers between devices, ring_gather(): slots.append(lax.ppermute(slots[-1], 'wide', self.ring))  42.8 us
    dot_general x9, matrix products, t_mm(): lax.dot_general(left, right, (((0,), (0,)), ((), ())), preferred_element_...  42.2 us
    unnamed x252, local copies, waits for them, and re-layouts  37.2 us
    ppermute x60, starting transfers between devices, hop(): lax.ppermute(value, 'narrow', [(i, i ^ bit) for i in range(self.narrow)])  36.6 us
  transfers between devices with their start and end apart: 96, of which 44 were waited for; matrix products, arithmetic and copies ran while one was open for 35% of the time, Pallas kernels for 0%

profile of v1, /device:TPU:0, one launch (start us, length us, event | category | flops | bytes accessed | tf_op | source)
XLA Modules:
  0.0 736.9 jit_solution(15670650332043913749)
XLA Ops:
  68.1 11.8 %collective-permute-done.3 = bf16[1,4,49,512]{3,1,2,0:T(4,128)(2,1)S(1)} collective-permute-done((bf16[1,4,49,512]{3,1,2,0:T(4,128)(2,1)S(1)}, bf16[1,4,49,512]{3,1,2,0:T(4,128)(2,1)S(1)}, u32[]{:S(2)}, u32[]{:S(2)}) %collective-permute-start.3) | collective-permute-done | bytes 200736 | tf_op jit(solution)/shard_map/ppermute | solution.py:80
  86.2 10.0 %collective-permute-done.4 = bf16[2,4,49,512]{3,1,2,0:T(4,128)(2,1)S(1)} collective-permute-done((bf16[2,4,49,512]{3,1,2,0:T(4,128)(2,1)S(1)}, bf16[2,4,49,512]{3,1,2,0:T(4,128)(2,1)S(1)}, u32[]{:S(2)}, u32[]{:S(2)}) %collective-permute-start.4) | collective-permute-done | bytes 401440 | tf_op jit(solution)/shard_map/ppermute | solution.py:80
  145.0 8.7 %collective-permute-done.21 = bf16[1,128,512]{1,0,2:T(2,128)(2,1)S(1)} collective-permute-done((bf16[1,128,512]{1,0,2:T(2,128)(2,1)S(1)}, bf16[1,128,512]{1,0,2:T(2,128)(2,1)S(1)}, u32[]{:S(2)}, u32[]{:S(2)}) %collective-permute-start.21) | collective-permute-done | bytes 131104 | tf_op jit(solution)/shard_map/ppermute | solution.py:80
  167.9 13.1 %collective-permute-done.37 = bf16[384,1120]{0,1:T(8,128)(2,1)} collective-permute-done((bf16[384,1120]{0,1:T(8,128)(2,1)}, bf16[384,1120]{0,1:T(8,128)(2,1)}, u32[]{:S(2)}, u32[]{:S(2)}) %collective-permute-start.37) | collective-permute-done | bytes 860192 | tf_op jit(solution)/shard_map/ppermute | solution.py:104
  207.9 15.8 %collective-permute-done.44 = bf16[1120,384]{1,0:T(8,128)(2,1)} collective-permute-done((bf16[1120,384]{1,0:T(8,128)(2,1)}, bf16[1120,384]{1,0:T(8,128)(2,1)}, u32[]{:S(2)}, u32[]{:S(2)}) %collective-permute-start.44) | collective-permute-done | bytes 860192 | tf_op jit(solution)/shard_map/ppermute | solution.py:104
  284.9 12.1 %collective-permute-done.31 = bf16[2,128,1536]{2,1,0:T(8,128)(2,1)S(1)} collective-permute-done((bf16[2,128,1536]{2,1,0:T(8,128)(2,1)S(1)}, bf16[2,128,1536]{2,1,0:T(8,128)(2,1)S(1)}, u32[]{:S(2)}, u32[]{:S(2)}) %collective-permute-start.31) | collective-permute-done | bytes 786464 | tf_op jit(solution)/shard_map/ppermute | solution.py:80
  299.4 9.7 %fusion.197 = f32[2048,1120]{0,1:T(8,128)} fusion(bf16[2048,1536]{1,0:T(8,128)(2,1)S(1)} %bitcast.450, bf16[1120,1536]{1,0:T(8,128)(2,1)S(1)} %copy-done.65), kind=kOutput, calls=%fused_computation.458 | convolution fusion | flops 7046430720 | bytes 18907136 | tf_op jit(solution)/shard_map/dot_general | solution.py:61
  313.1 11.6 %fusion.196 = f32[2048,1120]{0,1:T(8,128)} fusion(bf16[2048,1536]{1,0:T(8,128)(2,1)} %bitcast.455, bf16[1536,1120]{0,1:T(8,128)(2,1)S(1)} %copy-done.63), kind=kOutput, calls=%fused_computation.457 | convolution fusion | flops 7046430720 | bytes 18907136 | tf_op jit(solution)/shard_map/dot_general | solution.py:57
  324.7 21.3 %multiply_convert_fusion.1 = (bf16[2048,1120]{0,1:T(8,128)(2,1)}, bf16[2048,1120]{0,1:T(8,128)(2,1)}, bf16[2048,1120]{0,1:T(8,128)(2,1)}) fusion(f32[2048,1120]{0,1:T(8,128)} %fusion.197, f32[2048,1120]{0,1:T(8,128)} %fusion.196, bf16[2048,1536]{1,0:T(8,128)(2,1)} %bitcast.456, bf16[1536,1120]{0,1:T(8,128)(2,1)} %constant_dynamic-update-slice_fusion.4), kind=kOutput, calls=%fused_computation.11 | convolution fusion | flops 7080837120 | bytes 41844736 | tf_op jit(solution)/shard_map/dot_general | solution.py:57
  352.1 9.0 %convolution_convert_fusion = bf16[2048,1536]{1,0:T(8,128)(2,1)S(1)} fusion(bf16[2048,1120]{0,1:T(8,128)(2,1)S(1)} %copy-done.95, bf16[1120,1536]{1,0:T(8,128)(2,1)S(1)} %copy-done.66), kind=kOutput, calls=%fused_computation.15 | convolution fusion | flops 7049576448 | bytes 14319616 | tf_op jit(solution)/shard_map/dot_general | solution.py:57
  361.2 7.6 %convolution_convert_fusion.1 = bf16[1536,1120]{0,1:T(8,128)(2,1)S(1)} fusion(bf16[2048,1120]{0,1:T(8,128)(2,1)S(1)} %bitcast.549, bf16[2048,1536]{1,0:T(8,128)(2,1)S(1)} %bitcast.459), kind=kOutput, calls=%fused_computation.16 | convolution fusion | flops 7048151040 | bytes 14319616 | tf_op jit(solution)/shard_map/dot_general | solution.py:67
  368.7 11.2 %fusion.198 = f32[2048,1536]{1,0:T(8,128)} fusion(bf16[2048,1120]{0,1:T(8,128)(2,1)S(1)} %bitcast.549, bf16[1536,1120]{0,1:T(8,128)(2,1)S(1)} %copy-done.64), kind=kOutput, calls=%fused_computation.459 | convolution fusion | flops 7046430720 | bytes 20611072 | tf_op jit(solution)/shard_map/dot_general | solution.py:61
  381.0 9.3 %convolution_convert_fusion.2 = bf16[1536,1120]{0,1:T(8,128)(2,1)S(1)} fusion(bf16[2048,1120]{0,1:T(8,128)(2,1)} %get-tuple-element.28, bf16[2048,1536]{1,0:T(8,128)(2,1)S(1)} %bitcast.460), kind=kOutput, calls=%fused_computation.17 | convolution fusion | flops 7048151040 | bytes 14319616 | tf_op jit(solution)/shard_map/dot_general | solution.py:67
  394.7 13.4 %add_convert_fusion = bf16[2048,1536]{1,0:T(8,128)(2,1)S(1)} fusion(f32[2048,1536]{1,0:T(8,128)} %fusion.198, bf16[2048,1120]{0,1:T(8,128)(2,1)} %get-tuple-element.28, bf16[1536,1120]{0,1:T(8,128)(2,1)} %constant_dynamic-update-slice_fusion.4), kind=kOutput, calls=%fused_computation.2 | convolution fusion | flops 7052722176 | bytes 26902528 | tf_op jit(solution)/shard_map/dot_general | solution.py:61
  414.9 7.5 %collective-permute-done.90 = bf16[384,1120]{0,1:T(8,128)(2,1)} collective-permute-done((bf16[384,1120]{0,1:T(8,128)(2,1)}, bf16[384,1120]{0,1:T(8,128)(2,1)}, u32[]{:S(2)}, u32[]{:S(2)}) %collective-permute-start.90) | collective-permute-done | bytes 860192 | tf_op jit(solution)/shard_map/ppermute | solution.py:111
  423.8 16.5 %collective-permute-done.87 = bf16[384,1120]{0,1:T(8,128)(2,1)S(1)} collective-permute-done((bf16[384,1120]{0,1:T(8,128)(2,1)}, bf16[384,1120]{0,1:T(8,128)(2,1)S(1)}, u32[]{:S(2)}, u32[]{:S(2)}) %collective-permute-start.87) | collective-permute-done | bytes 860192 | tf_op jit(solution)/shard_map/ppermute | solution.py:111
  450.4 14.7 %collective-permute-done.94 = bf16[1120,384]{1,0:T(8,128)(2,1)S(1)} collective-permute-done((bf16[1120,384]{1,0:T(8,128)(2,1)S(1)}, bf16[1120,384]{1,0:T(8,128)(2,1)S(1)}, u32[]{:S(2)}, u32[]{:S(2)}) %collective-permute-start.94) | collective-permute-done | bytes 860192 | tf_op jit(solution)/shard_map/ppermute | solution.py:111
  468.1 15.3 %collective-permute-done.91 = bf16[384,1120]{0,1:T(8,128)(2,1)S(1)} collective-permute-done((bf16[384,1120]{0,1:T(8,128)(2,1)S(1)}, bf16[384,1120]{0,1:T(8,128)(2,1)S(1)}, u32[]{:S(2)}, u32[]{:S(2)}) %collective-permute-start.91) | collective-permute-done | bytes 860192 | tf_op jit(solution)/shard_map/ppermute | solution.py:111
  485.2 15.4 %collective-permute-done.88 = bf16[384,1120]{0,1:T(8,128)(2,1)S(1)} collective-permute-done((bf16[384,1120]{0,1:T(8,128)(2,1)S(1)}, bf16[384,1120]{0,1:T(8,128)(2,1)S(1)}, u32[]{:S(2)}, u32[]{:S(2)}) %collective-permute-start.88) | collective-permute-done | bytes 860192 | tf_op jit(solution)/shard_map/ppermute | solution.py:111
  506.0 18.4 %collective-permute-done.95 = bf16[1120,384]{1,0:T(8,128)(2,1)S(1)} collective-permute-done((bf16[1120,384]{1,0:T(8,128)(2,1)S(1)}, bf16[1120,384]{1,0:T(8,128)(2,1)S(1)}, u32[]{:S(2)}, u32[]{:S(2)}) %collective-permute-start.95) | collective-permute-done | bytes 860192 | tf_op jit(solution)/shard_map/ppermute | solution.py:111
  529.8 13.1 %collective-permute-done.92 = bf16[384,1120]{0,1:T(8,128)(2,1)S(1)} collective-permute-done((bf16[384,1120]{0,1:T(8,128)(2,1)S(1)}, bf16[384,1120]{0,1:T(8,128)(2,1)S(1)}, u32[]{:S(2)}, u32[]{:S(2)}) %collective-permute-start.92) | collective-permute-done | bytes 860192 | tf_op jit(solution)/shard_map/ppermute | solution.py:111
  648.3 9.8 %collective-permute-done.70 = bf16[2,4,49,512]{3,2,1,0:T(8,128)(2,1)S(1)} collective-permute-done((bf16[2,4,49,512]{3,2,1,0:T(8,128)(2,1)S(1)}, bf16[2,4,49,512]{3,2,1,0:T(8,128)(2,1)S(1)}, u32[]{:S(2)}, u32[]{:S(2)}) %collective-permute-start.70) | collective-permute-done | bytes 401440 | tf_op jit(solution)/shard_map/ppermute | solution.py:80
  673.9 20.4 %collective-permute-done.82 = bf16[2,4,48,1536]{3,2,1,0:T(8,128)(2,1)S(1)} collective-permute-done((bf16[2,4,48,1536]{3,2,1,0:T(8,128)(2,1)S(1)}, bf16[2,4,48,1536]{3,2,1,0:T(8,128)(2,1)S(1)}, u32[]{:S(2)}, u32[]{:S(2)}) %collective-permute-start.82) | collective-permute-done | bytes 1179680 | tf_op jit(solution)/shard_map/ppermute | solution.py:80
  698.5 10.1 %collective-permute-done.83 = bf16[1,4,48,1536]{3,2,1,0:T(8,128)(2,1)S(1)} collective-permute-done((bf16[1,4,48,1536]{3,2,1,0:T(8,128)(2,1)S(1)}, bf16[1,4,48,1536]{3,2,1,0:T(8,128)(2,1)S(1)}, u32[]{:S(2)}, u32[]{:S(2)}) %collective-permute-start.83) | collective-permute-done | bytes 589856 | tf_op jit(solution)/shard_map/ppermute | solution.py:80
  (696 shorter events, 427.3 us)
Async XLA Ops:
  5.5 39.2 %collective-permute-start = (bf16[49,512]{1,0:T(8,128)(2,1)}, bf16[49,512]{1,0:T(8,128)(2,1)S(1)}, u32[]{:S(2)}, u32[]{:S(2)}) collective-permute-start(bf16[49,512]{1,0:T(8,128)(2,1)} %get-tuple-element.108), channel_id=1, source_target_pairs={{0,8},{8,16},{16,24},{24,0},{1,9},{9,17},{17,25},{25,1},{2,10},{10... | collective-permute-start | bytes 150536 | tf_op jit(solution)/shard_map/ppermute | solution.py:118
  8.5 39.6 %collective-permute-start.1 = (bf16[49,512]{1,0:T(8,128)(2,1)}, bf16[49,512]{1,0:T(8,128)(2,1)S(1)}, u32[]{:S(2)}, u32[]{:S(2)}) collective-permute-start(bf16[49,512]{1,0:T(8,128)(2,1)} %get-tuple-element.108), channel_id=1, source_target_pairs={{0,16},{8,24},{16,0},{24,8},{1,17},{9,25},{17,1},{25,9},{2,18},{10... | collective-permute-start | bytes 150536 | tf_op jit(solution)/shard_map/ppermute | solution.py:118
  58.6 52.0 %collective-permute-start.39 = (bf16[384,1120]{0,1:T(8,128)(2,1)S(1)}, bf16[384,1120]{0,1:T(8,128)(2,1)}, u32[]{:S(2)}, u32[]{:S(2)}) collective-permute-start(bf16[384,1120]{0,1:T(8,128)(2,1)S(1)} %copy-done.57), channel_id=1, source_target_pairs={{0,8},{8,16},{16,24},{24,0},{1,9},{9,17},{17,25},{25,1},{2,10},{10... | collective-permute-start | bytes 2580488 | tf_op jit(solution)/shard_map/ppermute | solution.py:104
  65.9 46.9 %collective-permute-start.42 = (bf16[1120,384]{1,0:T(8,128)(2,1)}, bf16[1120,384]{1,0:T(8,128)(2,1)}, u32[]{:S(2)}, u32[]{:S(2)}) collective-permute-start(bf16[1120,384]{1,0:T(8,128)(2,1)} %param.33), channel_id=1, source_target_pairs={{0,8},{8,16},{16,24},{24,0},{1,9},{9,17},{17,25},{25,1},{2,10},{10... | collective-permute-start | bytes 2580488 | tf_op jit(solution)/shard_map/ppermute | solution.py:104
  79.9 42.7 %collective-permute-start.36 = (bf16[384,1120]{0,1:T(8,128)(2,1)S(1)}, bf16[384,1120]{0,1:T(8,128)(2,1)}, u32[]{:S(2)}, u32[]{:S(2)}) collective-permute-start(bf16[384,1120]{0,1:T(8,128)(2,1)S(1)} %copy-done.59), channel_id=1, source_target_pairs={{0,8},{8,16},{16,24},{24,0},{1,9},{9,17},{17,25},{25,1},{2,10},{10... | collective-permute-start | bytes 2580488 | tf_op jit(solution)/shard_map/ppermute | solution.py:104
  112.8 71.8 %collective-permute-start.19 = (bf16[2,4,48,1536]{3,2,1,0:T(8,128)(2,1)}, bf16[2,4,48,1536]{3,2,1,0:T(8,128)(2,1)}, u32[]{:S(2)}, u32[]{:S(2)}) collective-permute-start(bf16[2,4,48,1536]{3,2,1,0:T(8,128)(2,1)} %pad_maximum_fusion.10), channel_id=1, source_target_pairs={{0,4},{1,5},{2,6},{3,7},{4,0},{5,1},{6,2},{7,3},{8,12},{9,13},{10,... | collective-permute-start | bytes 3538952 | tf_op jit(solution)/shard_map/ppermute | solution.py:80
  125.4 39.8 %collective-permute-start.43 = (bf16[1120,384]{1,0:T(8,128)(2,1)}, bf16[1120,384]{1,0:T(8,128)(2,1)}, u32[]{:S(2)}, u32[]{:S(2)}) collective-permute-start(bf16[1120,384]{1,0:T(8,128)(2,1)} %collective-permute-done.42), channel_id=1, source_target_pairs={{0,8},{8,16},{16,24},{24,0},{1,9},{9,17},{17,25},{25,1},{2,10},{10... | collective-permute-start | bytes 2580488 | tf_op jit(solution)/shard_map/ppermute | solution.py:104
  127.4 53.6 %collective-permute-start.37 = (bf16[384,1120]{0,1:T(8,128)(2,1)}, bf16[384,1120]{0,1:T(8,128)(2,1)}, u32[]{:S(2)}, u32[]{:S(2)}) collective-permute-start(bf16[384,1120]{0,1:T(8,128)(2,1)} %collective-permute-done.36), channel_id=1, source_target_pairs={{0,8},{8,16},{16,24},{24,0},{1,9},{9,17},{17,25},{25,1},{2,10},{10... | collective-permute-start | bytes 2580488 | tf_op jit(solution)/shard_map/ppermute | solution.py:104
  183.4 40.3 %collective-permute-start.44 = (bf16[1120,384]{1,0:T(8,128)(2,1)}, bf16[1120,384]{1,0:T(8,128)(2,1)}, u32[]{:S(2)}, u32[]{:S(2)}) collective-permute-start(bf16[1120,384]{1,0:T(8,128)(2,1)} %collective-permute-done.43), channel_id=1, source_target_pairs={{0,8},{8,16},{16,24},{24,0},{1,9},{9,17},{17,25},{25,1},{2,10},{10... | collective-permute-start | bytes 2580488 | tf_op jit(solution)/shard_map/ppermute | solution.py:104
  194.2 75.2 %collective-permute-start.53 = (bf16[4,128,1536]{2,1,0:T(8,128)(2,1)}, bf16[4,128,1536]{2,1,0:T(8,128)(2,1)}, u32[]{:S(2)}, u32[]{:S(2)}) collective-permute-start(bf16[4,128,1536]{2,1,0:T(8,128)(2,1)} %pad_maximum_fusion.8), channel_id=1, source_target_pairs={{0,1},{1,0},{2,3},{3,2},{4,5},{5,4},{6,7},{7,6},{8,9},{9,8},{10,11... | collective-permute-start | bytes 4718600 | tf_op jit(solution)/shard_map/ppermute | solution.py:80
  199.2 83.3 %collective-permute-start.56 = (bf16[4,128,1536]{2,1,0:T(8,128)(2,1)}, bf16[4,128,1536]{2,1,0:T(8,128)(2,1)}, u32[]{:S(2)}, u32[]{:S(2)}) collective-permute-start(bf16[4,128,1536]{2,1,0:T(8,128)(2,1)} %pad_maximum_fusion.9), channel_id=1, source_target_pairs={{0,1},{1,0},{2,3},{3,2},{4,5},{5,4},{6,7},{7,6},{8,9},{9,8},{10,11... | collective-permute-start | bytes 4718600 | tf_op jit(solution)/shard_map/ppermute | solution.py:80
  205.3 61.5 %collective-permute-start.38 = (bf16[384,1120]{0,1:T(8,128)(2,1)}, bf16[384,1120]{0,1:T(8,128)(2,1)}, u32[]{:S(2)}, u32[]{:S(2)}) collective-permute-start(bf16[384,1120]{0,1:T(8,128)(2,1)} %collective-permute-done.37), channel_id=1, source_target_pairs={{0,8},{8,16},{16,24},{24,0},{1,9},{9,17},{17,25},{25,1},{2,10},{10... | collective-permute-start | bytes 2580488 | tf_op jit(solution)/shard_map/ppermute | solution.py:104
  381.0 41.4 %collective-permute-start.90 = (bf16[384,1120]{0,1:T(8,128)(2,1)}, bf16[384,1120]{0,1:T(8,128)(2,1)}, u32[]{:S(2)}, u32[]{:S(2)}) collective-permute-start(bf16[384,1120]{0,1:T(8,128)(2,1)} %slice.959), channel_id=1, source_target_pairs={{0,8},{8,16},{16,24},{24,0},{1,9},{9,17},{17,25},{25,1},{2,10},{10... | collective-permute-start | bytes 2580488 | tf_op jit(solution)/shard_map/ppermute | solution.py:111
  391.4 48.9 %collective-permute-start.87 = (bf16[384,1120]{0,1:T(8,128)(2,1)}, bf16[384,1120]{0,1:T(8,128)(2,1)S(1)}, u32[]{:S(2)}, u32[]{:S(2)}) collective-permute-start(bf16[384,1120]{0,1:T(8,128)(2,1)} %slice.955), channel_id=1, source_target_pairs={{0,8},{8,16},{16,24},{24,0},{1,9},{9,17},{17,25},{25,1},{2,10},{10... | collective-permute-start | bytes 2580488 | tf_op jit(solution)/shard_map/ppermute | solution.py:111
  394.1 48.5 %collective-permute-start.45 = (bf16[4,128,1536]{2,1,0:T(8,128)(2,1)}, bf16[4,128,1536]{2,1,0:T(8,128)(2,1)}, u32[]{:S(2)}, u32[]{:S(2)}) collective-permute-start(bf16[4,128,1536]{2,1,0:T(8,128)(2,1)} %bitcast.56), channel_id=1, source_target_pairs={{0,1},{1,0},{2,3},{3,2},{4,5},{5,4},{6,7},{7,6},{8,9},{9,8},{10,11... | collective-permute-start | bytes 4718600 | tf_op jit(solution)/shard_map/ppermute | solution.py:80
  394.2 50.4 %collective-permute-start.48 = (bf16[4,128,1536]{2,1,0:T(8,128)(2,1)}, bf16[4,128,1536]{2,1,0:T(8,128)(2,1)}, u32[]{:S(2)}, u32[]{:S(2)}) collective-permute-start(bf16[4,128,1536]{2,1,0:T(8,128)(2,1)} %bitcast.58), channel_id=1, source_target_pairs={{0,1},{1,0},{2,3},{3,2},{4,5},{5,4},{6,7},{7,6},{8,9},{9,8},{10,11... | collective-permute-start | bytes 4718600 | tf_op jit(solution)/shard_map/ppermute | solution.py:80
  442.6 40.8 %collective-permute-start.91 = (bf16[384,1120]{0,1:T(8,128)(2,1)S(1)}, bf16[384,1120]{0,1:T(8,128)(2,1)S(1)}, u32[]{:S(2)}, u32[]{:S(2)}) collective-permute-start(bf16[384,1120]{0,1:T(8,128)(2,1)S(1)} %add_convert_fusion.6), channel_id=1, source_target_pairs={{0,8},{8,16},{16,24},{24,0},{1,9},{9,17},{17,25},{25,1},{2,10},{10... | collective-permute-start | bytes 2580488 | tf_op jit(solution)/shard_map/ppermute | solution.py:111
  444.6 56.0 %collective-permute-start.88 = (bf16[384,1120]{0,1:T(8,128)(2,1)S(1)}, bf16[384,1120]{0,1:T(8,128)(2,1)S(1)}, u32[]{:S(2)}, u32[]{:S(2)}) collective-permute-start(bf16[384,1120]{0,1:T(8,128)(2,1)S(1)} %add_convert_fusion.8), channel_id=1, source_target_pairs={{0,8},{8,16},{16,24},{24,0},{1,9},{9,17},{17,25},{25,1},{2,10},{10... | collective-permute-start | bytes 2580488 | tf_op jit(solution)/shard_map/ppermute | solution.py:111
  447.2 54.6 %collective-permute-start.46 = (bf16[2,128,1536]{2,1,0:T(8,128)(2,1)S(1)}, bf16[2,128,1536]{2,1,0:T(8,128)(2,1)S(1)}, u32[]{:S(2)}, u32[]{:S(2)}) collective-permute-start(bf16[2,128,1536]{2,1,0:T(8,128)(2,1)S(1)} %slice.858), channel_id=1, source_target_pairs={{0,4},{1,5},{2,6},{3,7},{4,0},{5,1},{6,2},{7,3},{8,12},{9,13},{10,... | collective-permute-start | bytes 2359304 | tf_op jit(solution)/shard_map/ppermute | solution.py:80
  448.3 53.7 %collective-permute-start.49 = (bf16[2,128,1536]{2,1,0:T(8,128)(2,1)S(1)}, bf16[2,128,1536]{2,1,0:T(8,128)(2,1)S(1)}, u32[]{:S(2)}, u32[]{:S(2)}) collective-permute-start(bf16[2,128,1536]{2,1,0:T(8,128)(2,1)S(1)} %slice.864), channel_id=1, source_target_pairs={{0,2},{1,3},{2,0},{3,1},{4,6},{5,7},{6,4},{7,5},{8,10},{9,11},{10,... | collective-permute-start | bytes 2359304 | tf_op jit(solution)/shard_map/ppermute | solution.py:80
  501.8 41.1 %collective-permute-start.92 = (bf16[384,1120]{0,1:T(8,128)(2,1)S(1)}, bf16[384,1120]{0,1:T(8,128)(2,1)S(1)}, u32[]{:S(2)}, u32[]{:S(2)}) collective-permute-start(bf16[384,1120]{0,1:T(8,128)(2,1)S(1)} %add_convert_fusion.5), channel_id=1, source_target_pairs={{0,8},{8,16},{16,24},{24,0},{1,9},{9,17},{17,25},{25,1},{2,10},{10... | collective-permute-start | bytes 2580488 | tf_op jit(solution)/shard_map/ppermute | solution.py:111
  502.0 143.4 %collective-permute-start.89 = (bf16[384,1120]{0,1:T(8,128)(2,1)}, bf16[384,1120]{0,1:T(8,128)(2,1)}, u32[]{:S(2)}, u32[]{:S(2)}) collective-permute-start(bf16[384,1120]{0,1:T(8,128)(2,1)} %add_convert_fusion.7), channel_id=1, source_target_pairs={{0,8},{8,16},{16,24},{24,0},{1,9},{9,17},{17,25},{25,1},{2,10},{10... | collective-permute-start | bytes 2580488 | tf_op jit(solution)/shard_map/ppermute | solution.py:111
  503.4 41.3 %collective-permute-start.47 = (bf16[1,128,1536]{2,1,0:T(8,128)(2,1)S(1)}, bf16[1,128,1536]{2,1,0:T(8,128)(2,1)S(1)}, u32[]{:S(2)}, u32[]{:S(2)}) collective-permute-start(bf16[1,128,1536]{2,1,0:T(8,128)(2,1)S(1)} %slice.860), channel_id=1, source_target_pairs={{0,2},{1,3},{2,0},{3,1},{4,6},{5,7},{6,4},{7,5},{8,10},{9,11},{10,... | collective-permute-start | bytes 1179656 | tf_op jit(solution)/shard_map/ppermute | solution.py:80
  505.2 39.7 %collective-permute-start.50 = (bf16[1,128,1536]{2,1,0:T(8,128)(2,1)S(1)}, bf16[1,128,1536]{2,1,0:T(8,128)(2,1)S(1)}, u32[]{:S(2)}, u32[]{:S(2)}) collective-permute-start(bf16[1,128,1536]{2,1,0:T(8,128)(2,1)S(1)} %slice.866), channel_id=1, source_target_pairs={{0,4},{1,5},{2,6},{3,7},{4,0},{5,1},{6,2},{7,3},{8,12},{9,13},{10,... | collective-permute-start | bytes 1179656 | tf_op jit(solution)/shard_map/ppermute | solution.py:80
  (184 other events, 2685.8 us)

commit v2 on v0

--- a/solution.py
+++ b/solution.py
@@ -1,8 +1,12 @@
+import functools
 import math
 
 import jax
 import jax.numpy as jnp
+import numpy as np
 from jax import lax
+from jax.experimental import pallas as pl
+from jax.experimental.pallas import tpu as pltpu
 from jax.sharding import PartitionSpec as P
 
 Q_HEADS = 12
@@ -59,7 +63,7 @@
     return (d_gate, d_up)
 
 
-def on_device(
+def plain_device(
     layer_in,
     seg_ids,
     pad_mask,
@@ -257,9 +261,926 @@
     )
 
 
+F32 = jnp.float32
+BF16 = jnp.bfloat16
+VMEM_BYTES = 58 * 1024 * 1024
+ROWS = 2
+PARTS = 8
+WIDE = 4
+SEG = 128
+SHARE = 48
+GROUP = Q_HEADS // KV_HEADS
+SCALE = 1.0 / math.sqrt(HEAD)
+TOKENS = ROWS * SEG
+ROW_LEN = SEG * PARTS
+KV_BLOCK = SHARE + 16
+TILE = 512
+
+
+def dot_nn(left, right):
+    return lax.dot_general(left, right, (((1,), (0,)), ((), ())), preferred_element_type=F32)
+
+
+def dot_nt(left, right):
+    return lax.dot_general(left, right, (((1,), (1,)), ((), ())), preferred_element_type=F32)
+
+
+def flipped(value):
+    return value.astype(F32).T.astype(BF16)
+
+
+class Links:
+    def __init__(self):
+        self.orders = ((2, 4, 1), (4, 2, 1))
+
+    def hop(self, value, bit):
+        return lax.ppermute(value, "narrow", [(i, i ^ bit) for i in range(PARTS)])
+
+    def offsets(self, which):
+        found = [0]
+        for bit in self.orders[which]:
+            found = found + [o ^ bit for o in found]
+        return found
+
+    def near(self, value, which):
+        return jnp.concatenate([value, self.hop(value, self.orders[which][0])], axis=0)
+
+    def rest(self, near, which):
+        _, second, core = self.orders[which]
+        far = self.hop(near, second)
+        return [near, far, self.hop(near, core), self.hop(far, core)]
+
+    def gather(self, value, which):
+        return self.rest(self.near(value, which), which)
+
+    def scatter_core(self, own, other):
+        return own + self.hop(other, 1)
+
+    def scatter_second(self, held, which):
+        half = held.shape[0] // 2
+        return held[:half] + self.hop(held[half:], self.orders[which][1])
+
+    def scatter_first(self, held, which):
+        half = held.shape[0] // 2
+        return held[:half], self.hop(held[half:], self.orders[which][0])
+
+    def scatter(self, own, other, which):
+        held = self.scatter_second(self.scatter_core(own, other), which)
+        return self.scatter_first(held, which)
+
+    def over_wide(self, value, step):
+        return lax.ppermute(value, "wide", [(i, (i + step) % WIDE) for i in range(WIDE)])
+
+    def direct_gather(self, value):
+        return [value] + [self.over_wide(value, k) for k in range(1, WIDE)]
+
+    def direct_scatter(self, near, far):
+        slots = (near + far).reshape((WIDE, near.shape[0] // WIDE) + near.shape[1:])
+        total = slots[0].astype(F32)
+        for k in range(1, WIDE):
+            total = total + self.over_wide(slots[k], -k).astype(F32)
+        return total
+
+
+def after(values, *earlier):
+    return lax.optimization_barrier((values, earlier))[0]
+
+
+def in_vmem(count):
+    return [pl.BlockSpec(memory_space=pltpu.VMEM)] * count
+
+
+def in_smem(count):
+    return [pl.BlockSpec(memory_space=pltpu.SMEM)] * count
+
+
+def anywhere(count):
+    return [pl.BlockSpec(memory_space=pl.ANY)] * count
+
+
+def call(body, outs, scratch, in_specs, out_specs, flops, nbytes, grid=None, name=None):
+    return pl.pallas_call(
+        body,
+        out_shape=outs,
+        grid=grid if grid is not None else (),
+        in_specs=in_specs,
+        out_specs=out_specs,
+        scratch_shapes=scratch,
+        name=name,
+        compiler_params=pltpu.CompilerParams(vmem_limit_bytes=VMEM_BYTES),
+        cost_estimate=pl.CostEstimate(flops=int(flops) // 10, bytes_accessed=int(nbytes) // 10, transcendentals=0),
+    )
+
+
+def shaped(*dims, dtype=BF16):
+    return jax.ShapeDtypeStruct(dims, dtype)
+
+
+def weight_copies(pieces, held, starts, sems, stride, columns):
+    copies = []
+    for i in range(PARTS * WIDE):
+        piece = pieces[i // 8]
+        copies.append(
+            pltpu.make_async_copy(
+                piece.at[pl.ds((i % 8) * stride, SHARE), :],
+                held.at[pl.ds(pl.multiple_of(starts[i], 16), SHARE), columns],
+                sems.at[i],
+            )
+        )
+    return copies
+
+
+def grad_copies(held, own, other, starts, sems, stride, columns):
+    copies = []
+    for i in range(PARTS * WIDE):
+        target = own if i < 16 else other
+        copies.append(
+            pltpu.make_async_copy(
+                held.at[pl.ds(pl.multiple_of(starts[i], 16), SHARE), columns],
+                target.at[pl.ds((i % 16) * stride, SHARE), :],
+                sems.at[i],
+            )
+        )
+    return copies
+
+
+def half_copies(pieces, held, starts_a, starts_b, sems):
+    half = held.shape[1] // 2
+    return weight_copies(
+        pieces[:4], held, starts_a, sems.at[0], SHARE, slice(0, half)
+    ) + weight_copies(pieces[4:], held, starts_b, sems.at[1], SHARE, slice(half, 2 * half))
+
+
+def half_grad_copies(held, outs, starts_a, starts_b, sems):
+    half = held.shape[1] // 2
+    return grad_copies(
+        held, outs[0], outs[1], starts_a, sems.at[0], SHARE, slice(0, half)
+    ) + grad_copies(held, outs[2], outs[3], starts_b, sems.at[1], SHARE, slice(half, 2 * half))
+
+
+def vector_masks(start_column, lanes, block):
+    at = lax.broadcasted_iota(jnp.int32, (PARTS * WIDE, lanes), 1)
+    return (at >= start_column) & (at < start_column + block)
+
+
+def turn(value, cosine, sine):
+    return value * cosine + pltpu.roll(value, HEAD // 2, 1) * sine
+
+
+def project_kv(starts, x, cosine, sine, begin, begin_small, pick, pick_k, pick_v, *refs):
+    pieces, (kv_out, h_out, vec_out, held, vecs, sems, vec_sems) = refs[:4], refs[4:]
+    copies = weight_copies(pieces, held, starts, sems, KV_BLOCK, slice(None))
+    for i in range(PARTS * WIDE):
+        copies.append(
+            pltpu.make_async_copy(
+                pieces[i // 8].at[pl.ds((i % 8) * KV_BLOCK + SHARE, 16), :],
+                vecs.at[pl.ds(16 * i, 16), :],
+                vec_sems.at[i],
+            )
+        )
+    for copy in copies:
+        copy.start()
+    value = x[...].astype(F32)
+    unit = value * lax.rsqrt(jnp.mean(value * value, axis=-1, keepdims=True) + EPS)
+    for copy in copies:
+        copy.wait()
+    row = lax.broadcasted_iota(jnp.int32, (32, 512), 0) * 16
+    col = lax.broadcasted_iota(jnp.int32, (32, 512), 1)
+    packed = dot_nn((row == col).astype(BF16), vecs[...]).astype(BF16)
+    mask = vector_masks(begin[...], HQ, SHARE)
+    mask_small = vector_masks(begin_small[...], HK, 8)
+
+    def spread(lane, chosen, where):
+        found = dot_nn(packed[:, lane : lane + 128], chosen[...])
+        return jnp.sum(jnp.where(where, found, 0.0), axis=0, keepdims=True)
+
+    g_one = spread(0, pick, mask)
+    vec_out[...] = jnp.concatenate(
+        [g_one, spread(128, pick, mask), spread(256, pick, mask), jnp.zeros((5, HQ), F32)], axis=0
+    )
+    b_key = spread(384, pick_k, mask_small)
+    b_value = spread(384, pick_v, mask_small)
+    h_one = (unit * g_one).astype(BF16)
+    h_out[...] = h_one
+    lin = dot_nn(h_one, held[...])
+    for head in range(KV_HEADS):
+        cut = slice(head * HEAD, (head + 1) * HEAD)
+        key = turn(lin[:, cut] + b_key[:, cut], cosine[...], sine[...])
+        kv_out[:, cut] = key.astype(BF16)
+    kv_out[:, HK:] = (lin[:, HK:] + b_value).astype(BF16)
+
+
+def project_q(starts_a, starts_b, h_one, vec, cosine, sine, *refs):
+    pieces, (q_out, held, sems) = refs[:8], refs[8:]
+    copies = half_copies(pieces, held, starts_a, starts_b, sems)
+    for copy in copies:
+        copy.start()
+    for copy in copies:
+        copy.wait()
+    lin = dot_nn(h_one[...], held[...]) + vec[2:3, :]
+    for head in range(Q_HEADS):
+        cut = slice(head * HEAD, (head + 1) * HEAD)
+        q_out[:, cut] = turn(lin[:, cut], cosine[...], sine[...]).astype(BF16)
+
+
+def stacked(ref, row, kv_head):
+    first = kv_head * GROUP
+    return jnp.concatenate(
+        [
+            ref[row * SEG : (row + 1) * SEG, (first + g) * HEAD : (first + g + 1) * HEAD]
+            for g in range(GROUP)
+        ],
+        axis=0,
+    )
+
+
+def row_keys(pieces, row, column):
+    return jnp.concatenate(
+        [piece[:, column : column + HEAD] for piece in pieces[4 * row : 4 * row + 4]], axis=0
+    )
+
+
+def attend(starts_a, starts_b, q, x, vec, barred, *refs):
+    kv, pieces = refs[:8], refs[8:16]
+    att_out, lse_out, mid_out, h_out, held, sems = refs[16:]
+    copies = half_copies(pieces, held, starts_a, starts_b, sems)
+    for copy in copies:
+        copy.start()
+    for row in range(ROWS):
+        bar = barred[row]
+        bar = jnp.concatenate([bar] * GROUP, axis=1)
+        for kv_head in range(KV_HEADS):
+            keys = row_keys(kv, row, kv_head * HEAD)
+            values = row_keys(kv, row, HK + kv_head * HEAD)
+            scores = dot_nt(keys, stacked(q, row, kv_head)) * SCALE + bar
+            top = jnp.max(scores, axis=0, keepdims=True)
+            expo = jnp.exp(scores - top)
+            total = jnp.sum(expo, axis=0, keepdims=True)
+            lse_out[row * KV_HEADS + kv_head] = top + jnp.log(total)
+            probs = (expo / total).astype(BF16)
+            out = dot_nn(flipped(values), probs)
+            for g in range(GROUP):
+                head = kv_head * GROUP + g
+                att_out[row * SEG : (row + 1) * SEG, head * HEAD : (head + 1) * HEAD] = (
+                    out[:, g * SEG : (g + 1) * SEG].T.astype(BF16)
+                )
+    for copy in copies:
+        copy.wait()
+    mid = x[...].astype(F32) + dot_nn(att_out[...], held[...])
+    mid_out[...] = mid
+    factor = lax.rsqrt(jnp.mean(mid * mid, axis=-1, keepdims=True) + EPS)
+    h_out[...] = (mid * factor * vec[1:2, :]).astype(BF16)
+
+
+def mlp_front(*refs):
+    h_pieces, wg, wu = refs[:8], refs[8], refs[9]
+    hid_out, hid_t_out, gate_out, up_out, h_all = refs[10:15]
+    h_v, w_v, sems, w_sems, out_sems = refs[15:]
+    step = pl.program_id(0)
+    rows = h_pieces[0].shape[0]
+    units = hid_out.shape[1]
+    second = w_v.shape[0] // 2
+
+    def pieces_in():
+        return [
+            pltpu.make_async_copy(h_pieces[i], h_v.at[pl.ds(i * rows, rows), :], sems.at[i])
+            for i in range(8)
+        ]
+
+    def weights_in():
+        return [
+            pltpu.make_async_copy(wg, w_v.at[pl.ds(0, units), :], w_sems.at[0]),
+            pltpu.make_async_copy(wu, w_v.at[pl.ds(second, units), :], w_sems.at[1]),
+        ]
+
+    def h_over(tile):
+        at = pl.ds(pl.multiple_of(tile * TILE, TILE), TILE)
+        return pltpu.make_async_copy(h_v.at[at, :], h_all.at[at, :], out_sems.at[tile])
+
+    @pl.when(step == 0)
+    def _():
+        held = pieces_in()
+        for copy in held[:2] + weights_in() + held[2:]:
+            copy.start()
+        gap = jnp.zeros((second - units, w_v.shape[1]), BF16)
+        w_v[units:second, :] = gap
+        w_v[second + units :, :] = gap
+
+    for tile in range(4):
+
+        @pl.when(step == tile)
+        def _(tile=tile):
+            for copy in pieces_in()[2 * tile : 2 * tile + 2]:
+                copy.wait()
+            h_over(tile).start()
+
+    @pl.when(step == 0)
+    def _():
+        for copy in weights_in():
+            copy.wait()
+
+    h = h_v[pl.ds(pl.multiple_of(step * TILE, TILE), TILE), :]
+    both = dot_nt(h, w_v[...])
+    gate = both[:, :units]
+    up = both[:, second : second + units]
+    gate_out[...] = gate.astype(BF16)
+    up_out[...] = up.astype(BF16)
+    hidden = (gate * jax.nn.sigmoid(gate) * up).astype(BF16)
+    hid_out[...] = hidden
+    hid_t_out[...] = hidden.T
+
+    @pl.when(step == 3)
+    def _():
+        for tile in range(4):
+            h_over(tile).wait()
+
+
+def mlp_back(grad, gate_in, up_in, wd, wg, wu, *refs):
+    dg_out, du_out, own_h, other_h, wd_v, w_v, d_v, sems = refs
+    step = pl.program_id(0)
+    units = gate_in.shape[1]
+    second = w_v.shape[0] // 2
+
+    def down_in():
+        return [pltpu.make_async_copy(wd, wd_v, sems.at[0])]
+
+    def weights_in():
+        return [
+            pltpu.make_async_copy(wg, w_v.at[pl.ds(0, units), :], sems.at[1]),
+            pltpu.make_async_copy(wu, w_v.at[pl.ds(second, units), :], sems.at[2]),
+        ]
+
+    @pl.when(step == 0)
+    def _():
+        for copy in down_in() + weights_in():
+            copy.start()
+        gap = jnp.zeros((second - units, w_v.shape[1]), BF16)
+        w_v[units:second, :] = gap
+        w_v[second + units :, :] = gap
+        gap = jnp.zeros((TILE, second - units), BF16)
+        d_v[:, units:second] = gap
+        d_v[:, second + units :] = gap
+        for copy in down_in():
+            copy.wait()
+
+    d_hidden = dot_nt(grad[...], wd_v[...])
+    gate = gate_in[...].astype(F32)
+    up = up_in[...].astype(F32)
+    sigma = jax.nn.sigmoid(gate)
+    d_gate = (d_hidden * up * sigma * (1.0 + gate * (1.0 - sigma))).astype(BF16)
+    d_up = (d_hidden * (gate * sigma)).astype(BF16)
+    dg_out[...] = d_gate.T
+    du_out[...] = d_up.T
+    d_v[:, :units] = d_gate
+    d_v[:, second : second + units] = d_up
+
+    @pl.when(step == 0)
+    def _():
+        for copy in weights_in():
+            copy.wait()
+
+    d_h = dot_nn(d_v[...], w_v[...]).astype(BF16)
+
+    @pl.when(step % 2 == 0)
+    def _():
+        own_h[...] = d_h
+
+    @pl.when(step % 2 == 1)
+    def _():
+        other_h[...] = d_h
+
+
+def mlp_down(hid, wd, own_m, other_m):
+    step = pl.program_id(0)
+    mixed = dot_nn(hid[...], wd[...]).astype(BF16)
+
+    @pl.when(step % 2 == 0)
+    def _():
+        own_m[...] = mixed
+
+    @pl.when(step % 2 == 1)
+    def _():
+        other_m[...] = mixed
+
+
+def weight_grad(left, right, out):
+    found = dot_nn(left[...], right[...]).astype(BF16)
+    cut = out.shape[2]
+    out[0] = found[:, :cut]
+    out[1] = found[:, cut:]
+
+
+def branch_back(starts_a, starts_b, keep_a, got_a, keep_b, got_b, mid, grad, vec, att, *refs):
+    pieces, (d_mid_out, d_att_out, d_gain_out), outs = refs[:8], refs[8:11], refs[11:15]
+    held, held_d, sems, out_sems = refs[15:]
+    copies = half_copies(pieces, held, starts_a, starts_b, sems)
+    for copy in copies:
+        copy.start()
+    d_h = jnp.concatenate(
+        [
+            keep_a[...].astype(F32) + got_a[...].astype(F32),
+            keep_b[...].astype(F32) + got_b[...].astype(F32),
+        ],
+        axis=0,
+    )
+    x_mid = mid[...]
+    factor = lax.rsqrt(jnp.mean(x_mid * x_mid, axis=-1, keepdims=True) + EPS)
+    unit = x_mid * factor
+    d_gain_out[...] = jnp.sum(d_h * unit, axis=0, keepdims=True)
+    d_mid = grad[...].astype(F32) + norm_back(d_h, unit, factor, vec[1:2, :])
+    d_mid_out[...] = d_mid
+    d_branch = d_mid.astype(BF16)
+    held_d[...] = dot_nn(flipped(att[...]), d_branch).astype(BF16)
+    out_copies = half_grad_copies(held_d, outs, starts_a, starts_b, out_sems)
+    for copy in out_copies:
+        copy.start()
+    for copy in copies:
+        copy.wait()
+    d_att_out[...] = dot_nt(d_branch, held[...]).astype(BF16)
+    for copy in out_copies:
+        copy.wait()
+
+
+def attend_back(q, d_att, cosine, sine, barred, lse, *refs):
+    kv, (dq_out, own, other) = refs[:8], refs[8:]
+    for row in range(ROWS):
+        bar = barred[row]
+        bar = jnp.concatenate([bar] * GROUP, axis=1)
+        for kv_head in range(KV_HEADS):
+            keys = row_keys(kv, row, kv_head * HEAD)
+            values = row_keys(kv, row, HK + kv_head * HEAD)
+            queries = stacked(q, row, kv_head)
+            d_out = stacked(d_att, row, kv_head)
+            scores = dot_nt(keys, queries) * SCALE + bar
+            probs = jnp.exp(scores - lse[row * KV_HEADS + kv_head])
+            d_prob = dot_nt(values, d_out)
+            delta = jnp.sum(probs * d_prob, axis=0, keepdims=True)
+            d_score = (SCALE * probs * (d_prob - delta)).astype(BF16)
+            d_value = dot_nn(probs.astype(BF16), d_out).astype(BF16)
+            d_key = dot_nn(d_score, queries).astype(BF16)
+            half = ROW_LEN // 2
+            cut = slice(kv_head * HEAD, (kv_head + 1) * HEAD)
+            cut_v = slice(HK + kv_head * HEAD, HK + (kv_head + 1) * HEAD)
+            own[row, :, cut] = d_key[:half]
+            other[row, :, cut] = d_key[half:]
+            own[row, :, cut_v] = d_value[:half]
+            other[row, :, cut_v] = d_value[half:]
+            d_query = dot_nn(flipped(keys), d_score)
+            at = slice(row * SEG, (row + 1) * SEG)
+            for g in range(GROUP):
+                head = kv_head * GROUP + g
+                back = turn(d_query[:, g * SEG : (g + 1) * SEG].T, cosine[at, :], -sine[at, :])
+                dq_out[at, head * HEAD : (head + 1) * HEAD] = back.astype(BF16)
+
+
+def query_back(starts_a, starts_b, dq, h_one, *refs):
+    pieces, (d_h_out, d_bias_out), outs = refs[:8], refs[8:10], refs[10:14]
+    held, held_d, sems, out_sems = refs[14:]
+    copies = half_copies(pieces, held, starts_a, starts_b, sems)
+    for copy in copies:
+        copy.start()
+    held_d[...] = dot_nn(flipped(h_one[...]), dq[...]).astype(BF16)
+    out_copies = half_grad_copies(held_d, outs, starts_a, starts_b, out_sems)
+    for copy in out_copies:
+        copy.start()
+    d_bias_out[...] = jnp.sum(dq[...].astype(F32), axis=0, keepdims=True)
+    for copy in copies:
+        copy.wait()
+    d_h_out[...] = dot_nt(dq[...], held[...])
+    for copy in out_copies:
+        copy.wait()
+
+
+def kv_back(
+    starts, keep_a, got_a, keep_b, got_b, x, h_one, vec, cosine, sine, d_h_q, d_mid, d_gain, d_bias,
+    begin, begin_small, pick, pick_k, pick_v, *refs,
+):
+    pieces, (grad_out, own, other, held, held_d, vecs, sems, out_sems, vec_sems) = refs[:4], refs[4:]
+    copies = weight_copies(pieces, held, starts, sems, KV_BLOCK, slice(None))
+    for copy in copies:
+        copy.start()
+    d_kv = jnp.concatenate(
+        [
+            keep_a[...].astype(F32) + got_a[...].astype(F32),
+            keep_b[...].astype(F32) + got_b[...].astype(F32),
+        ],
+        axis=0,
+    )
+    parts = [
+        turn(d_kv[:, head * HEAD : (head + 1) * HEAD], cosine[...], -sine[...])
+        for head in range(KV_HEADS)
+    ]
+    d_lin = jnp.concatenate(parts + [d_kv[:, HK:]], axis=1).astype(BF16)
+    held_d[...] = dot_nn(flipped(h_one[...]), d_lin).astype(BF16)
+    out_copies = grad_copies(held_d, own, other, starts, out_sems, KV_BLOCK, slice(None))
+    for copy in out_copies:
+        copy.start()
+    for copy in copies:
+        copy.wait()
+    d_h = d_h_q[...] + dot_nt(d_lin, held[...])
+    value = x[...].astype(F32)
+    factor = lax.rsqrt(jnp.mean(value * value, axis=-1, keepdims=True) + EPS)
+    unit = value * factor
+    d_small = jnp.sum(d_lin.astype(F32), axis=0, keepdims=True)
+    mask = vector_masks(begin[...], HQ, SHARE)
+    mask_small = vector_masks(begin_small[...], HK, 8)
+
+    def collect(row, chosen, where):
+        return dot_nt(jnp.where(where, row, 0.0).astype(BF16), chosen[...])
+
+    packed = jnp.concatenate(
+        [
+            collect(jnp.sum(d_h * unit, axis=0, keepdims=True), pick, mask),
+            collect(d_gain[...], pick, mask),
+            collect(d_bias[...], pick, mask),
+            collect(d_small[:, :HK], pick_k, mask_small) + collect(d_small[:, HK:], pick_v, mask_small),
+        ],
+        axis=1,
+    ).astype(BF16)
+    row = lax.broadcasted_iota(jnp.int32, (512, 32), 0)
+    col = lax.broadcasted_iota(jnp.int32, (512, 32), 1) * 16
+    vecs[...] = dot_nn((row == col).astype(BF16), packed).astype(BF16)
+    vec_copies = [
+        pltpu.make_async_copy(
+            vecs.at[pl.ds(16 * i, 16), :],
+            (own if i < 16 else other).at[pl.ds((i % 16) * KV_BLOCK + SHARE, 16), :],
+            vec_sems.at[i],
+        )
+        for i in range(PARTS * WIDE)
+    ]
+    for copy in vec_copies:
+        copy.start()
+    grad_out[...] = (d_mid[...] + norm_back(d_h, unit, factor, vec[0:1, :])).astype(BF16)
+    for copy in out_copies + vec_copies:
+        copy.wait()
+
+
+def fast_device(
+    layer_in,
+    seg_ids,
+    pad_mask,
+    gain_attn,
+    w_query,
+    b_query,
+    w_key,
+    b_key,
+    w_value,
+    b_value,
+    w_out,
+    gain_mlp,
+    w_gate,
+    w_up,
+    w_down,
+    grad_out,
+):
+    width = layer_in.shape[2]
+    units = w_gate.shape[1]
+    links = Links()
+    here = lax.axis_index("wide")
+    me = lax.axis_index("narrow")
+    dma = pltpu.SemaphoreType.DMA
+    order = [0, 1]
+    x = layer_in.reshape(TOKENS, width)
+    grad = grad_out.reshape(TOKENS, width)
+
+    slots = (here - jnp.arange(WIDE, dtype=jnp.int32)) % WIDE * PARTS
+    blocks = [
+        ((me ^ jnp.array(links.offsets(o), jnp.int32))[:, None] + slots[None, :]).reshape(-1)
+        for o in order
+    ]
+    starts = [b * SHARE for b in blocks]
+    begin = starts[0][:, None]
+    begin_small = (blocks[0] * 8)[:, None]
+    lanes = np.arange(HQ)
+    pick = jnp.asarray((np.arange(128)[:, None] == lanes % SHARE).astype(np.float32), BF16)
+    pick_k = jnp.asarray((np.arange(128)[:, None] == lanes[:HK] % 8).astype(np.float32), BF16)
+    pick_v = jnp.asarray((np.arange(128)[:, None] == lanes[:HK] % 8 + 8).astype(np.float32), BF16)
+
+    def lane_pad(value, size):
+        return jnp.pad(value, (0, size - value.shape[0]))
+
+    packed = jnp.concatenate(
+        [
+            lane_pad(gain_attn, 128),
+            lane_pad(gain_mlp, 128),
+            lane_pad(b_query, 128),
+            lane_pad(jnp.concatenate([b_key, b_value]), 128),
+        ]
+    )[None]
+    kv_own = jnp.concatenate(
+        [jnp.concatenate([w_key, w_value], axis=1), jnp.pad(packed, ((0, 15), (0, 0)))], axis=0
+    )
+    half = HQ // 2
+
+    def two_halves(found):
+        return [
+            jnp.concatenate([s[:, :half] for s in found], axis=0),
+            jnp.concatenate([s[:, half:] for s in found], axis=0),
+        ]
+
+    kv_slots = jnp.concatenate(links.direct_gather(kv_own), axis=0)
+    q_slots = two_halves(links.direct_gather(w_query))
+    w_out, w_gate, w_up, w_down = after((w_out, w_gate, w_up, w_down), *q_slots)
+    o_slots = two_halves(links.direct_gather(w_out))
+    wg = lax.all_gather(w_gate.T, "wide", axis=1, tiled=True)
+    wu = lax.all_gather(w_up.T, "wide", axis=1, tiled=True)
+    wd = lax.all_gather(w_down, "wide", axis=1, tiled=True)
+    kv_weight = links.gather(kv_slots, 0)
+    q_weight = links.gather(q_slots[0], 0) + links.gather(q_slots[1], 1)
+    o_slots = after(o_slots, q_weight[1], q_weight[5])
+    o_weight = links.gather(o_slots[0], 0) + links.gather(o_slots[1], 1)
+
+    marks = jnp.stack(after((seg_ids, pad_mask), kv_slots), axis=1)
+    marks = jnp.stack([jnp.concatenate(links.gather(marks[r][None], order[r]), axis=0) for r in range(ROWS)])
+    ids_all = marks[:, :, 0].reshape(ROWS, ROW_LEN)
+    pads_all = marks[:, :, 1].reshape(ROWS, ROW_LEN)
+    sources = jnp.array([links.offsets(o) for o in order], jnp.int32) ^ me
+    key_idx = (
+        sources[:, :, None] * SEG + jnp.arange(SEG, dtype=jnp.int32)[None, None, :]
+    ).reshape(ROWS, ROW_LEN)
+    own_idx = me * SEG + jnp.arange(SEG, dtype=jnp.int32)
+    begins = jnp.sum((ids_all[:, None, :] < seg_ids[:, :, None]).astype(jnp.int32), axis=-1)
+    cosine, sine = angles((own_idx[None, :] - begins).reshape(TOKENS), HEAD)
+    cosine = jnp.concatenate([cosine, cosine], axis=-1)
+    sine = jnp.concatenate([-sine, sine], axis=-1)
+    allowed = (ids_all[:, :, None] == seg_ids[:, None, :]) & (
+        key_idx[:, :, None] < own_idx[None, None, :]
+    ) & (pads_all[:, :, None] == 1) | (key_idx[:, :, None] == own_idx[None, None, :])
+    barred = jnp.where(allowed, 0.0, -1e30).astype(F32)
+
+    kv, h_one, vec = call(
+        project_kv,
+        [shaped(TOKENS, 2 * HK), shaped(TOKENS, width), shaped(8, width, dtype=F32)],
+        [
+            pltpu.VMEM((width, 2 * HK), BF16),
+            pltpu.VMEM((512, 2 * HK), BF16),
+            dma((32,)),
+            dma((32,)),
+        ],
+        in_smem(1) + in_vmem(8) + anywhere(4),
+        in_vmem(3),
+        2 * TOKENS * width * 2 * HK,
+        4e6,
+        name="project_kv",
+    )(starts[0], x, cosine, sine, begin, begin_small, pick, pick_k, pick_v, *kv_weight)
+    kv_rows = []
+    for r in range(ROWS):
+        kv_rows += links.gather(kv[r * SEG : (r + 1) * SEG], order[r])
+    q = call(
+        project_q,
+        shaped(TOKENS, HQ),
+        [pltpu.VMEM((width, HQ), BF16), dma((2, 32))],
+        in_smem(2) + in_vmem(4) + anywhere(8),
+        pl.BlockSpec(memory_space=pltpu.VMEM),
+        2 * TOKENS * width * HQ,
+        7e6,
+        name="project_q",
+    )(starts[0], starts[1], h_one, vec, cosine, sine, *q_weight)
+    attended, lse, x_mid, h_two = call(
+        attend,
+        [
+            shaped(TOKENS, HQ),
+            shaped(ROWS * KV_HEADS, 1, GROUP * SEG, dtype=F32),
+            shaped(TOKENS, width, dtype=F32),
+            shaped(TOKENS, width),
+        ],
+        [pltpu.VMEM((HQ, width), BF16), dma((2, 32))],
+        in_smem(2) + in_vmem(4) + in_vmem(8) + anywhere(8),
+        in_vmem(4),
+        2 * TOKENS * width * HQ + 4 * TOKENS * ROW_LEN * HQ,
+        1e7,
+        name="attend",
+    )(*starts, q, x, vec, barred, *kv_rows, *o_weight)
+
+    at_row = [slice(r * SEG, (r + 1) * SEG) for r in range(ROWS)]
+    grad_near = [links.near(after(grad[at_row[r]], *kv_rows), order[r]) for r in range(ROWS)]
+    h_near = [links.near(h_two[at_row[r]], order[r]) for r in range(ROWS)]
+    grad_near = after(grad_near, *h_near)
+    h_pieces, grad_pieces = [], []
+    for r in range(ROWS):
+        h_pieces += links.rest(h_near[r], order[r])
+        grad_pieces += links.rest(grad_near[r], order[r])
+    many = ROWS * ROW_LEN
+    cut = width // WIDE
+    paired = 2 * -(-units // 128) * 128
+    tile_f = pl.BlockSpec((TILE, units), lambda t: (t, 0))
+    tile_t = pl.BlockSpec((units, TILE), lambda t: (0, t))
+    hidden, hidden_t, gate, up, h_all = call(
+        mlp_front,
+        [shaped(many, units), shaped(units, many), shaped(many, units), shaped(many, units)]
+        + [shaped(many, width)],
+        [
+            pltpu.VMEM((many, width), BF16),
+            pltpu.VMEM((paired, width), BF16),
+            dma((8,)),
+            dma((2,)),
+            dma((4,)),
+        ],
+        anywhere(10),
+        [tile_f, tile_t, tile_f, tile_f] + anywhere(1),
+        4 * many * width * units,
+        4e7,
+        grid=(many // TILE,),
+        name="mlp_front",
+    )(*h_pieces, wg, wu)
+    grad_all = jnp.concatenate(grad_pieces, axis=0)
+
+    def grad_of(left, right):
+        out = call(
+            weight_grad,
+            shaped(WIDE, units, cut),
+            [],
+            [
+                pl.BlockSpec((units, many), lambda k: (0, 0)),
+                pl.BlockSpec((many, 2 * cut), lambda k: (0, k)),
+            ],
+            pl.BlockSpec((2, units, cut), lambda k: (k, 0, 0)),
+            2 * many * width * units,
+            1.4e7,
+            grid=(WIDE // 2,),
+            name="weight_grad",
+        )(left, right)
+        return out
+
+    def sum_wide(slots):
+        return lax.psum_scatter(slots, "wide", scatter_dimension=0, tiled=False).astype(F32)
+
+    slots_d = grad_of(hidden_t, grad_all)
+    grad_w_down = sum_wide(slots_d)
+    tile_d = pl.BlockSpec((TILE, width), lambda t: (t, 0))
+    half_d = pl.BlockSpec((TILE, width), lambda t: (t // 2, 0))
+    d_gate, d_up, own_h, other_h = call(
+        mlp_back,
+        [shaped(units, many)] * 2 + [shaped(many // 2, width)] * 2,
+        [
+            pltpu.VMEM((units, width), BF16),
+            pltpu.VMEM((paired, width), BF16),
+            pltpu.VMEM((TILE, paired), BF16),
+            dma((3,)),
+        ],
+        [tile_d, tile_f, tile_f] + anywhere(3),
+        [tile_t, tile_t] + [half_d] * 2,
+        6 * many * width * units,
+        6e7,
+        grid=(many // TILE,),
+        name="mlp_back",
+    )(after(grad_all, slots_d), gate, up, wd, wg, wu)
+
+    def by_row(value):
+        size = value.shape[0] // ROWS
+        return [value[r * size : (r + 1) * size] for r in range(ROWS)]
+
+    def core_rows(own, other):
+        return by_row(links.scatter_core(own, other))
+
+    def second_rows(held):
+        return [links.scatter_second(held[r], order[r]) for r in range(ROWS)]
+
+    def first_rows(held):
+        found = []
+        for r in range(ROWS):
+            found += links.scatter_first(held[r], order[r])
+        return found
+
+    slots_g = grad_of(d_gate, h_all)
+    grad_w_gate = sum_wide(slots_g).T
+    held_h = core_rows(after(own_h, slots_g), other_h)
+    slots_u = grad_of(after(d_up, *held_h), h_all)
+    grad_w_up = sum_wide(slots_u).T
+    held_h = second_rows(held_h)
+    d_h = first_rows(held_h)
+    own_m, other_m = call(
+        mlp_down,
+        [shaped(many // 2, width)] * 2,
+        [],
+        [tile_f, pl.BlockSpec((units, width), lambda t: (0, 0))],
+        [half_d] * 2,
+        2 * many * width * units,
+        2e7,
+        grid=(many // TILE,),
+        name="mlp_down",
+    )(after(hidden, slots_u, *held_h), wd)
+    d_h = after(d_h, own_m)
+
+    def finish_weight(held):
+        near_a, far_a = links.scatter_first(held[0], 0)
+        near_b, far_b = links.scatter_first(held[1], 1)
+        return links.direct_scatter(
+            jnp.concatenate([near_a, near_b], axis=1), jnp.concatenate([far_a, far_b], axis=1)
+        )
+
+    blocks_half = 16 * SHARE
+    d_mid, d_att, d_gain, *halves_o = call(
+        branch_back,
+        [
+            shaped(TOKENS, width, dtype=F32),
+            shaped(TOKENS, HQ),
+            shaped(1, width, dtype=F32),
+        ]
+        + [shaped(blocks_half, half)] * 4,
+        [pltpu.VMEM((HQ, width), BF16), pltpu.VMEM((HQ, width), BF16), dma((2, 32)), dma((2, 32))],
+        in_smem(2) + in_vmem(8) + anywhere(8),
+        in_vmem(3) + anywhere(4),
+        4 * TOKENS * width * HQ,
+        1.5e7,
+        name="branch_back",
+    )(*starts, *d_h, x_mid, grad, vec, attended, *o_weight)
+    dq, own_kv, other_kv = call(
+        attend_back,
+        [shaped(TOKENS, HQ)] + [shaped(ROWS, ROW_LEN // 2, 2 * HK)] * 2,
+        [],
+        in_vmem(6) + in_vmem(8),
+        in_vmem(3),
+        10 * TOKENS * ROW_LEN * HQ,
+        1e7,
+        name="attend_back",
+    )(q, d_att, cosine, sine, barred, lse, *kv_rows)
+    held_kv = core_rows(own_kv.reshape(ROW_LEN, 2 * HK), other_kv.reshape(ROW_LEN, 2 * HK))
+    held_kv = second_rows(held_kv)
+    d_kv = first_rows(held_kv)
+    held_o = [
+        links.scatter_core(after(halves_o[0], dq), halves_o[1]),
+        links.scatter_core(after(halves_o[2], dq), halves_o[3]),
+    ]
+    d_h_q, d_bias, *halves_q = call(
+        query_back,
+        [shaped(TOKENS, width, dtype=F32), shaped(1, HQ, dtype=F32)] + [shaped(blocks_half, half)] * 4,
+        [pltpu.VMEM((width, HQ), BF16), pltpu.VMEM((width, HQ), BF16), dma((2, 32)), dma((2, 32))],
+        in_smem(2) + in_vmem(2) + anywhere(8),
+        in_vmem(2) + anywhere(4),
+        4 * TOKENS * width * HQ,
+        1.2e7,
+        name="query_back",
+    )(starts[0], starts[1], dq, h_one, *q_weight)
+    held_o = after(held_o, d_h_q)
+    grad_w_out = finish_weight([links.scatter_second(held_o[i], i) for i in range(2)])
+    held_q = [
+        links.scatter_core(halves_q[0], halves_q[1]),
+        links.scatter_core(halves_q[2], halves_q[3]),
+    ]
+    grad_w_query = finish_weight([links.scatter_second(held_q[i], i) for i in range(2)])
+    grad_in, own_w, other_w = call(
+        kv_back,
+        [shaped(TOKENS, width)] + [shaped(16 * KV_BLOCK, 2 * HK)] * 2,
+        [
+            pltpu.VMEM((width, 2 * HK), BF16),
+            pltpu.VMEM((width, 2 * HK), BF16),
+            pltpu.VMEM((512, 2 * HK), BF16),
+            dma((32,)),
+            dma((32,)),
+            dma((32,)),
+        ],
+        in_smem(1) + in_vmem(18) + anywhere(4),
+        in_vmem(1) + anywhere(2),
+        4 * TOKENS * width * 2 * HK,
+        1e7,
+        name="kv_back",
+    )(
+        starts[0], *d_kv, x, h_one, vec, cosine, sine, d_h_q, d_mid, d_gain, d_bias,
+        begin, begin_small, pick, pick_k, pick_v, *kv_weight,
+    )
+    kv_sum = links.direct_scatter(*links.scatter(own_w, other_w, 0))
+    mixed = first_rows(second_rows(core_rows(after(own_m, own_w), other_m)))
+    layer_out = (
+        x_mid
+        + jnp.concatenate([mixed[0], mixed[2]], axis=0).astype(F32)
+        + jnp.concatenate([mixed[1], mixed[3]], axis=0).astype(F32)
+    ).astype(BF16)
+    last = kv_sum[SHARE]
+    small = b_key.shape[0]
+    return (
+        layer_out.reshape(layer_in.shape),
+        grad_in.reshape(layer_in.shape),
+        last[:SHARE],
+        grad_w_query,
+        last[256 : 256 + SHARE],
+        kv_sum[:SHARE, :HK],
+        last[384 : 384 + small],
+        kv_sum[:SHARE, HK:],
+        last[384 + small : 384 + 2 * small],
+        grad_w_out,
+        last[128 : 128 + SHARE],
+        grad_w_gate,
+        grad_w_up,
+        grad_w_down,
+    )
+
+
+def choose(*args):
+    rows, seg_len, _ = args[0].shape
+    fits = (rows, seg_len, lax.axis_size("narrow"), lax.axis_size("wide"), args[4].shape[0]) == (
+        ROWS,
+        SEG,
+        PARTS,
+        WIDE,
+        SHARE,
+    )
+    return (fast_device if fits else plain_device)(*args)
+
+
 def solution(mesh):
     return jax.shard_map(
-        on_device,
+        choose,
         mesh=mesh,
         in_specs=(
             P("wide", "narrow", None),

time: 1830 us -> 558 us (0.30)
  waiting for transfers between devices: 1360 us -> 204 us
  matrix products: 200 us -> 0 us
  blocking collectives: 187 us -> 0 us
  Pallas kernels: 0 us -> 179 us
  starting transfers between devices: 1.7 us -> 81.8 us
    reduce_scatter x11 -> x3, waiting for transfers between devices: 979 us -> 0.02 us  [sum_wide(): lax.psum_scatter(slots, 'wide', scatter_dimension=0, tiled=False)]
    all_gather x9 -> x3, waiting for transfers between devices: 378 us -> 0.02 us  [the longest x1 0.02 us: fast_device(): wd = lax.all_gather(w_down, 'wide', axis=1, tiled=True)]
    ppermute x0 -> x100, waiting for transfers between devices: none -> 204 us  [the longest x82 151 us: hop(): return lax.ppermute(value, 'narrow', [(i, i ^ bit) for i in range(PARTS)])]
    dot_general x31 -> x0, matrix products: 189 us -> none  [the longest x1 19.4 us: on_device(): jnp.einsum('rtd,fd->rtf', grad_all, wd, preferred_element_type=f32)]
    pallas_call x0 -> x13, Pallas kernels: none -> 179 us  [the longest x3 36.1 us: grad_of(): call(weight_grad, shaped(WIDE, units, cut), [], [pl.BlockSpec((units, man...]
    all_gather x4 -> x0, blocking collectives: 98.7 us -> none  [the longest x1 42.7 us: on_device(): lax.all_gather(w_value, ('wide', 'narrow'), axis=0, tiled=True)]
    unnamed x2 -> x0, blocking collectives: 88 us -> none
    ppermute x0 -> x100, starting transfers between devices: none -> 81.1 us  [the longest x82 55.9 us: hop(): return lax.ppermute(value, 'narrow', [(i, i ^ bit) for i in range(PARTS)])]
  transfers between devices with their start and end apart: 20 -> 106, of which waited for: 18 -> 34; matrix products, arithmetic and copies ran while one was open for 9% -> 11% of each run, Pallas kernels for 0% -> 32%
where the time goes in v2:
time: 558 us; the launch traced here: 551 us
  waiting for transfers between devices  204 us (37%)
  Pallas kernels  179 us (32%)
  starting transfers between devices  81.8 us (15%)
  local copies, waits for them, and re-layouts  39.2 us (7%)
  other arithmetic  32.4 us (6%)
  between operations  15.6 us (3%)
    ppermute x82, waiting for transfers between devices, hop(): return lax.ppermute(value, 'narrow', [(i, i ^ bit) for i in range(PARTS)])  151 us
    ppermute x82, starting transfers between devices, hop(): return lax.ppermute(value, 'narrow', [(i, i ^ bit) for i in range(PARTS)])  55.9 us
    ppermute x18, waiting for transfers between devices, over_wide(): lax.ppermute(value, 'wide', [(i, (i + step) % WIDE) for i in range(WIDE)])  52.5 us
    pallas_call x3, Pallas kernels, grad_of(): call(weight_grad, shaped(WIDE, units, cut), [], [pl.BlockSpec((units, man...  36.1 us
    pallas_call x1, Pallas kernels, fast_device(): call(mlp_back, [shaped(units, many)] * 2 + [shaped(many // 2, width)] * 2...  35.2 us
    ppermute x18, starting transfers between devices, over_wide(): lax.ppermute(value, 'wide', [(i, (i + step) % WIDE) for i in range(WIDE)])  25.1 us
    pallas_call x1, Pallas kernels, fast_device(): call(mlp_front, [shaped(many, units), shaped(units, many), shaped(many, u...  23.7 us
    unnamed x144, local copies, waits for them, and re-layouts  19.9 us
  transfers between devices with their start and end apart: 106, of which 34 were waited for; matrix products, arithmetic and copies ran while one was open for 11% of the time, Pallas kernels for 32%

profile of v2, /device:TPU:0, one launch (start us, length us, event | category | flops | bytes accessed | tf_op | source)
XLA Modules:
  0.0 551.4 jit_solution(5247173204668111076)
XLA Ops:
  17.4 5.4 collective-permute-done.16
  65.8 6.9 %collective-permute-done.36 = bf16[48,1536]{1,0:T(8,128)(2,1)S(1)} collective-permute-done((bf16[48,1536]{1,0:T(8,128)(2,1)S(1)}, bf16[48,1536]{1,0:T(8,128)(2,1)S(1)}, u32[]{:S(2)}, u32[]{:S(2)}) %collective-permute-start.36) | collective-permute-done | bytes 147488 | tf_op jit(solution)/shard_map/ppermute | solution.py:332
  73.0 21.2 %collective-permute-done.35 = bf16[48,1536]{1,0:T(8,128)(2,1)S(1)} collective-permute-done((bf16[48,1536]{1,0:T(8,128)(2,1)S(1)}, bf16[48,1536]{1,0:T(8,128)(2,1)S(1)}, u32[]{:S(2)}, u32[]{:S(2)}) %collective-permute-start.35) | collective-permute-done | bytes 147488 | tf_op jit(solution)/shard_map/ppermute | solution.py:332
  121.8 12.9 %collective-permute-done.27.refs_1_ = bf16[256,512]{1,0:T(8,128)(2,1)S(1)} collective-permute-done((bf16[256,512]{1,0:T(8,128)(2,1)S(1)}, bf16[256,512]{1,0:T(8,128)(2,1)S(1)}, u32[]{:S(2)}, u32[]{:S(2)}) %collective-permute-start.27) | collective-permute-done | bytes 262176 | tf_op jit(solution)/shard_map/ppermute | solution.py:297
  140.3 6.7 %project_q.1.q = bf16[256,1536]{1,0:T(8,128)(2,1)} custom-call(s32[32]{0:T(128)} %mul.67.starts.starts_a, s32[32]{0:T(128)} %mul.69.starts_b, bf16[256,1536]{1,0:T(8,128)(2,1)} %get-tuple-element.77.h_one, f32[8,1536]{1,0:T(8,128)} %get-tuple-element.78.vec, f32[256,128]{1,0:T(8,128)} %get-tuple-element.231.cosine, f32[256,128]{1,0:T(8,128)} %get-tuple-element.232.sine, ...), custom_call_target="tpu_custom_call" | custom-call | flops 120795952 | bytes 700000 | tf_op jit(solution)/shard_map/project_q/pallas_call | solution.py:929
  151.1 11.6 %attend.1 = (bf16[256,1536]{1,0:T(8,128)(2,1)}, f32[4,1,768]{2,1,0:T(1,128)}, f32[256,1536]{1,0:T(8,128)}, bf16[256,1536]{1,0:T(8,128)(2,1)}) custom-call(s32[32]{0:T(128)} %mul.67.starts.starts_a, s32[32]{0:T(128)} %mul.69.starts_b, bf16[256,1536]{1,0:T(8,128)(2,1)} %project_q.1.q, bf16[256,1536]{1,0:T(8,128)(2,1)} %bitcast.63, ...), custom_call_target="tpu_custom_call" | custom-call | flops 281857216 | bytes 1000000 | tf_op jit(solution)/shard_map/attend/pallas_call | solution.py:939
  167.3 7.5 %collective-permute-done.49 = bf16[128,1536]{1,0:T(8,128)(2,1)S(1)} collective-permute-done((bf16[128,1536]{1,0:T(8,128)(2,1)S(1)}, bf16[128,1536]{1,0:T(8,128)(2,1)S(1)}, u32[]{:S(2)}, u32[]{:S(2)}) %collective-permute-start.49) | collective-permute-done | bytes 393248 | tf_op jit(solution)/shard_map/ppermute | solution.py:297
  178.8 16.2 %collective-permute-done.55 = bf16[256,1536]{1,0:T(8,128)(2,1)S(1)} collective-permute-done((bf16[256,1536]{1,0:T(8,128)(2,1)S(1)}, bf16[256,1536]{1,0:T(8,128)(2,1)S(1)}, u32[]{:S(2)}, u32[]{:S(2)}) %collective-permute-start.55) | collective-permute-done | bytes 786464 | tf_op jit(solution)/shard_map/ppermute | solution.py:297
  201.8 13.1 %collective-permute-done.46.refs_1_ = bf16[256,1536]{1,0:T(8,128)(2,1)S(1)} collective-permute-done((bf16[256,1536]{1,0:T(8,128)(2,1)S(1)}, bf16[256,1536]{1,0:T(8,128)(2,1)S(1)}, u32[]{:S(2)}, u32[]{:S(2)}) %collective-permute-start.46) | collective-permute-done | bytes 786464 | tf_op jit(solution)/shard_map/ppermute | solution.py:297
  220.9 23.7 %mlp_front.1 = (bf16[2048,1120]{1,0:T(8,128)(2,1)}, bf16[1120,2048]{1,0:T(8,128)(2,1)}, bf16[2048,1120]{1,0:T(8,128)(2,1)}, bf16[2048,1120]{1,0:T(8,128)(2,1)}, bf16[2048,1536]{1,0:T(8,128)(2,1)}) custom-call(bf16[256,1536]{1,0:T(8,128)(2,1)} %copy-done.7, bf16[256,1536]{1,0:T(8,128)(2,1)} %copy-done.40, bf16[256,1536]{1,0:T(8,128)(2,1)} %copy-done.42, ...), custom_call_target="tpu_custom_call" | custom-call | flops 1409286144 | bytes 4000000 | tf_op jit(solution)/shard_map/mlp_front/pallas_call | solution.py:968
  244.6 12.0 %weight_grad.3 = bf16[4,1120,384]{2,1,0:T(8,128)(2,1)} custom-call(bf16[1120,2048]{1,0:T(8,128)(2,1)} %get-tuple-element.92.left, bf16[2048,1536]{1,0:T(8,128)(2,1)} %constant_dynamic-update-slice_fusion.27.right.grad), custom_call_target="tpu_custom_call" | custom-call | flops 704643072 | bytes 1400000 | tf_op jit(solution)/shard_map/weight_grad/pallas_call | solution.py:989
  256.8 35.2 %mlp_back.1 = (bf16[1120,2048]{1,0:T(8,128)(2,1)}, bf16[1120,2048]{1,0:T(8,128)(2,1)}, bf16[1024,1536]{1,0:T(8,128)(2,1)}, bf16[1024,1536]{1,0:T(8,128)(2,1)}) custom-call(bf16[2048,1536]{1,0:T(8,128)(2,1)} %constant_dynamic-update-slice_fusion.27.right.grad, bf16[2048,1120]{1,0:T(8,128)(2,1)} %get-tuple-element.94.gate_in, ...), custom_call_target="tpu_custom_call" | custom-call | flops 2113929216 | bytes 6000000 | tf_op jit(solution)/shard_map/mlp_back/pallas_call | solution.py:1012
  292.0 12.1 %weight_grad.4 = bf16[4,1120,384]{2,1,0:T(8,128)(2,1)} custom-call(bf16[1120,2048]{1,0:T(8,128)(2,1)} %get-tuple-element.97.left, bf16[2048,1536]{1,0:T(8,128)(2,1)} %get-tuple-element.98.right), custom_call_target="tpu_custom_call" | custom-call | flops 704643072 | bytes 1400000 | tf_op jit(solution)/shard_map/weight_grad/pallas_call | solution.py:989
  306.5 12.0 %weight_grad.5 = bf16[4,1120,384]{2,1,0:T(8,128)(2,1)} custom-call(bf16[1120,2048]{1,0:T(8,128)(2,1)} %get-tuple-element.100.left, bf16[2048,1536]{1,0:T(8,128)(2,1)} %get-tuple-element.98.right), custom_call_target="tpu_custom_call" | custom-call | flops 704643072 | bytes 1400000 | tf_op jit(solution)/shard_map/weight_grad/pallas_call | solution.py:989
  323.9 19.1 %collective-permute-done.63 = bf16[256,1536]{1,0:T(8,128)(2,1)} collective-permute-done((bf16[256,1536]{1,0:T(8,128)(2,1)}, bf16[256,1536]{1,0:T(8,128)(2,1)}, u32[]{:S(2)}, u32[]{:S(2)}) %collective-permute-start.63) | collective-permute-done | bytes 786464 | tf_op jit(solution)/shard_map/ppermute | solution.py:297
  347.1 17.6 %collective-permute-done.62 = bf16[256,1536]{1,0:T(8,128)(2,1)S(1)} collective-permute-done((bf16[256,1536]{1,0:T(8,128)(2,1)S(1)}, bf16[256,1536]{1,0:T(8,128)(2,1)S(1)}, u32[]{:S(2)}, u32[]{:S(2)}) %collective-permute-start.62) | collective-permute-done | bytes 786464 | tf_op jit(solution)/shard_map/ppermute | solution.py:297
  366.3 13.9 %mlp_down.1 = (bf16[1024,1536]{1,0:T(8,128)(2,1)}, bf16[1024,1536]{1,0:T(8,128)(2,1)}) custom-call(bf16[2048,1120]{1,0:T(8,128)(2,1)} %get-tuple-element.103.hid, bf16[1120,1536]{1,0:T(8,128)(2,1)} %all-gather.8.cloned.1.call-done.wd), custom_call_target="tpu_custom_call" | custom-call | flops 704643072 | bytes 2000000 | tf_op jit(solution)/shard_map/mlp_down/pallas_call | solution.py:1052
  381.2 12.4 %branch_back.1 = (f32[256,1536]{1,0:T(8,128)}, bf16[256,1536]{1,0:T(8,128)(2,1)}, f32[1,1536]{1,0:T(1,128)}, bf16[768,768]{1,0:T(8,128)(2,1)}, bf16[768,768]{1,0...) custom-call(s32[32]{0:T(128)} %mul.67.starts.starts_a, s32[32]{0:T(128)} %mul.69.starts_b, ...), custom_call_target="tpu_custom_call" | custom-call | flops 241591904 | bytes 1500000 | tf_op jit(solution)/shard_map/branch_back/pallas_call | solution.py:1073
  393.6 13.8 %attend_back.1 = (bf16[256,1536]{1,0:T(8,128)(2,1)}, bf16[2,512,512]{2,1,0:T(8,128)(2,1)}, bf16[2,512,512]{2,1,0:T(8,128)(2,1)}) custom-call(bf16[256,1536]{1,0:T(8,128)(2,1)} %project_q.1.q, bf16[256,1536]{1,0:T(8,128)(2,1)} %get-tuple-element.110.d_att, f32[256,128]{1,0:T(8,128)} %get-tuple-element.231.cosine, f32[256,128]{1,0:T(8,128)} %get-tuple-element.232.sine, ...), custom_call_target="tpu_custom_call" | custom-call | flops 402653184 | bytes 1000000 | tf_op jit(solution)/shard_map/attend_back/pallas_call | solution.py:1088
  413.6 10.3 %query_back.1 = (f32[256,1536]{1,0:T(8,128)}, f32[1,1536]{1,0:T(1,128)}, bf16[768,768]{1,0:T(8,128)(2,1)}, bf16[768,768]{1,0:T(8,128)(2,1)}, bf16[768,768]{1,0:T(8,128)(2,1)}, /*index=5*/bf16[768,768]{1,0:T(8,128)(2,1)}) custom-call(s32[32]{0:T(128)} %mul.67.starts.starts_a, s32[32]{0:T(128)} %mul.69.starts_b, bf16[256,1536]{1,0:T(8,128)(2,1)} %get-tuple-element.114.dq, ...), custom_call_target="tpu_custom_call" | custom-call | flops 241591904 | bytes 1200000 | tf_op jit(solution)/shard_map/query_back/pallas_call | solution.py:1105
  425.7 7.1 %collective-permute-done.67 = bf16[256,512]{1,0:T(8,128)(2,1)S(1)} collective-permute-done((bf16[256,512]{1,0:T(8,128)(2,1)S(1)}, bf16[256,512]{1,0:T(8,128)(2,1)S(1)}, u32[]{:S(2)}, u32[]{:S(2)}) %collective-permute-start.67) | collective-permute-done | bytes 262176 | tf_op jit(solution)/shard_map/ppermute | solution.py:297
  444.7 9.3 %kv_back.1 = (bf16[256,1536]{1,0:T(8,128)(2,1)}, bf16[1024,512]{1,0:T(8,128)(2,1)}, bf16[1024,512]{1,0:T(8,128)(2,1)}) custom-call(s32[32]{0:T(128)} %mul.67.starts.starts_a, bf16[128,512]{1,0:T(8,128)(2,1)} %get-tuple-element.174.keep_a, bf16[128,512]{1,0:T(8,128)(2,1)} %copy-done.48, bf16[128,512]{1,0:T(8,128)(2,1)} %get-tuple-element.172.keep_b, ...), custom_call_target="tpu_custom_call" | custom-call | flops 80530640 | bytes 1000000 | tf_op jit(solution)/shard_map/kv_back/pallas_call | solution.py:1122
  484.1 7.7 %collective-permute-done.97 = bf16[48,1536]{1,0:T(8,128)(2,1)S(1)} collective-permute-done((bf16[48,1536]{1,0:T(8,128)(2,1)S(1)}, bf16[48,1536]{1,0:T(8,128)(2,1)S(1)}, u32[]{:S(2)}, u32[]{:S(2)}) %collective-permute-start.97) | collective-permute-done | bytes 147488 | tf_op jit(solution)/shard_map/ppermute | solution.py:332
  518.6 16.6 %collective-permute-done.73 = bf16[256,1536]{1,0:T(8,128)(2,1)S(1)} collective-permute-done((bf16[256,1536]{1,0:T(8,128)(2,1)S(1)}, bf16[256,1536]{1,0:T(8,128)(2,1)S(1)}, u32[]{:S(2)}, u32[]{:S(2)}) %collective-permute-start.73) | collective-permute-done | bytes 786464 | tf_op jit(solution)/shard_map/ppermute | solution.py:297
  (459 shorter events, 211.3 us)
Async XLA Ops:
  7.2 213.2 %all-gather.6.cloned.1.call-start = ((), (), s32[]{:S(2)}) async-start(), calls=%async_computation.4 | async-start | bytes 4300800 | tf_op jit(solution)/shard_map/all_gather | solution.py:886
  23.0 197.4 %all-gather.4.cloned.1.call-start = ((), (), s32[]{:S(2)}) async-start(), calls=%async_computation.3 | async-start | bytes 4300800 | tf_op jit(solution)/shard_map/all_gather | solution.py:885
  30.4 226.3 %all-gather.8.cloned.1.call-start = ((), (), s32[]{:S(2)}) async-start(), calls=%async_computation.5 | async-start | bytes 4300800 | tf_op jit(solution)/shard_map/all_gather | solution.py:887
  58.4 36.1 %collective-permute-start.12 = (bf16[512,512]{1,0:T(8,128)(2,1)S(1)}, bf16[512,512]{1,0:T(8,128)(2,1)S(1)}, u32[]{:S(2)}, u32[]{:S(2)}) collective-permute-start(bf16[512,512]{1,0:T(8,128)(2,1)S(1)} %constant_dynamic-update-slice_fusion.6.refs_0_), channel_id=1, source_target_pairs={{0,4},{1,5},{2,6},{3,7},{4,0},{5,1},{6,2},{7,3},{8,12},{9,13},{10,... | collective-permute-start | bytes 1572872 | tf_op jit(solution)/shard_map/ppermute | solution.py:297
  60.8 33.5 %collective-permute-start.35 = (bf16[48,1536]{1,0:T(8,128)(2,1)S(1)}, bf16[48,1536]{1,0:T(8,128)(2,1)S(1)}, u32[]{:S(2)}, u32[]{:S(2)}) collective-permute-start(bf16[48,1536]{1,0:T(8,128)(2,1)S(1)} %copy-done.47), channel_id=1, source_target_pairs={{0,16},{8,24},{16,0},{24,8},{1,17},{9,25},{17,1},{25,9},{2,18},{10... | collective-permute-start | bytes 442376 | tf_op jit(solution)/shard_map/ppermute | solution.py:332
  63.4 31.4 %collective-permute-start.34 = (bf16[48,1536]{1,0:T(8,128)(2,1)S(1)}, bf16[48,1536]{1,0:T(8,128)(2,1)S(1)}, u32[]{:S(2)}, u32[]{:S(2)}) collective-permute-start(bf16[48,1536]{1,0:T(8,128)(2,1)S(1)} %copy-done.47), channel_id=1, source_target_pairs={{0,8},{8,16},{16,24},{24,0},{1,9},{9,17},{17,25},{25,1},{2,10},{10... | collective-permute-start | bytes 442376 | tf_op jit(solution)/shard_map/ppermute | solution.py:332
  65.4 30.3 %collective-permute-start.23 = (bf16[384,768]{1,0:T(8,128)(2,1)S(1)}, bf16[384,768]{1,0:T(8,128)(2,1)S(1)}, u32[]{:S(2)}, u32[]{:S(2)}) collective-permute-start(bf16[384,768]{1,0:T(8,128)(2,1)S(1)} %constant_dynamic-update-slice_fusion.18.refs_4_), channel_id=1, source_target_pairs={{0,2},{1,3},{2,0},{3,1},{4,6},{5,7},{6,4},{7,5},{8,10},{9,11},{10,... | collective-permute-start | bytes 1769480 | tf_op jit(solution)/shard_map/ppermute | solution.py:297
  72.7 23.4 %collective-permute-start.19 = (bf16[384,768]{1,0:T(8,128)(2,1)S(1)}, bf16[384,768]{1,0:T(8,128)(2,1)S(1)}, u32[]{:S(2)}, u32[]{:S(2)}) collective-permute-start(bf16[384,768]{1,0:T(8,128)(2,1)S(1)} %constant_dynamic-update-slice_fusion.13.refs_0_), channel_id=1, source_target_pairs={{0,4},{1,5},{2,6},{3,7},{4,0},{5,1},{6,2},{7,3},{8,12},{9,13},{10,... | collective-permute-start | bytes 1769480 | tf_op jit(solution)/shard_map/ppermute | solution.py:297
  113.4 21.9 %collective-permute-start.42 = (bf16[384,768]{1,0:T(8,128)(2,1)S(1)}, bf16[384,768]{1,0:T(8,128)(2,1)S(1)}, u32[]{:S(2)}, u32[]{:S(2)}) collective-permute-start(bf16[384,768]{1,0:T(8,128)(2,1)S(1)} %constant_dynamic-update-slice_fusion.25.refs_12_.refs_4_), channel_id=1, source_target_pairs={{0,2},{1,3},{2,0},{3,1},{4,6},{5,7},{6,4},{7,5},{8,10},{9,11},{10,... | collective-permute-start | bytes 1769480 | tf_op jit(solution)/shard_map/ppermute | solution.py:297
  114.6 21.2 %collective-permute-start.38 = (bf16[384,768]{1,0:T(8,128)(2,1)S(1)}, bf16[384,768]{1,0:T(8,128)(2,1)S(1)}, u32[]{:S(2)}, u32[]{:S(2)}) collective-permute-start(bf16[384,768]{1,0:T(8,128)(2,1)S(1)} %constant_dynamic-update-slice_fusion.23.refs_8_.refs_0_), channel_id=1, source_target_pairs={{0,4},{1,5},{2,6},{3,7},{4,0},{5,1},{6,2},{7,3},{8,12},{9,13},{10,... | collective-permute-start | bytes 1769480 | tf_op jit(solution)/shard_map/ppermute | solution.py:297
  120.7 333.4 %reduce-scatter.8.cloned.1.call-start = ((), (), s32[]{:S(2)}) async-start(), calls=%async_computation.8 | async-start | bytes 4300800 | tf_op jit(solution)/shard_map/reduce_scatter | solution.py:1006
  177.8 22.4 %collective-permute-start.58 = (bf16[256,1536]{1,0:T(8,128)(2,1)S(1)}, bf16[256,1536]{1,0:T(8,128)(2,1)S(1)}, u32[]{:S(2)}, u32[]{:S(2)}) collective-permute-start(bf16[256,1536]{1,0:T(8,128)(2,1)S(1)} %pad_maximum_fusion.3), channel_id=1, source_target_pairs={{0,2},{1,3},{2,0},{3,1},{4,6},{5,7},{6,4},{7,5},{8,10},{9,11},{10,... | collective-permute-start | bytes 2359304 | tf_op jit(solution)/shard_map/ppermute | solution.py:297
  256.7 199.8 %reduce-scatter.6.cloned.1.call-start = ((), (), s32[]{:S(2)}) async-start(), calls=%async_computation.7 | async-start | bytes 4300800 | tf_op jit(solution)/shard_map/reduce_scatter | solution.py:1006
  304.1 154.9 %reduce-scatter.4.cloned.1.call-start = ((), (), s32[]{:S(2)}) async-start(), calls=%async_computation.6 | async-start | bytes 4300800 | tf_op jit(solution)/shard_map/reduce_scatter | solution.py:1006
  344.2 20.5 %collective-permute-start.62 = (bf16[256,1536]{1,0:T(8,128)(2,1)S(1)}, bf16[256,1536]{1,0:T(8,128)(2,1)S(1)}, u32[]{:S(2)}, u32[]{:S(2)}) collective-permute-start(bf16[256,1536]{1,0:T(8,128)(2,1)S(1)} %get-tuple-element.139), channel_id=1, source_target_pairs={{0,4},{1,5},{2,6},{3,7},{4,0},{5,1},{6,2},{7,3},{8,12},{9,13},{10,... | collective-permute-start | bytes 2359304 | tf_op jit(solution)/shard_map/ppermute | solution.py:297
  345.9 34.3 %collective-permute-start.65 = (bf16[128,1536]{1,0:T(8,128)(2,1)S(1)}, bf16[128,1536]{1,0:T(8,128)(2,1)S(1)}, u32[]{:S(2)}, u32[]{:S(2)}) collective-permute-start(bf16[128,1536]{1,0:T(8,128)(2,1)S(1)} %get-tuple-element.146), channel_id=1, source_target_pairs={{0,4},{1,5},{2,6},{3,7},{4,0},{5,1},{6,2},{7,3},{8,12},{9,13},{10,... | collective-permute-start | bytes 1179656 | tf_op jit(solution)/shard_map/ppermute | solution.py:297
  413.1 21.0 %collective-permute-start.91 = (bf16[768,768]{1,0:T(8,128)(2,1)}, bf16[768,768]{1,0:T(8,128)(2,1)S(1)}, u32[]{:S(2)}, u32[]{:S(2)}) collective-permute-start(bf16[768,768]{1,0:T(8,128)(2,1)} %get-tuple-element.130), channel_id=1, source_target_pairs={{0,1},{1,0},{2,3},{3,2},{4,5},{5,4},{6,7},{7,6},{8,9},{9,8},{10,11... | collective-permute-start | bytes 3538952 | tf_op jit(solution)/shard_map/ppermute | solution.py:297
  413.1 22.2 %collective-permute-start.92 = (bf16[768,768]{1,0:T(8,128)(2,1)}, bf16[768,768]{1,0:T(8,128)(2,1)S(1)}, u32[]{:S(2)}, u32[]{:S(2)}) collective-permute-start(bf16[768,768]{1,0:T(8,128)(2,1)} %get-tuple-element.133), channel_id=1, source_target_pairs={{0,1},{1,0},{2,3},{3,2},{4,5},{5,4},{6,7},{7,6},{8,9},{9,8},{10,11... | collective-permute-start | bytes 3538952 | tf_op jit(solution)/shard_map/ppermute | solution.py:297
  435.2 61.5 %collective-permute-start.71 = (bf16[1024,1536]{1,0:T(8,128)(2,1)}, bf16[1024,1536]{1,0:T(8,128)(2,1)}, u32[]{:S(2)}, u32[]{:S(2)}) collective-permute-start(bf16[1024,1536]{1,0:T(8,128)(2,1)} %get-tuple-element.121), channel_id=1, source_target_pairs={{0,1},{1,0},{2,3},{3,2},{4,5},{5,4},{6,7},{7,6},{8,9},{9,8},{10,11... | collective-permute-start | bytes 9437192 | tf_op jit(solution)/shard_map/ppermute | solution.py:297
  438.2 23.3 %collective-permute-start.94 = (bf16[384,768]{1,0:T(8,128)(2,1)}, bf16[384,768]{1,0:T(8,128)(2,1)}, u32[]{:S(2)}, u32[]{:S(2)}) collective-permute-start(bf16[384,768]{1,0:T(8,128)(2,1)} %slice.410), channel_id=1, source_target_pairs={{0,2},{1,3},{2,0},{3,1},{4,6},{5,7},{6,4},{7,5},{8,10},{9,11},{10,... | collective-permute-start | bytes 1769480 | tf_op jit(solution)/shard_map/ppermute | solution.py:297
  440.7 22.1 %collective-permute-start.93 = (bf16[384,768]{1,0:T(8,128)(2,1)}, bf16[384,768]{1,0:T(8,128)(2,1)}, u32[]{:S(2)}, u32[]{:S(2)}) collective-permute-start(bf16[384,768]{1,0:T(8,128)(2,1)} %slice.407), channel_id=1, source_target_pairs={{0,4},{1,5},{2,6},{3,7},{4,0},{5,1},{6,2},{7,3},{8,12},{9,13},{10,... | collective-permute-start | bytes 1769480 | tf_op jit(solution)/shard_map/ppermute | solution.py:297
  443.4 26.5 %collective-permute-start.83 = (bf16[384,768]{1,0:T(8,128)(2,1)}, bf16[384,768]{1,0:T(8,128)(2,1)}, u32[]{:S(2)}, u32[]{:S(2)}) collective-permute-start(bf16[384,768]{1,0:T(8,128)(2,1)} %slice.470), channel_id=1, source_target_pairs={{0,4},{1,5},{2,6},{3,7},{4,0},{5,1},{6,2},{7,3},{8,12},{9,13},{10,... | collective-permute-start | bytes 1769480 | tf_op jit(solution)/shard_map/ppermute | solution.py:297
  443.9 28.0 %collective-permute-start.85 = (bf16[384,768]{1,0:T(8,128)(2,1)}, bf16[384,768]{1,0:T(8,128)(2,1)}, u32[]{:S(2)}, u32[]{:S(2)}) collective-permute-start(bf16[384,768]{1,0:T(8,128)(2,1)} %slice.473), channel_id=1, source_target_pairs={{0,2},{1,3},{2,0},{3,1},{4,6},{5,7},{6,4},{7,5},{8,10},{9,11},{10,... | collective-permute-start | bytes 1769480 | tf_op jit(solution)/shard_map/ppermute | solution.py:297
  516.3 23.0 %collective-permute-start.74 = (bf16[128,1536]{1,0:T(8,128)(2,1)S(1)}, bf16[128,1536]{1,0:T(8,128)(2,1)S(1)}, u32[]{:S(2)}, u32[]{:S(2)}) collective-permute-start(bf16[128,1536]{1,0:T(8,128)(2,1)S(1)} %get-tuple-element.142), channel_id=1, source_target_pairs={{0,2},{1,3},{2,0},{3,1},{4,6},{5,7},{6,4},{7,5},{8,10},{9,11},{10,... | collective-permute-start | bytes 1179656 | tf_op jit(solution)/shard_map/ppermute | solution.py:297
  (145 other events, 1520.7 us)
Sparse Core Ops, SparseCore 0:
  23.1 83.0 all-gather.5
  107.8 66.7 all-gather.3
  176.2 66.9 all-gather.7
  256.8 62.2 reduce-scatter.7
  321.3 65.0 reduce-scatter.5
  388.6 65.0 reduce-scatter.3

commit v3 on v0

--- a/solution.py
+++ b/solution.py
@@ -1,8 +1,12 @@
+import functools
 import math
 
 import jax
 import jax.numpy as jnp
+import numpy as np
 from jax import lax
+from jax.experimental import pallas as pl
+from jax.experimental.pallas import tpu as pltpu
 from jax.sharding import PartitionSpec as P
 
 Q_HEADS = 12
@@ -59,7 +63,7 @@
     return (d_gate, d_up)
 
 
-def on_device(
+def plain_device(
     layer_in,
     seg_ids,
     pad_mask,
@@ -257,9 +261,1012 @@
     )
 
 
+F32 = jnp.float32
+BF16 = jnp.bfloat16
+ROWS = 2
+PARTS = 8
+WIDE = 4
+SEG = 128
+SHARE = 48
+GROUP = Q_HEADS // KV_HEADS
+SCALE = 1.0 / math.sqrt(HEAD)
+TOKENS = ROWS * SEG
+ROW_LEN = SEG * PARTS
+KV_COLUMNS = 2 * HK + 128
+FIRST = KV_COLUMNS + 512
+TILE = 512
+
+
+def dot_nn(left, right):
+    return lax.dot_general(left, right, (((1,), (0,)), ((), ())), preferred_element_type=F32)
+
+
+def dot_nt(left, right):
+    return lax.dot_general(left, right, (((1,), (1,)), ((), ())), preferred_element_type=F32)
+
+
+def flipped(value):
+    return value.astype(F32).T.astype(BF16)
+
+
+class Links:
+    def __init__(self):
+        self.orders = ((2, 4, 1), (4, 2, 1))
+
+    def hop(self, value, bit):
+        return lax.ppermute(value, "narrow", [(i, i ^ bit) for i in range(PARTS)])
+
+    def offsets(self, which):
+        found = [0]
+        for bit in self.orders[which]:
+            found = found + [o ^ bit for o in found]
+        return found
+
+    def first(self, value, which):
+        return self.hop(value, self.orders[which][0])
+
+    def second(self, value, which):
+        return self.hop(value, self.orders[which][1])
+
+    def core(self, value):
+        return self.hop(value, 1)
+
+    def gather(self, value, which):
+        near = jnp.concatenate([value, self.first(value, which)], axis=0)
+        far = self.second(near, which)
+        return [near, far, self.core(near), self.core(far)]
+
+    def scatter_second(self, held, which):
+        half = held.shape[0] // 2
+        return held[:half], self.second(held[half:], which)
+
+    def scatter_first(self, held, which):
+        half = held.shape[0] // 2
+        return held[:half], self.first(held[half:], which)
+
+    def over_wide(self, value, step):
+        return lax.ppermute(value, "wide", [(i, (i + step) % WIDE) for i in range(WIDE)])
+
+    def direct_gather(self, value):
+        return [value] + [self.over_wide(value, k) for k in range(1, WIDE)]
+
+    def direct_scatter(self, held):
+        slots = held.reshape((WIDE, held.shape[0] // WIDE) + held.shape[1:])
+        total = slots[0].astype(F32)
+        for k in range(1, WIDE):
+            total = total + self.over_wide(slots[k], -k).astype(F32)
+        return total
+
+
+def tie(one, other):
+    return lax.optimization_barrier((one, other))
+
+
+def together(values):
+    return list(lax.optimization_barrier(tuple(values)))
+
+
+def in_vmem(count):
+    return [pl.BlockSpec(memory_space=pltpu.VMEM)] * count
+
+
+def in_smem(count):
+    return [pl.BlockSpec(memory_space=pltpu.SMEM)] * count
+
+
+def in_hbm(count):
+    return [pl.BlockSpec(memory_space=pltpu.HBM)] * count
+
+
+def call(body, outs, scratch, in_specs, out_specs, flops, nbytes, vmem, grid=None, name=None):
+    return pl.pallas_call(
+        body,
+        out_shape=outs,
+        grid=grid if grid is not None else (),
+        in_specs=in_specs,
+        out_specs=out_specs,
+        scratch_shapes=scratch,
+        name=name,
+        compiler_params=pltpu.CompilerParams(vmem_limit_bytes=vmem * 1024 * 1024),
+        cost_estimate=pl.CostEstimate(
+            flops=10 * int(flops), bytes_accessed=10 * int(nbytes), transcendentals=0
+        ),
+    )
+
+
+def shaped(*dims, dtype=BF16):
+    return jax.ShapeDtypeStruct(dims, dtype)
+
+
+def weight_copies(pieces, held, starts, sems, source, target):
+    copies = []
+    for i in range(PARTS * WIDE):
+        copies.append(
+            pltpu.make_async_copy(
+                pieces[i // 8].at[pl.ds((i % 8) * SHARE, SHARE), source],
+                held.at[pl.ds(pl.multiple_of(starts[i], 16), SHARE), target],
+                sems.at[i],
+            )
+        )
+    return copies
+
+
+def grad_copies(held, own, other, starts, sems, columns):
+    copies = []
+    for i in range(PARTS * WIDE):
+        target = own if i < 16 else other
+        copies.append(
+            pltpu.make_async_copy(
+                held.at[pl.ds(pl.multiple_of(starts[i], 16), SHARE), columns],
+                target.at[pl.ds((i % 16) * SHARE, SHARE), :],
+                sems.at[i],
+            )
+        )
+    return copies
+
+
+def half_copies(pieces, held, starts_a, starts_b, sems):
+    half = held.shape[1] // 2
+    every = slice(None)
+    return weight_copies(
+        pieces[:4], held, starts_a, sems.at[0], every, slice(0, half)
+    ) + weight_copies(pieces[4:], held, starts_b, sems.at[1], every, slice(half, 2 * half))
+
+
+def query_copies(pieces, held, starts_a, starts_b, sems):
+    cut = FIRST - KV_COLUMNS
+    return weight_copies(
+        pieces[:4], held, starts_a, sems.at[0], slice(KV_COLUMNS, FIRST), slice(0, cut)
+    ) + weight_copies(pieces[4:], held, starts_b, sems.at[1], slice(None), slice(cut, HQ))
+
+
+def half_grad_copies(held, outs, starts_a, starts_b, sems):
+    half = held.shape[1] // 2
+    return grad_copies(
+        held, outs[0], outs[1], starts_a, sems.at[0], slice(0, half)
+    ) + grad_copies(held, outs[2], outs[3], starts_b, sems.at[1], slice(half, 2 * half))
+
+
+def turn(value, cosine, sine):
+    return value * cosine + pltpu.roll(value, HEAD // 2, 1) * sine
+
+
+def project_kv(starts, x, cosine, sine, pick_k, pick_v, *refs):
+    pieces, (kv_out, h_out, vec_out, whole, held, sems, out_sem) = refs[:4], refs[4:]
+    copies = weight_copies(pieces, held, starts, sems, slice(0, KV_COLUMNS), slice(None))
+    for copy in copies:
+        copy.start()
+    value = x[...].astype(F32)
+    unit = value * lax.rsqrt(jnp.mean(value * value, axis=-1, keepdims=True) + EPS)
+    for copy in copies:
+        copy.wait()
+    over = pltpu.make_async_copy(held, whole, out_sem)
+    over.start()
+    vec = held[:, 2 * HK :].astype(F32).T[:8, :]
+    vec_out[...] = vec
+    low = vec.astype(BF16)
+    b_key = dot_nn(low, pick_k[...])[3:4, :]
+    b_value = dot_nn(low, pick_v[...])[3:4, :]
+    h_one = (unit * vec[0:1, :]).astype(BF16)
+    h_out[...] = h_one
+    lin = dot_nn(h_one, held[:, : 2 * HK])
+    for head in range(KV_HEADS):
+        cut = slice(head * HEAD, (head + 1) * HEAD)
+        key = turn(lin[:, cut] + b_key[:, cut], cosine[...], sine[...])
+        kv_out[:, cut] = key.astype(BF16)
+    kv_out[:, HK:] = (lin[:, HK:] + b_value).astype(BF16)
+    over.wait()
+
+
+def project_q(starts_a, starts_b, h_one, vec, cosine, sine, *refs):
+    pieces, (q_out, whole, held, sems, out_sem) = refs[:8], refs[8:]
+    copies = query_copies(pieces, held, starts_a, starts_b, sems)
+    for copy in copies:
+        copy.start()
+    for copy in copies:
+        copy.wait()
+    over = pltpu.make_async_copy(held, whole, out_sem)
+    over.start()
+    lin = dot_nn(h_one[...], held[...]) + vec[2:3, :]
+    for head in range(Q_HEADS):
+        cut = slice(head * HEAD, (head + 1) * HEAD)
+        q_out[:, cut] = turn(lin[:, cut], cosine[...], sine[...]).astype(BF16)
+    over.wait()
+
+
+def stacked(ref, row, kv_head):
+    first = kv_head * GROUP
+    return jnp.concatenate(
+        [
+            ref[row * SEG : (row + 1) * SEG, (first + g) * HEAD : (first + g + 1) * HEAD]
+            for g in range(GROUP)
+        ],
+        axis=0,
+    )
+
+
+def row_keys(pieces, row, column):
+    return jnp.concatenate(
+        [piece[:, column : column + HEAD] for piece in pieces[4 * row : 4 * row + 4]], axis=0
+    )
+
+
+def attend(q, barred, *refs):
+    kv, (att_out, lse_out) = refs[:8], refs[8:]
+    for row in range(ROWS):
+        bar = barred[row]
+        bar = jnp.concatenate([bar] * GROUP, axis=1)
+        for kv_head in range(KV_HEADS):
+            keys = row_keys(kv, row, kv_head * HEAD)
+            values = row_keys(kv, row, HK + kv_head * HEAD)
+            scores = dot_nt(keys, stacked(q, row, kv_head)) * SCALE + bar
+            top = jnp.max(scores, axis=0, keepdims=True)
+            expo = jnp.exp(scores - top)
+            total = jnp.sum(expo, axis=0, keepdims=True)
+            lse_out[row * KV_HEADS + kv_head] = top + jnp.log(total)
+            probs = (expo / total).astype(BF16)
+            out = dot_nn(flipped(values), probs)
+            for g in range(GROUP):
+                head = kv_head * GROUP + g
+                att_out[row * SEG : (row + 1) * SEG, head * HEAD : (head + 1) * HEAD] = (
+                    out[:, g * SEG : (g + 1) * SEG].T.astype(BF16)
+                )
+
+
+def branch(starts_a, starts_b, att, x, vec, *refs):
+    pieces, (mid_out, h_out, whole, held, sems, out_sem) = refs[:8], refs[8:]
+    copies = half_copies(pieces, held, starts_a, starts_b, sems)
+    for copy in copies:
+        copy.start()
+    for copy in copies:
+        copy.wait()
+    over = pltpu.make_async_copy(held, whole, out_sem)
+    over.start()
+    mid = x[...].astype(F32) + dot_nn(att[...], held[...])
+    mid_out[...] = mid
+    factor = lax.rsqrt(jnp.mean(mid * mid, axis=-1, keepdims=True) + EPS)
+    h_out[...] = (mid * factor * vec[1:2, :]).astype(BF16)
+    over.wait()
+
+
+def swiglu_parts(h, grad, weights):
+    units = weights.shape[0] // 3
+    d_hidden = dot_nt(grad, weights[:units, :])
+    both = dot_nt(h, weights[units:, :])
+    gate, up = both[:, :units], both[:, units:]
+    sigma = jax.nn.sigmoid(gate)
+    active = gate * sigma
+    hidden = (active * up).astype(BF16)
+    d_gate = (d_hidden * up * sigma * (1.0 + gate * (1.0 - sigma))).astype(BF16)
+    d_up = (d_hidden * active).astype(BF16)
+    return hidden, d_gate, d_up
+
+
+def mlp_first(grad, *refs):
+    h_pieces, weights, refs = refs[:8], refs[8], refs[9:]
+    d_t_out, d_h_out, mixed_out, h_all, h_v, w_v, sems, w_sem, out_sems = refs
+    step = pl.program_id(0)
+    rows = h_pieces[0].shape[0]
+    units = w_v.shape[0] // 3
+
+    def pieces_in():
+        return [
+            pltpu.make_async_copy(h_pieces[i], h_v.at[pl.ds(i * rows, rows), :], sems.at[i])
+            for i in range(8)
+        ]
+
+    def weights_in():
+        return pltpu.make_async_copy(weights, w_v, w_sem.at[0])
+
+    def h_over(tile):
+        at = pl.ds(pl.multiple_of(tile * TILE, TILE), TILE)
+        return pltpu.make_async_copy(h_v.at[at, :], h_all.at[at, :], out_sems.at[tile])
+
+    @pl.when(step == 0)
+    def _():
+        held = pieces_in()
+        for copy in held[:2] + [weights_in()] + held[2:]:
+            copy.start()
+
+    for tile in range(4):
+
+        @pl.when(step == tile)
+        def _(tile=tile):
+            for copy in pieces_in()[2 * tile : 2 * tile + 2]:
+                copy.wait()
+            h_over(tile).start()
+
+    @pl.when(step == 0)
+    def _():
+        weights_in().wait()
+
+    h = h_v[pl.ds(pl.multiple_of(step * TILE, TILE), TILE), :]
+    hidden, d_gate, d_up = swiglu_parts(h, grad[...], w_v)
+    d_t_out[:units, :] = hidden.T
+    d_t_out[units : 2 * units, :] = d_gate.T
+    d_t_out[2 * units :, :] = d_up.T
+    d_pair = jnp.concatenate([d_gate, d_up], axis=1)
+    d_h_out[...] = dot_nn(d_pair, w_v[units:, :]).astype(BF16)
+    mixed_out[...] = dot_nn(hidden, w_v[:units, :]).astype(BF16)
+
+    @pl.when(step == 3)
+    def _():
+        for tile in range(4):
+            h_over(tile).wait()
+
+
+def put_halves(value, outs, step):
+    if len(outs) == 1:
+        outs[0][...] = value
+        return
+    half = value.shape[0] // 2
+    outs[0][...] = value[:half, :]
+    for row in range(ROWS):
+
+        @pl.when(step == row)
+        def _(row=row):
+            outs[1 + row][...] = value[half:, :]
+
+
+def mlp_second(grad, h, weights, *refs):
+    count = 3 if len(refs) == 10 else 1
+    added, d_t_out, hid_out = refs[: -5 - count], refs[-5 - count], refs[-4 - count]
+    h_outs, (d_v, w_v, sems) = refs[-3 - count : -3], refs[-3:]
+    step = pl.program_id(0)
+    units = w_v.shape[0] // 3
+
+    def weights_in():
+        return [
+            pltpu.make_async_copy(
+                weights.at[pl.ds(i * units, (1 + i) * units), :],
+                w_v.at[pl.ds(i * units, (1 + i) * units), :],
+                sems.at[i],
+            )
+            for i in range(2)
+        ]
+
+    @pl.when(step == 0)
+    def _():
+        for copy in weights_in():
+            copy.start()
+        for copy in weights_in():
+            copy.wait()
+
+    hidden, d_gate, d_up = swiglu_parts(h[...], grad[...], w_v)
+    hid_out[...] = hidden
+    d_t_out[:units, :] = hidden.T
+    d_t_out[units : 2 * units, :] = d_gate.T
+    d_t_out[2 * units :, :] = d_up.T
+    d_v[:, :units] = d_gate
+    d_v[:, units:] = d_up
+    d_h = dot_nn(d_v[...], w_v[units:, :])
+    for ref in added:
+        d_h = d_h + ref[...].astype(F32)
+    put_halves(d_h.astype(BF16), h_outs, step)
+
+
+def mlp_down(hid, weights, *refs):
+    count = 3 if len(refs) == 5 else 1
+    added, outs = refs[:-count], refs[-count:]
+    mixed = dot_nn(hid[...], weights[...])
+    for ref in added:
+        mixed = mixed + ref[...].astype(F32)
+    put_halves(mixed.astype(BF16), outs, pl.program_id(0))
+
+
+def weight_grad(left_own, left_other, right_grad, right_h, out):
+    half = left_own.shape[1]
+    cut = out.shape[2]
+
+    def put(right):
+        found = dot_nn(left_own[...], right[:half, :]) + dot_nn(left_other[...], right[half:, :])
+        found = found.astype(BF16)
+        out[0] = found[:, :cut]
+        out[1] = found[:, cut:]
+
+    @pl.when(pl.program_id(1) == 0)
+    def _():
+        put(right_grad)
+
+    @pl.when(pl.program_id(1) > 0)
+    def _():
+        put(right_h)
+
+
+def branch_back(starts_a, starts_b, keep_a, got_a, keep_b, got_b, mid, grad, vec, att, weight, *refs):
+    (d_mid_out, d_att_out, d_gain_out), outs = refs[:3], refs[3:7]
+    held, held_d, sem, out_sems = refs[7:]
+    copy = pltpu.make_async_copy(weight, held, sem)
+    copy.start()
+    d_h = jnp.concatenate(
+        [
+            keep_a[...].astype(F32) + got_a[...].astype(F32),
+            keep_b[...].astype(F32) + got_b[...].astype(F32),
+        ],
+        axis=0,
+    )
+    x_mid = mid[...]
+    factor = lax.rsqrt(jnp.mean(x_mid * x_mid, axis=-1, keepdims=True) + EPS)
+    unit = x_mid * factor
+    d_gain_out[...] = jnp.sum(d_h * unit, axis=0, keepdims=True)
+    d_mid = grad[...].astype(F32) + norm_back(d_h, unit, factor, vec[1:2, :])
+    d_mid_out[...] = d_mid
+    d_branch = d_mid.astype(BF16)
+    held_d[...] = dot_nn(flipped(att[...]), d_branch).astype(BF16)
+    out_copies = half_grad_copies(held_d, outs, starts_a, starts_b, out_sems)
+    for out_copy in out_copies:
+        out_copy.start()
+    copy.wait()
+    d_att_out[...] = dot_nt(d_branch, held[...]).astype(BF16)
+    for out_copy in out_copies:
+        out_copy.wait()
+
+
+def attend_back(row, q, d_att, cosine, sine, barred, lse, *refs):
+    kv, (dq_out, own, other) = refs[:4], refs[4:]
+    bar = jnp.concatenate([barred[row]] * GROUP, axis=1)
+    at = slice(row * SEG, (row + 1) * SEG)
+    for kv_head in range(KV_HEADS):
+        keys = row_keys(kv, 0, kv_head * HEAD)
+        values = row_keys(kv, 0, HK + kv_head * HEAD)
+        queries = stacked(q, row, kv_head)
+        d_out = stacked(d_att, row, kv_head)
+        scores = dot_nt(keys, queries) * SCALE + bar
+        probs = jnp.exp(scores - lse[row * KV_HEADS + kv_head])
+        d_prob = dot_nt(values, d_out)
+        delta = jnp.sum(probs * d_prob, axis=0, keepdims=True)
+        d_score = (SCALE * probs * (d_prob - delta)).astype(BF16)
+        d_value = dot_nn(probs.astype(BF16), d_out).astype(BF16)
+        d_key = dot_nn(d_score, queries).astype(BF16)
+        half = ROW_LEN // 2
+        cut = slice(kv_head * HEAD, (kv_head + 1) * HEAD)
+        cut_v = slice(HK + kv_head * HEAD, HK + (kv_head + 1) * HEAD)
+        own[:, cut] = d_key[:half]
+        other[:, cut] = d_key[half:]
+        own[:, cut_v] = d_value[:half]
+        other[:, cut_v] = d_value[half:]
+        d_query = dot_nn(flipped(keys), d_score)
+        for g in range(GROUP):
+            head = kv_head * GROUP + g
+            back = turn(d_query[:, g * SEG : (g + 1) * SEG].T, cosine[at, :], -sine[at, :])
+            dq_out[:, head * HEAD : (head + 1) * HEAD] = back.astype(BF16)
+
+
+def query_back(starts_a, starts_b, dq_a, dq_b, h_one, weight, *refs):
+    (d_h_out, d_bias_out), outs = refs[:2], refs[2:6]
+    held, held_d, sem, out_sems = refs[6:]
+    copy = pltpu.make_async_copy(weight, held, sem)
+    copy.start()
+    dq = jnp.concatenate([dq_a[...], dq_b[...]], axis=0)
+    held_d[...] = dot_nn(flipped(h_one[...]), dq).astype(BF16)
+    out_copies = half_grad_copies(held_d, outs, starts_a, starts_b, out_sems)
+    for out_copy in out_copies:
+        out_copy.start()
+    d_bias_out[...] = jnp.sum(dq.astype(F32), axis=0, keepdims=True)
+    copy.wait()
+    d_h_out[...] = dot_nt(dq, held[...])
+    for out_copy in out_copies:
+        out_copy.wait()
+
+
+def kv_back(
+    starts, keep_a, got_a, keep_b, got_b, x, h_one, vec, cosine, sine, d_h_q, d_mid, d_gain, d_bias,
+    pick_k, pick_v, weight, *refs,
+):
+    grad_out, own, other, held_d, out_sems = refs
+    d_kv = jnp.concatenate(
+        [
+            keep_a[...].astype(F32) + got_a[...].astype(F32),
+            keep_b[...].astype(F32) + got_b[...].astype(F32),
+        ],
+        axis=0,
+    )
+    parts = [
+        turn(d_kv[:, head * HEAD : (head + 1) * HEAD], cosine[...], -sine[...])
+        for head in range(KV_HEADS)
+    ]
+    d_lin = jnp.concatenate(parts + [d_kv[:, HK:]], axis=1).astype(BF16)
+    held_d[:, : 2 * HK] = dot_nn(flipped(h_one[...]), d_lin).astype(BF16)
+    d_small = jnp.sum(d_lin.astype(F32), axis=0, keepdims=True).astype(BF16)
+    value = x[...].astype(F32)
+    factor = lax.rsqrt(jnp.mean(value * value, axis=-1, keepdims=True) + EPS)
+    unit = value * factor
+    d_h = d_h_q[...] + dot_nt(d_lin, weight[:, : 2 * HK])
+    packed = jnp.concatenate(
+        [
+            jnp.sum(d_h * unit, axis=0, keepdims=True),
+            d_gain[...],
+            d_bias[...],
+            dot_nt(d_small[:, :HK], pick_k[...]) + dot_nt(d_small[:, HK:], pick_v[...]),
+            jnp.zeros((124, HQ), F32),
+        ],
+        axis=0,
+    )
+    held_d[:, 2 * HK :] = packed.T.astype(BF16)
+    out_copies = grad_copies(held_d, own, other, starts, out_sems, slice(None))
+    for copy in out_copies:
+        copy.start()
+    grad_out[...] = (d_mid[...] + norm_back(d_h, unit, factor, vec[0:1, :])).astype(BF16)
+    for copy in out_copies:
+        copy.wait()
+
+
+def fast_device(
+    layer_in,
+    seg_ids,
+    pad_mask,
+    gain_attn,
+    w_query,
+    b_query,
+    w_key,
+    b_key,
+    w_value,
+    b_value,
+    w_out,
+    gain_mlp,
+    w_gate,
+    w_up,
+    w_down,
+    grad_out,
+):
+    width = layer_in.shape[2]
+    units = w_gate.shape[1]
+    split = units * 4 // 7
+    links = Links()
+    here = lax.axis_index("wide")
+    me = lax.axis_index("narrow")
+    dma = pltpu.SemaphoreType.DMA
+    order = [0, 1]
+    x = layer_in.reshape(TOKENS, width)
+    grad = grad_out.reshape(TOKENS, width)
+
+    slots = jnp.arange(WIDE, dtype=jnp.int32)
+    partners = [me ^ jnp.array(links.offsets(o), jnp.int32) for o in order]
+    starts = [
+        (p[:, None] + (slots * PARTS)[None, :]).reshape(-1) * SHARE for p in partners
+    ]
+    ends = [
+        (p[:, None] + ((here - slots) % WIDE * PARTS)[None, :]).reshape(-1) * SHARE for p in partners
+    ]
+    cut = width // WIDE
+    lanes = np.arange(HQ)
+    small = b_key.shape[0]
+    in_block = lanes % SHARE
+    head_lane = lanes // SHARE * small + in_block
+    pick_k = (in_block < small)[:, None] & (head_lane[:, None] == np.arange(HK))
+    pick_v = ((in_block >= small) & (in_block < 2 * small))[:, None] & (
+        (head_lane - small)[:, None] == np.arange(HK)
+    )
+    pick_k, pick_v = jnp.asarray(pick_k, BF16), jnp.asarray(pick_v, BF16)
+
+    half = HQ // 2
+    rows = range(ROWS)
+    both = range(2)
+    at_row = [slice(r * SEG, (r + 1) * SEG) for r in rows]
+
+    vectors = jnp.stack(
+        [gain_attn, gain_mlp, b_query, jnp.pad(jnp.concatenate([b_key, b_value]), (0, SHARE - 2 * small))],
+        axis=1,
+    )
+    vectors = jnp.pad(vectors, ((0, 0), (0, 124)))
+    own = jnp.concatenate([w_key, w_value, vectors, w_query, w_out], axis=1)
+    w_rows = lax.all_gather(own, "wide", axis=0, tiled=True)
+    parts = [(0, split), (split, units)]
+    own_parts = [
+        jnp.concatenate([w_down[p:q], w_gate.T[p:q], w_up.T[p:q]], axis=0) for p, q in parts
+    ]
+
+    grad_own = [grad[at_row[r]] for r in rows]
+    grad_one = [links.first(grad_own[r], order[r]) for r in rows]
+    grad_one = together(grad_one)
+    marks = jnp.stack([seg_ids, pad_mask])[None]
+    marks = jnp.concatenate([marks, links.first(marks, 0)], axis=0)
+    marks = jnp.concatenate([marks, links.second(marks, 0)], axis=0)
+    marks = jnp.concatenate([marks, links.core(marks)], axis=0)
+    grad_near = [jnp.concatenate([grad_own[r], grad_one[r]], axis=0) for r in rows]
+    grad_far = [links.second(grad_near[r], order[r]) for r in rows]
+
+    at = {o: i for i, o in enumerate(links.offsets(0))}
+    marks = [jnp.stack([marks[at[o], :, r] for o in links.offsets(order[r])]) for r in rows]
+    ids_all = jnp.stack([m[:, 0].reshape(ROW_LEN) for m in marks])
+    pads_all = jnp.stack([m[:, 1].reshape(ROW_LEN) for m in marks])
+    sources = jnp.array([links.offsets(o) for o in order], jnp.int32) ^ me
+    key_idx = (
+        sources[:, :, None] * SEG + jnp.arange(SEG, dtype=jnp.int32)[None, None, :]
+    ).reshape(ROWS, ROW_LEN)
+    own_idx = me * SEG + jnp.arange(SEG, dtype=jnp.int32)
+    begins = jnp.sum((ids_all[:, None, :] < seg_ids[:, :, None]).astype(jnp.int32), axis=-1)
+    cosine, sine = angles((own_idx[None, :] - begins).reshape(TOKENS), HEAD)
+    cosine = jnp.concatenate([cosine, cosine], axis=-1)
+    sine = jnp.concatenate([-sine, sine], axis=-1)
+    allowed = (ids_all[:, :, None] == seg_ids[:, None, :]) & (
+        key_idx[:, :, None] < own_idx[None, None, :]
+    ) & (pads_all[:, :, None] == 1) | (key_idx[:, :, None] == own_idx[None, None, :])
+    barred = jnp.where(allowed, 0.0, -1e30).astype(F32)
+
+    w_rows, (cosine, sine, barred, grad_far) = tie(w_rows, (cosine, sine, barred, grad_far))
+    w_rows, own_parts[0] = tie(w_rows, own_parts[0])
+    weights = [lax.all_gather(own_parts[0], "wide", axis=1, tiled=True)]
+    bounds = (0, FIRST, KV_COLUMNS + HQ, KV_COLUMNS + HQ + half, KV_COLUMNS + HQ + width)
+    w_slots = [w_rows[:, bounds[i] : bounds[i + 1]] for i in both]
+    w_one = [links.first(w_slots[i], i) for i in both]
+    w_one = together(w_one)
+    w_near = [jnp.concatenate([w_slots[i], w_one[i]], axis=0) for i in both]
+    w_far = [links.second(w_near[i], i) for i in both]
+    w_far = together(w_far)
+    grad_pieces = [p for r in rows for p in (grad_near[r], grad_far[r])]
+    grad_pieces += [links.core(p) for p in grad_pieces]
+    grad_all = jnp.concatenate(grad_pieces, axis=0)
+    w_far, grad_all = tie(w_far, grad_all)
+    w_pieces = [
+        [w_near[i], w_far[i], links.core(w_near[i]), links.core(w_far[i])] for i in both
+    ]
+    o_slots = [w_rows[:, bounds[i + 2] : bounds[i + 3]] for i in both]
+    o_slots, w_far = tie(o_slots, w_far)
+    o_one = [links.first(o_slots[i], i) for i in both]
+    o_one = together(o_one)
+    kv, h_one, vec, w_kv = call(
+        project_kv,
+        [
+            shaped(TOKENS, 2 * HK),
+            shaped(TOKENS, width),
+            shaped(8, width, dtype=F32),
+            shaped(width, KV_COLUMNS),
+        ],
+        [pltpu.VMEM((width, KV_COLUMNS), BF16), dma((32,)), dma],
+        in_smem(1) + in_vmem(5) + in_hbm(4),
+        in_vmem(3) + in_hbm(1),
+        2 * TOKENS * width * 2 * HK,
+        4e6,
+        20,
+        name="project_kv",
+    )(starts[0], x, cosine, sine, pick_k, pick_v, *w_pieces[0])
+    kv_own = [kv[at_row[r]] for r in rows]
+    kv_one = [links.first(kv_own[r], order[r]) for r in rows]
+    kv_one = together(kv_one)
+    q, w_q = call(
+        project_q,
+        [shaped(TOKENS, HQ), shaped(width, HQ)],
+        [pltpu.VMEM((width, HQ), BF16), dma((2, 32)), dma],
+        in_smem(2) + in_vmem(4) + in_hbm(8),
+        in_vmem(1) + in_hbm(1),
+        2 * TOKENS * width * HQ,
+        7e6,
+        20,
+        name="project_q",
+    )(*starts, h_one, vec, cosine, sine, *w_pieces[0], *w_pieces[1])
+    kv_near = [jnp.concatenate([kv_own[r], kv_one[r]], axis=0) for r in rows]
+    kv_far = [links.second(kv_near[r], order[r]) for r in rows]
+    kv_far = together(kv_far)
+    kv_far, q = tie(kv_far, q)
+    kv_far, o_one = tie(kv_far, o_one)
+    kv_rows = []
+    for r in rows:
+        kv_rows += [kv_near[r], kv_far[r], links.core(kv_near[r]), links.core(kv_far[r])]
+    o_near = [jnp.concatenate([o_slots[i], o_one[i]], axis=0) for i in both]
+    o_far = [links.second(o_near[i], i) for i in both]
+    o_far = together(o_far)
+    attended, lse = call(
+        attend,
+        [shaped(TOKENS, HQ), shaped(ROWS * KV_HEADS, 1, GROUP * SEG, dtype=F32)],
+        [],
+        in_vmem(2) + in_vmem(8),
+        in_vmem(2),
+        4 * TOKENS * ROW_LEN * HQ,
+        4e6,
+        40,
+        name="attend",
+    )(q, barred, *kv_rows)
+    o_weight = []
+    for i in both:
+        o_weight += [o_near[i], o_far[i], links.core(o_near[i]), links.core(o_far[i])]
+    x_mid, h_two, w_o = call(
+        branch,
+        [shaped(TOKENS, width, dtype=F32), shaped(TOKENS, width), shaped(HQ, width)],
+        [pltpu.VMEM((HQ, width), BF16), dma((2, 32)), dma],
+        in_smem(2) + in_vmem(3) + in_hbm(8),
+        in_vmem(2) + in_hbm(1),
+        2 * TOKENS * width * HQ,
+        8e6,
+        24,
+        name="branch",
+    )(*starts, attended, x, vec, *o_weight)
+
+    h_own = [h_two[at_row[r]] for r in rows]
+    h_one_hop = [links.first(h_own[r], order[r]) for r in rows]
+    h_one_hop = together(h_one_hop)
+    h_one_hop, own_parts[1] = tie(h_one_hop, own_parts[1])
+    weights.append(lax.all_gather(own_parts[1], "wide", axis=1, tiled=True))
+    h_near = [jnp.concatenate([h_own[r], h_one_hop[r]], axis=0) for r in rows]
+    h_far = [links.second(h_near[r], order[r]) for r in rows]
+    h_far = together(h_far)
+    h_pieces = [p for r in rows for p in (h_near[r], h_far[r])]
+    h_pieces += [links.core(p) for p in h_pieces]
+    many = ROWS * ROW_LEN
+    tile_d = pl.BlockSpec((TILE, width), lambda t: (t, 0))
+    size = 3 * split
+    d_t, d_h, mixed, h_all = call(
+        mlp_first,
+        [shaped(size, many), shaped(many, width), shaped(many, width), shaped(many, width)],
+        [
+            pltpu.VMEM((many, width), BF16),
+            pltpu.VMEM((size, width), BF16),
+            dma((8,)),
+            dma((1,)),
+            dma((4,)),
+        ],
+        [tile_d] + in_hbm(9),
+        [pl.BlockSpec((size, TILE), lambda t: (0, t)), tile_d, tile_d] + in_hbm(1),
+        many * width * split,
+        4e6,
+        56,
+        grid=(many // TILE,),
+        name="mlp_first",
+    )(grad_all, *h_pieces, weights[0])
+
+    def grad_of(left_own, left_other, place):
+        size = left_own.shape[0]
+        block = size // 3
+        half_t = [
+            pl.BlockSpec((block, many // 2), lambda k, m, at=at: (m, at)) for at in (0, place)
+        ]
+        right = pl.BlockSpec((many, 2 * cut), lambda k, m: (0, k))
+        return call(
+            weight_grad,
+            shaped(WIDE, size, cut),
+            [],
+            half_t + [right, right],
+            pl.BlockSpec((2, block, cut), lambda k, m: (k, m, 0)),
+            (2.0 if place == 0 else 0.2) * many * width * size,
+            2e7 if place == 0 else 2e6,
+            48,
+            grid=(WIDE // 2, 3),
+            name="weight_grad",
+        )(left_own, left_other, grad_all, h_all)
+
+    def sum_wide(slots):
+        return lax.psum_scatter(slots, "wide", scatter_dimension=0, tiled=False)
+
+    slots_a = grad_of(d_t, d_t, 1)
+    sum_a = sum_wide(slots_a)
+    grad_all, slots_a = tie(grad_all, slots_a)
+    rest = units - split
+
+    def sums(last):
+        if not last:
+            return [shaped(many // 2, width)], [pl.BlockSpec((TILE, width), lambda t: (t, 0))]
+        size = TILE // 2
+        return (
+            [shaped(2 * size, width), shaped(size, width), shaped(size, width)],
+            [pl.BlockSpec((size, width), lambda t: (t, 0))]
+            + [pl.BlockSpec((size, width), lambda t: (0, 0))] * 2,
+        )
+
+    def half_of(place, got):
+        tiles = many // TILE // 2
+        tile_d = pl.BlockSpec((TILE, width), lambda t: (t + place * tiles, 0))
+        tile_o = pl.BlockSpec((TILE, width), lambda t: (t, 0))
+        shapes, specs = sums(bool(got))
+        return call(
+            mlp_second,
+            [shaped(3 * rest, many // 2), shaped(many // 2, rest)] + shapes,
+            [
+                pltpu.VMEM((TILE, 2 * rest), BF16),
+                pltpu.VMEM((3 * rest, width), BF16),
+                dma((2,)),
+            ],
+            [tile_d, tile_d] + in_hbm(1) + [tile_d] + [tile_o] * len(got),
+            [
+                pl.BlockSpec((3 * rest, TILE), lambda t: (0, t)),
+                pl.BlockSpec((TILE, rest), lambda t: (t, 0)),
+            ]
+            + specs,
+            5 * many * width * rest,
+            3e7,
+            50,
+            grid=(tiles,),
+            name="mlp_second",
+        )(grad_all, h_all, weights[1], d_h, *got)
+
+    def down_of(hidden, place, got):
+        tiles = many // TILE // 2
+        tile_o = pl.BlockSpec((TILE, width), lambda t: (t, 0))
+        shapes, specs = sums(bool(got))
+        return call(
+            mlp_down,
+            shapes,
+            [],
+            [
+                pl.BlockSpec((TILE, rest), lambda t: (t, 0)),
+                pl.BlockSpec((rest, width), lambda t: (0, 0)),
+                pl.BlockSpec((TILE, width), lambda t: (t + place * tiles, 0)),
+            ]
+            + [tile_o] * len(got),
+            specs,
+            many * width * rest,
+            1e7,
+            36,
+            grid=(tiles,),
+            name="mlp_down",
+        )(hidden, weights[1], mixed, *got)
+
+    def by_row(value):
+        size = value.shape[0] // ROWS
+        return [value[r * size : (r + 1) * size] for r in rows]
+
+    def second_rows(held):
+        found = [links.scatter_second(held[r], order[r]) for r in rows]
+        return [f[0] for f in found], [f[1] for f in found]
+
+    def first_rows(held):
+        return [part for r in rows for part in links.scatter_first(held[r], order[r])]
+
+    def added(keep, got):
+        return [k + g for k, g in zip(keep, got)]
+
+    d_other, hid_other, other_h = half_of(1, [])
+    got_h = links.core(other_h)
+    (other_m,) = down_of(hid_other, 1, [])
+    got_m = links.core(other_m)
+    got_h, other_m = tie(got_h, other_m)
+    d_own, hid_own, keep_h, *send_h = half_of(0, [got_h])
+    got_h = [links.second(send_h[r], order[r]) for r in rows]
+    got_h = together(got_h)
+    slots_b = grad_of(d_own, d_other, 0)
+    sum_b = sum_wide(slots_b)
+    keep_h, slots_b = tie(keep_h, slots_b)
+    d_h = together(first_rows(added(by_row(keep_h), got_h)))
+    d_h[0], hid_own = tie(d_h[0], hid_own)
+    keep_m, *send_m = down_of(hid_own, 0, [got_m])
+    d_h[0], keep_m = tie(d_h[0], keep_m)
+    send_m, d_h = tie(send_m, d_h)
+    got_m = [links.second(send_m[r], order[r]) for r in rows]
+    got_m = together(got_m)
+
+    def last_sums(held):
+        found = [links.scatter_first(held[i], i) for i in both]
+        return [near + far for near, far in found]
+
+    blocks_half = 16 * SHARE
+    d_mid, d_att, d_gain, *halves_o = call(
+        branch_back,
+        [
+            shaped(TOKENS, width, dtype=F32),
+            shaped(TOKENS, HQ),
+            shaped(1, width, dtype=F32),
+        ]
+        + [shaped(blocks_half, half)] * 4,
+        [pltpu.VMEM((HQ, width), BF16), pltpu.VMEM((HQ, width), BF16), dma, dma((2, 32))],
+        in_smem(2) + in_vmem(8) + in_hbm(1),
+        in_vmem(3) + in_hbm(4),
+        4 * TOKENS * width * HQ,
+        1.5e7,
+        36,
+        name="branch_back",
+    )(*ends, *d_h, x_mid, grad, vec, attended, w_o)
+    own_o, other_o = halves_o[0::2], halves_o[1::2]
+    got_o = [links.core(o) for o in other_o]
+    def back_of(row, d_att):
+        return call(
+            functools.partial(attend_back, row),
+            [shaped(SEG, HQ)] + [shaped(ROW_LEN // 2, 2 * HK)] * 2,
+            [],
+            in_vmem(6) + in_vmem(4),
+            in_vmem(3),
+            5 * TOKENS * ROW_LEN * HQ,
+            5e6,
+            48,
+            name="attend_back",
+        )(q, d_att, cosine, sine, barred, lse, *kv_rows[4 * row : 4 * row + 4])
+
+    dq_a, own_a, other_a = back_of(0, d_att)
+    got_a = links.core(other_a)
+    own_o, dq_a = tie(own_o, dq_a)
+    held_o = added(own_o, got_o)
+    keep_o = [links.scatter_second(held_o[i], i) for i in both]
+    d_att, held_o = tie(d_att, held_o)
+    got_m, d_att = tie(got_m, d_att)
+    keep_m = added(by_row(keep_m), got_m)
+    mixed = first_rows(keep_m)
+    mixed[0], d_att = tie(mixed[0], d_att)
+    dq_b, own_b, other_b = back_of(1, d_att)
+    got_b = links.core(other_b)
+    own_a, dq_b = tie(own_a, dq_b)
+    keep_a, got_a = links.scatter_second(own_a + got_a, order[0])
+    keep_a, dq_b = tie(keep_a, dq_b)
+    d_h_q, d_bias, *halves_q = call(
+        query_back,
+        [shaped(TOKENS, width, dtype=F32), shaped(1, HQ, dtype=F32)] + [shaped(blocks_half, half)] * 4,
+        [pltpu.VMEM((width, HQ), BF16), pltpu.VMEM((width, HQ), BF16), dma, dma((2, 32))],
+        in_smem(2) + in_vmem(3) + in_hbm(1),
+        in_vmem(2) + in_hbm(4),
+        4 * TOKENS * width * HQ,
+        1.2e7,
+        32,
+        name="query_back",
+    )(*ends, dq_a, dq_b, h_one, w_q)
+    own_q, other_q = halves_q[0::2], halves_q[1::2]
+    got_q = [links.core(o) for o in other_q]
+    own_b, d_h_q = tie(own_b, d_h_q)
+    keep_b, got_b = links.scatter_second(own_b + got_b, order[1])
+    keep_a, keep_b = tie(keep_a, keep_b)
+    d_kv = list(links.scatter_first(keep_a + got_a, order[0]))
+    own_q, d_kv = tie(own_q, d_kv)
+    own_q, sum_a = tie(own_q, sum_a)
+    held_q = added(own_q, got_q)
+    keep_b, held_q = tie(keep_b, held_q)
+    d_kv += links.scatter_first(keep_b + got_b, order[1])
+    keep_q = [links.scatter_second(held_q[i], i) for i in both]
+    grad_in, own_w, other_w = call(
+        kv_back,
+        [shaped(TOKENS, width)] + [shaped(16 * SHARE, KV_COLUMNS)] * 2,
+        [pltpu.VMEM((width, KV_COLUMNS), BF16), dma((32,))],
+        in_smem(1) + in_vmem(16),
+        in_vmem(1) + in_hbm(2),
+        4 * TOKENS * width * 2 * HK,
+        1e7,
+        24,
+        name="kv_back",
+    )(
+        ends[0], *d_kv, x, h_one, vec, cosine, sine, d_h_q, d_mid, d_gain, d_bias,
+        pick_k, pick_v, w_kv,
+    )
+    got_w = links.core(other_w)
+    keep_o, d_h_q = tie(keep_o, d_h_q)
+    sum_o = last_sums([k + g for k, g in keep_o])
+    got_w, sum_o = tie(got_w, sum_o)
+    keep_w, got_w = links.scatter_second(own_w + got_w, 0)
+    grad_w_out = links.direct_scatter(jnp.concatenate(sum_o, axis=1))
+    keep_w, keep_q = tie(keep_w, keep_q)
+    near, far = links.scatter_first(keep_w + got_w, 0)
+    sums_q = last_sums([k + g for k, g in keep_q])
+    last = links.direct_scatter(jnp.concatenate([near + far] + sums_q, axis=1))
+    kv_sum, grad_w_query = last[:, :KV_COLUMNS], last[:, KV_COLUMNS:]
+    layer_out = (
+        x_mid
+        + jnp.concatenate([mixed[0], mixed[2]], axis=0).astype(F32)
+        + jnp.concatenate([mixed[1], mixed[3]], axis=0).astype(F32)
+    ).astype(BF16)
+    grad_w_down, grad_w_gate, grad_w_up = [
+        jnp.concatenate(
+            [sum_a[i * split : (i + 1) * split], sum_b[i * rest : (i + 1) * rest]], axis=0
+        ).astype(F32)
+        for i in range(3)
+    ]
+    last = kv_sum[:, 2 * HK : 2 * HK + 4]
+    return (
+        layer_out.reshape(layer_in.shape),
+        grad_in.reshape(layer_in.shape),
+        last[:, 0],
+        grad_w_query,
+        last[:, 2],
+        kv_sum[:, :HK],
+        last[:small, 3],
+        kv_sum[:, HK : 2 * HK],
+        last[small : 2 * small, 3],
+        grad_w_out,
+        last[:, 1],
+        grad_w_gate.T,
+        grad_w_up.T,
+        grad_w_down,
+    )
+
+
+def choose(*args):
+    rows, seg_len, _ = args[0].shape
+    fits = (rows, seg_len, lax.axis_size("narrow"), lax.axis_size("wide"), args[4].shape[0]) == (
+        ROWS,
+        SEG,
+        PARTS,
+        WIDE,
+        SHARE,
+    )
+    return (fast_device if fits else plain_device)(*args)
+
+
 def solution(mesh):
     return jax.shard_map(
-        on_device,
+        choose,
         mesh=mesh,
         in_specs=(
             P("wide", "narrow", None),

time: 1830 us -> 511 us (0.28)
  waiting for transfers between devices: 1360 us -> 143 us
  matrix products: 200 us -> 0 us
  blocking collectives: 187 us -> 0 us
  Pallas kernels: 0 us -> 162 us
  starting transfers between devices: 1.7 us -> 62.8 us
  local copies, waits for them, and re-layouts: 31.7 us -> 85.2 us
    reduce_scatter x11 -> x2, waiting for transfers between devices: 979 us -> 0.01 us  [sum_wide(): return lax.psum_scatter(slots, 'wide', scatter_dimension=0, tiled=False)]
    all_gather x9 -> x3, waiting for transfers between devices: 378 us -> 0.01 us  [the longest x1 0.01 us: fast_device(): w_rows = lax.all_gather(own, 'wide', axis=0, tiled=True)]
    dot_general x31 -> x0, matrix products: 189 us -> none  [the longest x1 19.4 us: on_device(): jnp.einsum('rtd,fd->rtf', grad_all, wd, preferred_element_type=f32)]
    pallas_call x0 -> x16, Pallas kernels: none -> 162 us  [the longest x1 37.3 us: fast_device(): call(mlp_first, [shaped(size, many), shaped(many, width), shaped(many, wi...]
    ppermute x0 -> x80, waiting for transfers between devices: none -> 142 us  [the longest x74 119 us: hop(): return lax.ppermute(value, 'narrow', [(i, i ^ bit) for i in range(PARTS)])]
    all_gather x4 -> x0, blocking collectives: 98.7 us -> none  [the longest x1 42.7 us: on_device(): lax.all_gather(w_value, ('wide', 'narrow'), axis=0, tiled=True)]
    unnamed x2 -> x0, blocking collectives: 88 us -> none
    ppermute x0 -> x80, starting transfers between devices: none -> 62.6 us  [the longest x74 53.7 us: hop(): return lax.ppermute(value, 'narrow', [(i, i ^ bit) for i in range(PARTS)])]
  transfers between devices with their start and end apart: 20 -> 85, of which waited for: 18 -> 35; matrix products, arithmetic and copies ran while one was open for 9% -> 14% of each run, Pallas kernels for 0% -> 29%
where the time goes in v3:
time: 511 us; the launch traced here: 505 us
  Pallas kernels  162 us (32%)
  waiting for transfers between devices  143 us (28%)
  local copies, waits for them, and re-layouts  85.2 us (17%)
  starting transfers between devices  62.8 us (12%)
  other arithmetic  36.3 us (7%)
  between operations  15.8 us (3%)
    ppermute x74, waiting for transfers between devices, hop(): return lax.ppermute(value, 'narrow', [(i, i ^ bit) for i in range(PARTS)])  119 us
    unnamed x236, local copies, waits for them, and re-layouts  59.8 us
    ppermute x74, starting transfers between devices, hop(): return lax.ppermute(value, 'narrow', [(i, i ^ bit) for i in range(PARTS)])  53.7 us
    pallas_call x1, Pallas kernels, fast_device(): call(mlp_first, [shaped(size, many), shaped(many, width), shaped(many, wi...  37.3 us
    pallas_call x2, Pallas kernels, grad_of(): call(weight_grad, shaped(WIDE, size, cut), [], half_t + [right, right], p...  34.8 us
    pallas_call x2, Pallas kernels, half_of(): call(mlp_second, [shaped(3 * rest, many // 2), shaped(many // 2, rest)] +...  33.4 us
    ppermute x6, waiting for transfers between devices, over_wide(): lax.ppermute(value, 'wide', [(i, (i + step) % WIDE) for i in range(WIDE)])  23.7 us
  transfers between devices with their start and end apart: 85, of which 35 were waited for; matrix products, arithmetic and copies ran while one was open for 14% of the time, Pallas kernels for 29%

profile of v3, /device:TPU:0, one launch (start us, length us, event | category | flops | bytes accessed | tf_op | source)
XLA Modules:
  0.0 505.1 jit_solution(15668356736689568870)
XLA Ops:
  38.3 13.2 %collective-permute-done.6 = bf16[256,1536]{1,0:T(8,128)(2,1)} collective-permute-done((bf16[256,1536]{1,0:T(8,128)(2,1)}, bf16[256,1536]{1,0:T(8,128)(2,1)}, u32[]{:S(2)}, u32[]{:S(2)}) %collective-permute-start.6) | collective-permute-done | bytes 786464 | tf_op jit(solution)/shard_map/ppermute | solution.py:297
  75.7 10.1 %collective-permute-done.10.refs_5_ = bf16[384,1024]{1,0:T(8,128)(2,1)} collective-permute-done((bf16[384,1024]{1,0:T(8,128)(2,1)S(1)}, bf16[384,1024]{1,0:T(8,128)(2,1)}, u32[]{:S(2)}, u32[]{:S(2)}) %collective-permute-start.10) | collective-permute-done | bytes 786464 | tf_op jit(solution)/shard_map/ppermute | solution.py:297
  120.8 5.2 %project_q.1 = (bf16[256,1536]{1,0:T(8,128)(2,1)S(1)}, bf16[1536,1536]{1,0:T(8,128)(2,1)S(1)}) custom-call(s32[32]{0:T(128)S(1)} %mul.70.starts.starts_a, s32[32]{0:T(128)S(1)} %mul.72.starts_b, bf16[256,1536]{1,0:T(8,128)(2,1)S(1)} %copy-done.45, f32[8,1536]{1,0:T(8,128)S(1)} %copy-done.59, f32[256,128]{1,0:T(8,128)S(1)} %copy-done.15, ...), custom_call_target="tpu_custom_call" | custom-call | flops 12079595520 | bytes 70000000 | tf_op jit(solution)/shard_map/project_q/pallas_call | solution.py:927
  131.6 11.3 %collective-permute-done.30.refs_5_ = bf16[384,768]{1,0:T(8,128)(2,1)S(1)} collective-permute-done((bf16[384,768]{1,0:T(8,128)(2,1)S(1)}, bf16[384,768]{1,0:T(8,128)(2,1)S(1)}, u32[]{:S(2)}, u32[]{:S(2)}) %collective-permute-start.30) | collective-permute-done | bytes 589856 | tf_op jit(solution)/shard_map/ppermute | solution.py:297
  144.4 5.8 %attend.1 = (bf16[256,1536]{1,0:T(8,128)(2,1)S(1)}, f32[4,1,768]{2,1,0:T(1,128)S(1)}) custom-call(bf16[256,1536]{1,0:T(8,128)(2,1)S(1)} %get-tuple-element.185.q, f32[2,1024,128]{2,1,0:T(8,128)S(1)} %or_select_fusion.barred, bf16[256,512]{1,0:T(8,128)(2,1)S(1)} %pad_maximum_fusion.9.refs_0_, bf16[256,512]{1,0:T(8,128)(2,1)S(1)} %collective-permute-done.19.refs_1_, ...), custom_call_target="tpu_custom_call" | custom-call | flops 16106127360 | bytes 40000000 | tf_op jit(solution)/shard_map/attend/pallas_call | solution.py:949
  162.5 6.0 %collective-permute-done.36 = bf16[128,1536]{1,0:T(8,128)(2,1)S(1)} collective-permute-done((bf16[128,1536]{1,0:T(8,128)(2,1)S(1)}, bf16[128,1536]{1,0:T(8,128)(2,1)S(1)}, u32[]{:S(2)}, u32[]{:S(2)}) %collective-permute-start.36) | collective-permute-done | bytes 393248 | tf_op jit(solution)/shard_map/ppermute | solution.py:297
  174.8 15.8 %collective-permute-done.38.refs_3_ = bf16[256,1536]{1,0:T(8,128)(2,1)S(1)} collective-permute-done((bf16[256,1536]{1,0:T(8,128)(2,1)S(1)}, bf16[256,1536]{1,0:T(8,128)(2,1)S(1)}, u32[]{:S(2)}, u32[]{:S(2)}) %collective-permute-start.38) | collective-permute-done | bytes 786464 | tf_op jit(solution)/shard_map/ppermute | solution.py:297
  195.9 37.3 %mlp_first.1 = (bf16[1920,2048]{1,0:T(8,128)(2,1)}, bf16[2048,1536]{1,0:T(8,128)(2,1)}, bf16[2048,1536]{1,0:T(8,128)(2,1)}, bf16[2048,1536]{1,0:T(8,128)(2,1)}) custom-call(bf16[2048,1536]{1,0:T(8,128)(2,1)} %constant_dynamic-update-slice_fusion.21.grad.right_grad, bf16[256,1536]{1,0:T(8,128)(2,1)} %copy-done.88, bf16[256,1536]{1,0:T(8,128)(2,1)} %copy-done.101, ...), custom_call_target="tpu_custom_call" | custom-call | flops 20132659200 | bytes 40000000 | tf_op jit(solution)/shard_map/mlp_first/pallas_call | solution.py:988
  233.2 19.0 %weight_grad.2 = bf16[4,1920,384]{2,1,0:T(8,128)(2,1)S(1)} custom-call(bf16[1920,2048]{1,0:T(8,128)(2,1)} %get-tuple-element.210.left_own.left_other, bf16[1920,2048]{1,0:T(8,128)(2,1)} %get-tuple-element.210.left_own.left_other, bf16[2048,1536]{1,0:T(8,128)(2,1)} %constant_dynamic-update-slice_fusion.21.grad.right_grad, ...), custom_call_target="tpu_custom_call" | custom-call | flops 12079595520 | bytes 20000000 | tf_op jit(solution)/shard_map/weight_grad/pallas_call | solution.py:1014
  254.8 15.8 %mlp_second.2 = (bf16[1440,1024]{1,0:T(8,128)(2,1)S(1)}, bf16[1024,480]{1,0:T(8,128)(2,1)S(1)}, bf16[1024,1536]{1,0:T(8,128)(2,1)}) custom-call(bf16[2048,1536]{1,0:T(8,128)(2,1)} %constant_dynamic-update-slice_fusion.21.grad.right_grad, bf16[2048,1536]{1,0:T(8,128)(2,1)} %get-tuple-element.211.right_h.h, ...), custom_call_target="tpu_custom_call" | custom-call | flops 75497472000 | bytes 300000000 | tf_op jit(solution)/shard_map/mlp_second/pallas_call | solution.py:1050
  281.2 17.5 %mlp_second.3 = (bf16[1440,1024]{1,0:T(8,128)(2,1)}, bf16[1024,480]{1,0:T(8,128)(2,1)S(1)}, bf16[512,1536]{1,0:T(8,128)(2,1)}, bf16[256,1536]{1,0:T(8,128)(2,1)}, bf16[256,1536]{1,0:T(8,128)(2,1)S(1)}) custom-call(bf16[2048,1536]{1,0:T(8,128)(2,1)} %constant_dynamic-update-slice_fusion.21.grad.right_grad, bf16[2048,1536]{1,0:T(8,128)(2,1)} %get-tuple-element.211.right_h.h, ...), custom_call_target="tpu_custom_call" | custom-call | flops 75497472000 | bytes 300000000 | tf_op jit(solution)/shard_map/mlp_second/pallas_call | solution.py:1050
  304.4 15.8 %weight_grad.3 = bf16[4,1440,384]{2,1,0:T(8,128)(2,1)} custom-call(bf16[1440,1024]{1,0:T(8,128)(2,1)S(1)} %copy-done.72, bf16[1440,1024]{1,0:T(8,128)(2,1)S(1)} %copy-done.74, bf16[2048,1536]{1,0:T(8,128)(2,1)} %constant_dynamic-update-slice_fusion.21.grad.right_grad, bf16[2048,1536]{1,0:T(8,128)(2,1)} %get-tuple-element.211.right_h.h), custom_call_target="tpu_custom_call" | custom-call | flops 90596966400 | bytes 200000000 | tf_op jit(solution)/shard_map/weight_grad/pallas_call | solution.py:1014
  326.1 7.5 %collective-permute-done.47.got_b = bf16[128,1536]{1,0:T(8,128)(2,1)S(1)} collective-permute-done((bf16[128,1536]{1,0:T(8,128)(2,1)}, bf16[128,1536]{1,0:T(8,128)(2,1)S(1)}, u32[]{:S(2)}, u32[]{:S(2)}) %collective-permute-start.47) | collective-permute-done | bytes 393248 | tf_op jit(solution)/shard_map/ppermute | solution.py:297
  341.0 4.8 mlp_down.3
  351.9 7.4 %branch_back.1 = (f32[256,1536]{1,0:T(8,128)S(1)}, bf16[256,1536]{1,0:T(8,128)(2,1)S(1)}, f32[1,1536]{1,0:T(1,128)S(1)}, bf16[768,768]{1,0:T(8,128)(2,1)S(1)}, b...) custom-call(s32[32]{0:T(128)S(1)} %mul.82.starts_a.starts, ...), custom_call_target="tpu_custom_call" | custom-call | flops 24159191040 | bytes 150000000 | tf_op jit(solution)/shard_map/branch_back/pallas_call | solution.py:1131
  361.0 4.9 attend_back.2
  372.0 5.2 %attend_back.3 = (bf16[128,1536]{1,0:T(8,128)(2,1)S(1)}, bf16[512,512]{1,0:T(8,128)(2,1)S(1)}, bf16[512,512]{1,0:T(8,128)(2,1)S(1)}) custom-call(bf16[256,1536]{1,0:T(8,128)(2,1)S(1)} %copy-done.67, bf16[256,1536]{1,0:T(8,128)(2,1)S(1)} %copy-done.71, f32[256,128]{1,0:T(8,128)S(1)} %copy-done.16, f32[256,128]{1,0:T(8,128)S(1)} %copy-done.12, ...), custom_call_target="tpu_custom_call" | custom-call | flops 20132659200 | bytes 50000000 | tf_op jit(solution)/shard_map/attend_back/pallas_call | solution.py:1150
  383.3 5.2 %query_back.1 = (f32[256,1536]{1,0:T(8,128)S(1)}, f32[1,1536]{1,0:T(1,128)S(1)}, bf16[768,768]{1,0:T(8,128)(2,1)S(1)}, bf16[768,768]{1,0:T(8,128)(2,1)}, bf16[76...) custom-call(s32[32]{0:T(128)S(1)} %mul.82.starts_a.starts, s32[32]{0:T(128)S(1)} %mul.84.starts_b, ...), custom_call_target="tpu_custom_call" | custom-call | flops 24159191040 | bytes 120000000 | tf_op jit(solution)/shard_map/query_back/pallas_call | solution.py:1177
  399.7 4.7 collective-permute-done.53
  420.3 6.7 %kv_back.1 = (bf16[256,1536]{1,0:T(8,128)(2,1)}, bf16[768,640]{1,0:T(8,128)(2,1)S(1)}, bf16[768,640]{1,0:T(8,128)(2,1)S(1)}) custom-call(s32[32]{0:T(128)S(1)} %mul.82.starts_a.starts, bf16[128,512]{1,0:T(8,128)(2,1)S(1)} %copy-done.18, bf16[128,512]{1,0:T(8,128)(2,1)S(1)} %copy-done.37, bf16[128,512]{1,0:T(8,128)(2,1)S(1)} %get-tuple-element.364.keep_b, ...), custom_call_target="tpu_custom_call" | custom-call | flops 8053063680 | bytes 100000000 | tf_op jit(solution)/shard_map/kv_back/pallas_call | solution.py:1200
  431.9 11.5 %collective-permute-done.68 = bf16[384,768]{1,0:T(8,128)(2,1)S(1)} collective-permute-done((bf16[384,768]{1,0:T(8,128)(2,1)S(1)}, bf16[384,768]{1,0:T(8,128)(2,1)S(1)}, u32[]{:S(2)}, u32[]{:S(2)}) %collective-permute-start.68) | collective-permute-done | bytes 589856 | tf_op jit(solution)/shard_map/ppermute | solution.py:297
  465.4 6.8 %collective-permute-done.78 = bf16[48,1536]{1,0:T(8,128)(2,1)S(1)} collective-permute-done((bf16[48,1536]{1,0:T(8,128)(2,1)S(1)}, bf16[48,1536]{1,0:T(8,128)(2,1)S(1)}, u32[]{:S(2)}, u32[]{:S(2)}) %collective-permute-start.78) | collective-permute-done | bytes 147488 | tf_op jit(solution)/shard_map/ppermute | solution.py:328
  473.0 6.9 %collective-permute-done.76 = bf16[48,2176]{1,0:T(8,128)(2,1)S(1)} collective-permute-done((bf16[48,2176]{1,0:T(8,128)(2,1)S(1)}, bf16[48,2176]{1,0:T(8,128)(2,1)S(1)}, u32[]{:S(2)}, u32[]{:S(2)}) %collective-permute-start.76) | collective-permute-done | bytes 208928 | tf_op jit(solution)/shard_map/ppermute | solution.py:328
  480.0 10.0 %collective-permute-done.75 = bf16[48,2176]{1,0:T(8,128)(2,1)S(1)} collective-permute-done((bf16[48,2176]{1,0:T(8,128)(2,1)S(1)}, bf16[48,2176]{1,0:T(8,128)(2,1)S(1)}, u32[]{:S(2)}, u32[]{:S(2)}) %collective-permute-start.75) | collective-permute-done | bytes 208928 | tf_op jit(solution)/shard_map/ppermute | solution.py:328
  (516 shorter events, 234.8 us)
Async XLA Ops:
  7.2 45.9 %all-gather.4.cloned.1.call-start = ((), (), s32[]{:S(2)}) async-start(), calls=%async_computation.2 | async-start | bytes 1781760 | tf_op jit(solution)/shard_map/all_gather | solution.py:853
  16.6 179.3 %all-gather.6.cloned.1.call-start = ((), (), s32[]{:S(2)}) async-start(), calls=%async_computation.3 | async-start | bytes 7372800 | tf_op jit(solution)/shard_map/all_gather | solution.py:889
  31.6 19.9 %collective-permute-start.6 = (bf16[256,1536]{1,0:T(8,128)(2,1)}, bf16[256,1536]{1,0:T(8,128)(2,1)}, u32[]{:S(2)}, u32[]{:S(2)}) collective-permute-start(bf16[256,1536]{1,0:T(8,128)(2,1)} %pad_maximum_fusion.5), channel_id=1, source_target_pairs={{0,2},{1,3},{2,0},{3,1},{4,6},{5,7},{6,4},{7,5},{8,10},{9,11},{10,... | collective-permute-start | bytes 2359304 | tf_op jit(solution)/shard_map/ppermute | solution.py:297
  33.5 19.6 %collective-permute-start.5 = (bf16[256,1536]{1,0:T(8,128)(2,1)}, bf16[256,1536]{1,0:T(8,128)(2,1)}, u32[]{:S(2)}, u32[]{:S(2)}) collective-permute-start(bf16[256,1536]{1,0:T(8,128)(2,1)} %pad_maximum_fusion.4), channel_id=1, source_target_pairs={{0,4},{1,5},{2,6},{3,7},{4,0},{5,1},{6,2},{7,3},{8,12},{9,13},{10,... | collective-permute-start | bytes 2359304 | tf_op jit(solution)/shard_map/ppermute | solution.py:297
  37.0 35.7 %collective-permute-start.13 = (bf16[256,1536]{1,0:T(8,128)(2,1)}, bf16[256,1536]{1,0:T(8,128)(2,1)}, u32[]{:S(2)}, u32[]{:S(2)}) collective-permute-start(bf16[256,1536]{1,0:T(8,128)(2,1)} %pad_maximum_fusion.5), channel_id=1, source_target_pairs={{0,1},{1,0},{2,3},{3,2},{4,5},{5,4},{6,7},{7,6},{8,9},{9,8},{10,11... | collective-permute-start | bytes 2359304 | tf_op jit(solution)/shard_map/ppermute | solution.py:297
  37.1 32.0 %collective-permute-start.11 = (bf16[256,1536]{1,0:T(8,128)(2,1)}, bf16[256,1536]{1,0:T(8,128)(2,1)}, u32[]{:S(2)}, u32[]{:S(2)}) collective-permute-start(bf16[256,1536]{1,0:T(8,128)(2,1)} %pad_maximum_fusion.4), channel_id=1, source_target_pairs={{0,1},{1,0},{2,3},{3,2},{4,5},{5,4},{6,7},{7,6},{8,9},{9,8},{10,11... | collective-permute-start | bytes 2359304 | tf_op jit(solution)/shard_map/ppermute | solution.py:297
  55.4 199.4 %all-gather.8.cloned.1.call-start = ((), (), s32[]{:S(2)}) async-start(), calls=%async_computation.4 | async-start | bytes 5529600 | tf_op jit(solution)/shard_map/all_gather | solution.py:979
  69.1 19.6 %collective-permute-start.9 = (bf16[384,1152]{1,0:T(8,128)(2,1)S(1)}, bf16[384,1152]{1,0:T(8,128)(2,1)}, u32[]{:S(2)}, u32[]{:S(2)}) collective-permute-start(bf16[384,1152]{1,0:T(8,128)(2,1)S(1)} %pad_maximum_fusion.2.refs_0_), channel_id=1, source_target_pairs={{0,4},{1,5},{2,6},{3,7},{4,0},{5,1},{6,2},{7,3},{8,12},{9,13},{10,... | collective-permute-start | bytes 2654216 | tf_op jit(solution)/shard_map/ppermute | solution.py:297
  71.7 21.1 %collective-permute-start.15 = (bf16[384,1152]{1,0:T(8,128)(2,1)S(1)}, bf16[384,1152]{1,0:T(8,128)(2,1)}, u32[]{:S(2)}, u32[]{:S(2)}) collective-permute-start(bf16[384,1152]{1,0:T(8,128)(2,1)S(1)} %pad_maximum_fusion.2.refs_0_), channel_id=1, source_target_pairs={{0,1},{1,0},{2,3},{3,2},{4,5},{5,4},{6,7},{7,6},{8,9},{9,8},{10,11... | collective-permute-start | bytes 2654216 | tf_op jit(solution)/shard_map/ppermute | solution.py:297
  91.3 25.7 %collective-permute-start.21 = (bf16[384,1024]{1,0:T(8,128)(2,1)S(1)}, bf16[384,1024]{1,0:T(8,128)(2,1)}, u32[]{:S(2)}, u32[]{:S(2)}) collective-permute-start(bf16[384,1024]{1,0:T(8,128)(2,1)S(1)} %pad_maximum_fusion.6.refs_4_), channel_id=1, source_target_pairs={{0,1},{1,0},{2,3},{3,2},{4,5},{5,4},{6,7},{7,6},{8,9},{9,8},{10,11... | collective-permute-start | bytes 2359304 | tf_op jit(solution)/shard_map/ppermute | solution.py:297
  91.8 25.2 %collective-permute-start.22 = (bf16[384,1024]{1,0:T(8,128)(2,1)}, bf16[384,1024]{1,0:T(8,128)(2,1)}, u32[]{:S(2)}, u32[]{:S(2)}) collective-permute-start(bf16[384,1024]{1,0:T(8,128)(2,1)} %collective-permute-done.10.refs_5_), channel_id=1, source_target_pairs={{0,1},{1,0},{2,3},{3,2},{4,5},{5,4},{6,7},{7,6},{8,9},{9,8},{10,11... | collective-permute-start | bytes 2359304 | tf_op jit(solution)/shard_map/ppermute | solution.py:297
  169.1 240.8 %reduce-scatter.3.cloned.1.call-start = ((), (), s32[]{:S(2)}) async-start(), calls=%async_computation.5 | async-start | bytes 7372800 | tf_op jit(solution)/shard_map/reduce_scatter | solution.py:1028
  272.4 220.5 %reduce-scatter.5.cloned.1.call-start = ((), (), s32[]{:S(2)}) async-start(), calls=%async_computation.6 | async-start | bytes 5529600 | tf_op jit(solution)/shard_map/reduce_scatter | solution.py:1028
  280.8 54.0 %collective-permute-start.48 = (bf16[1024,1536]{1,0:T(8,128)(2,1)}, bf16[1024,1536]{1,0:T(8,128)(2,1)}, u32[]{:S(2)}, u32[]{:S(2)}) collective-permute-start(bf16[1024,1536]{1,0:T(8,128)(2,1)} %mlp_down.2), channel_id=1, source_target_pairs={{0,1},{1,0},{2,3},{3,2},{4,5},{5,4},{6,7},{7,6},{8,9},{9,8},{10,11... | collective-permute-start | bytes 9437192 | tf_op jit(solution)/shard_map/ppermute | solution.py:297
  299.7 20.5 %collective-permute-start.44 = (bf16[256,1536]{1,0:T(8,128)(2,1)}, bf16[256,1536]{1,0:T(8,128)(2,1)}, u32[]{:S(2)}, u32[]{:S(2)}) collective-permute-start(bf16[256,1536]{1,0:T(8,128)(2,1)} %get-tuple-element.223), channel_id=1, source_target_pairs={{0,4},{1,5},{2,6},{3,7},{4,0},{5,1},{6,2},{7,3},{8,12},{9,13},{10,... | collective-permute-start | bytes 2359304 | tf_op jit(solution)/shard_map/ppermute | solution.py:297
  301.1 19.2 %collective-permute-start.45 = (bf16[256,1536]{1,0:T(8,128)(2,1)S(1)}, bf16[256,1536]{1,0:T(8,128)(2,1)}, u32[]{:S(2)}, u32[]{:S(2)}) collective-permute-start(bf16[256,1536]{1,0:T(8,128)(2,1)S(1)} %get-tuple-element.224), channel_id=1, source_target_pairs={{0,2},{1,3},{2,0},{3,1},{4,6},{5,7},{6,4},{7,5},{8,10},{9,11},{10,... | collective-permute-start | bytes 2359304 | tf_op jit(solution)/shard_map/ppermute | solution.py:297
  345.8 20.3 %collective-permute-start.49 = (bf16[256,1536]{1,0:T(8,128)(2,1)}, bf16[256,1536]{1,0:T(8,128)(2,1)}, u32[]{:S(2)}, u32[]{:S(2)}) collective-permute-start(bf16[256,1536]{1,0:T(8,128)(2,1)} %get-tuple-element.239), channel_id=1, source_target_pairs={{0,4},{1,5},{2,6},{3,7},{4,0},{5,1},{6,2},{7,3},{8,12},{9,13},{10,... | collective-permute-start | bytes 2359304 | tf_op jit(solution)/shard_map/ppermute | solution.py:297
  368.7 22.6 %collective-permute-start.64 = (bf16[384,768]{1,0:T(8,128)(2,1)}, bf16[384,768]{1,0:T(8,128)(2,1)S(1)}, u32[]{:S(2)}, u32[]{:S(2)}) collective-permute-start(bf16[384,768]{1,0:T(8,128)(2,1)} %get-tuple-element.332), channel_id=1, source_target_pairs={{0,4},{1,5},{2,6},{3,7},{4,0},{5,1},{6,2},{7,3},{8,12},{9,13},{10,... | collective-permute-start | bytes 1769480 | tf_op jit(solution)/shard_map/ppermute | solution.py:297
  388.5 21.5 %collective-permute-start.59 = (bf16[768,768]{1,0:T(8,128)(2,1)}, bf16[768,768]{1,0:T(8,128)(2,1)}, u32[]{:S(2)}, u32[]{:S(2)}) collective-permute-start(bf16[768,768]{1,0:T(8,128)(2,1)} %get-tuple-element.285), channel_id=1, source_target_pairs={{0,1},{1,0},{2,3},{3,2},{4,5},{5,4},{6,7},{7,6},{8,9},{9,8},{10,11... | collective-permute-start | bytes 3538952 | tf_op jit(solution)/shard_map/ppermute | solution.py:297
  388.8 23.0 %collective-permute-start.60 = (bf16[768,768]{1,0:T(8,128)(2,1)}, bf16[768,768]{1,0:T(8,128)(2,1)}, u32[]{:S(2)}, u32[]{:S(2)}) collective-permute-start(bf16[768,768]{1,0:T(8,128)(2,1)} %get-tuple-element.287), channel_id=1, source_target_pairs={{0,1},{1,0},{2,3},{3,2},{4,5},{5,4},{6,7},{7,6},{8,9},{9,8},{10,11... | collective-permute-start | bytes 3538952 | tf_op jit(solution)/shard_map/ppermute | solution.py:297
  409.2 20.1 %collective-permute-start.67 = (bf16[192,768]{1,0:T(8,128)(2,1)}, bf16[192,768]{1,0:T(8,128)(2,1)}, u32[]{:S(2)}, u32[]{:S(2)}) collective-permute-start(bf16[192,768]{1,0:T(8,128)(2,1)} %slice.477), channel_id=1, source_target_pairs={{0,4},{1,5},{2,6},{3,7},{4,0},{5,1},{6,2},{7,3},{8,12},{9,13},{10,... | collective-permute-start | bytes 884744 | tf_op jit(solution)/shard_map/ppermute | solution.py:297
  430.8 23.7 %collective-permute-start.70 = (bf16[384,640]{1,0:T(8,128)(2,1)S(1)}, bf16[384,640]{1,0:T(8,128)(2,1)S(1)}, u32[]{:S(2)}, u32[]{:S(2)}) collective-permute-start(bf16[384,640]{1,0:T(8,128)(2,1)S(1)} %get-tuple-element.337), channel_id=1, source_target_pairs={{0,4},{1,5},{2,6},{3,7},{4,0},{5,1},{6,2},{7,3},{8,12},{9,13},{10,... | collective-permute-start | bytes 1474568 | tf_op jit(solution)/shard_map/ppermute | solution.py:297
  452.3 19.9 %collective-permute-start.78 = (bf16[48,1536]{1,0:T(8,128)(2,1)S(1)}, bf16[48,1536]{1,0:T(8,128)(2,1)S(1)}, u32[]{:S(2)}, u32[]{:S(2)}) collective-permute-start(bf16[48,1536]{1,0:T(8,128)(2,1)S(1)} %get-tuple-element.356), channel_id=1, source_target_pairs={{0,16},{8,24},{16,0},{24,8},{1,17},{9,25},{17,1},{25,9},{2,18},{10... | collective-permute-start | bytes 442376 | tf_op jit(solution)/shard_map/ppermute | solution.py:328
  464.5 25.4 %collective-permute-start.75 = (bf16[48,2176]{1,0:T(8,128)(2,1)S(1)}, bf16[48,2176]{1,0:T(8,128)(2,1)S(1)}, u32[]{:S(2)}, u32[]{:S(2)}) collective-permute-start(bf16[48,2176]{1,0:T(8,128)(2,1)S(1)} %get-tuple-element.341), channel_id=1, source_target_pairs={{0,16},{8,24},{16,0},{24,8},{1,17},{9,25},{17,1},{25,9},{2,18},{10... | collective-permute-start | bytes 626696 | tf_op jit(solution)/shard_map/ppermute | solution.py:328
  (168 other events, 1463.6 us)
Sparse Core Ops, SparseCore 0:
  16.7 34.9 all-gather.3
  55.5 109.6 all-gather.5
  169.3 85.3 all-gather.7
  272.5 104.1 reduce-scatter.2
  378.8 88.2 reduce-scatter.4

commit v4 on v3

--- a/solution.py
+++ b/solution.py
@@ -369,7 +369,7 @@
         name=name,
         compiler_params=pltpu.CompilerParams(vmem_limit_bytes=vmem * 1024 * 1024),
         cost_estimate=pl.CostEstimate(
-            flops=10 * int(flops), bytes_accessed=10 * int(nbytes), transcendentals=0
+            flops=int(flops), bytes_accessed=int(nbytes), transcendentals=0
         ),
     )
 
@@ -918,7 +918,7 @@
         in_vmem(3) + in_hbm(1),
         2 * TOKENS * width * 2 * HK,
         4e6,
-        20,
+        60,
         name="project_kv",
     )(starts[0], x, cosine, sine, pick_k, pick_v, *w_pieces[0])
     kv_own = [kv[at_row[r]] for r in rows]
@@ -932,20 +932,18 @@
         in_vmem(1) + in_hbm(1),
         2 * TOKENS * width * HQ,
         7e6,
-        20,
+        60,
         name="project_q",
     )(*starts, h_one, vec, cosine, sine, *w_pieces[0], *w_pieces[1])
     kv_near = [jnp.concatenate([kv_own[r], kv_one[r]], axis=0) for r in rows]
     kv_far = [links.second(kv_near[r], order[r]) for r in rows]
     kv_far = together(kv_far)
     kv_far, q = tie(kv_far, q)
-    kv_far, o_one = tie(kv_far, o_one)
     kv_rows = []
     for r in rows:
         kv_rows += [kv_near[r], kv_far[r], links.core(kv_near[r]), links.core(kv_far[r])]
     o_near = [jnp.concatenate([o_slots[i], o_one[i]], axis=0) for i in both]
     o_far = [links.second(o_near[i], i) for i in both]
-    o_far = together(o_far)
     attended, lse = call(
         attend,
         [shaped(TOKENS, HQ), shaped(ROWS * KV_HEADS, 1, GROUP * SEG, dtype=F32)],
@@ -957,6 +955,7 @@
         40,
         name="attend",
     )(q, barred, *kv_rows)
+    attended, o_far = tie(attended, o_far)
     o_weight = []
     for i in both:
         o_weight += [o_near[i], o_far[i], links.core(o_near[i]), links.core(o_far[i])]
@@ -968,7 +967,7 @@
         in_vmem(2) + in_hbm(1),
         2 * TOKENS * width * HQ,
         8e6,
-        24,
+        60,
         name="branch",
     )(*starts, attended, x, vec, *o_weight)
 
@@ -1085,7 +1084,7 @@
             specs,
             many * width * rest,
             1e7,
-            36,
+            60,
             grid=(tiles,),
             name="mlp_down",
         )(hidden, weights[1], mixed, *got)
@@ -1115,7 +1114,7 @@
     slots_b = grad_of(d_own, d_other, 0)
     sum_b = sum_wide(slots_b)
     keep_h, slots_b = tie(keep_h, slots_b)
-    d_h = together(first_rows(added(by_row(keep_h), got_h)))
+    d_h = first_rows(added(by_row(keep_h), got_h))
     d_h[0], hid_own = tie(d_h[0], hid_own)
     keep_m, *send_m = down_of(hid_own, 0, [got_m])
     d_h[0], keep_m = tie(d_h[0], keep_m)
@@ -1141,7 +1140,7 @@
         in_vmem(3) + in_hbm(4),
         4 * TOKENS * width * HQ,
         1.5e7,
-        36,
+        60,
         name="branch_back",
     )(*ends, *d_h, x_mid, grad, vec, attended, w_o)
     own_o, other_o = halves_o[0::2], halves_o[1::2]
@@ -1165,11 +1164,8 @@
     held_o = added(own_o, got_o)
     keep_o = [links.scatter_second(held_o[i], i) for i in both]
     d_att, held_o = tie(d_att, held_o)
-    got_m, d_att = tie(got_m, d_att)
-    keep_m = added(by_row(keep_m), got_m)
-    mixed = first_rows(keep_m)
-    mixed[0], d_att = tie(mixed[0], d_att)
     dq_b, own_b, other_b = back_of(1, d_att)
+    dq_b, sum_a = tie(dq_b, sum_a)
     got_b = links.core(other_b)
     own_a, dq_b = tie(own_a, dq_b)
     keep_a, got_a = links.scatter_second(own_a + got_a, order[0])
@@ -1182,7 +1178,7 @@
         in_vmem(2) + in_hbm(4),
         4 * TOKENS * width * HQ,
         1.2e7,
-        32,
+        60,
         name="query_back",
     )(*ends, dq_a, dq_b, h_one, w_q)
     own_q, other_q = halves_q[0::2], halves_q[1::2]
@@ -1192,7 +1188,6 @@
     keep_a, keep_b = tie(keep_a, keep_b)
     d_kv = list(links.scatter_first(keep_a + got_a, order[0]))
     own_q, d_kv = tie(own_q, d_kv)
-    own_q, sum_a = tie(own_q, sum_a)
     held_q = added(own_q, got_q)
     keep_b, held_q = tie(keep_b, held_q)
     d_kv += links.scatter_first(keep_b + got_b, order[1])
@@ -1215,12 +1210,16 @@
     keep_o, d_h_q = tie(keep_o, d_h_q)
     sum_o = last_sums([k + g for k, g in keep_o])
     got_w, sum_o = tie(got_w, sum_o)
+    got_m, own_w = tie(got_m, own_w)
+    mixed = first_rows(added(by_row(keep_m), got_m))
     keep_w, got_w = links.scatter_second(own_w + got_w, 0)
     grad_w_out = links.direct_scatter(jnp.concatenate(sum_o, axis=1))
     keep_w, keep_q = tie(keep_w, keep_q)
     near, far = links.scatter_first(keep_w + got_w, 0)
     sums_q = last_sums([k + g for k, g in keep_q])
-    last = links.direct_scatter(jnp.concatenate([near + far] + sums_q, axis=1))
+    held_last = jnp.concatenate([near + far] + sums_q, axis=1)
+    held_last, sum_b = tie(held_last, sum_b)
+    last = links.direct_scatter(held_last)
     kv_sum, grad_w_query = last[:, :KV_COLUMNS], last[:, KV_COLUMNS:]
     layer_out = (
         x_mid

time: 511 us -> 488 us (0.955)
  local copies, waits for them, and re-layouts: 85.2 us -> 56.1 us
  Pallas kernels: 162 us -> 185 us
  waiting for transfers between devices: 143 us -> 133 us
  other arithmetic: 36.3 us -> 29.7 us
    unnamed x236 -> x170, local copies, waits for them, and re-layouts: 59.8 us -> 31.4 us
    ppermute x74, waiting for transfers between devices: 119 us -> 106 us  [hop(): return lax.ppermute(value, 'narrow', [(i, i ^ bit) for i in range(PARTS)])]
    all_gather x1, waiting for transfers between devices: 0.01 us -> 5.23 us  [fast_device(): weights.append(lax.all_gather(own_parts[1], 'wide', axis=1, tiled=True))]
  transfers between devices with their start and end apart: 85 -> 85, of which waited for: 35 -> 40; matrix products, arithmetic and copies ran while one was open for 14% -> 13% of each run, Pallas kernels for 29% -> 38%
where the time goes in v4:
time: 488 us; the launch traced here: 484 us
  Pallas kernels  185 us (38%)
  waiting for transfers between devices  133 us (27%)
  starting transfers between devices  64.4 us (13%)
  local copies, waits for them, and re-layouts  56.1 us (11%)
  other arithmetic  29.7 us (6%)
  between operations  15.4 us (3%)
    ppermute x74, waiting for transfers between devices, hop(): return lax.ppermute(value, 'narrow', [(i, i ^ bit) for i in range(PARTS)])  106 us
    ppermute x74, starting transfers between devices, hop(): return lax.ppermute(value, 'narrow', [(i, i ^ bit) for i in range(PARTS)])  58 us
    pallas_call x1, Pallas kernels, fast_device(): call(mlp_first, [shaped(size, many), shaped(many, width), shaped(many, wi...  36.9 us
    pallas_call x2, Pallas kernels, grad_of(): call(weight_grad, shaped(WIDE, size, cut), [], half_t + [right, right], p...  35.1 us
    pallas_call x2, Pallas kernels, half_of(): call(mlp_second, [shaped(3 * rest, many // 2), shaped(many // 2, rest)] +...  33 us
    unnamed x170, local copies, waits for them, and re-layouts  31.4 us
    ppermute x6, waiting for transfers between devices, over_wide(): lax.ppermute(value, 'wide', [(i, (i + step) % WIDE) for i in range(WIDE)])  19.6 us
    pallas_call x1, Pallas kernels, fast_device(): call(branch_back, [shaped(TOKENS, width, dtype=F32), shaped(TOKENS, HQ),...  12.1 us
  transfers between devices with their start and end apart: 85, of which 40 were waited for; matrix products, arithmetic and copies ran while one was open for 13% of the time, Pallas kernels for 38%

profile of v4, /device:TPU:0, one launch (start us, length us, event | category | flops | bytes accessed | tf_op | source)
XLA Modules:
  0.0 483.6 jit_solution(9314778655725578742)
XLA Ops:
  35.4 14.5 %collective-permute-done.6 = bf16[256,1536]{1,0:T(8,128)(2,1)} collective-permute-done((bf16[256,1536]{1,0:T(8,128)(2,1)S(1)}, bf16[256,1536]{1,0:T(8,128)(2,1)}, u32[]{:S(2)}, u32[]{:S(2)}) %collective-permute-start.6) | collective-permute-done | bytes 786464 | tf_op jit(solution)/shard_map/ppermute | solution.py:297
  73.6 12.6 %collective-permute-done.10.refs_5_ = bf16[384,1024]{1,0:T(8,128)(2,1)} collective-permute-done((bf16[384,1024]{1,0:T(8,128)(2,1)S(1)}, bf16[384,1024]{1,0:T(8,128)(2,1)}, u32[]{:S(2)}, u32[]{:S(2)}) %collective-permute-start.10) | collective-permute-done | bytes 786464 | tf_op jit(solution)/shard_map/ppermute | solution.py:297
  94.0 5.9 %project_kv.1 = (bf16[256,512]{1,0:T(8,128)(2,1)}, bf16[256,1536]{1,0:T(8,128)(2,1)}, f32[8,1536]{1,0:T(8,128)}, bf16[1536,640]{1,0:T(8,128)(2,1)}) custom-call(s32[32]{0:T(128)} %mul.70.starts.starts_a, bf16[256,1536]{1,0:T(8,128)(2,1)} %bitcast.106, f32[256,128]{1,0:T(8,128)} %pad_maximum_fusion.11.cosine, f32[256,128]{1,0:T(8,128)} %pad_maximum_fusion.12.sine, ...), custom_call_target="tpu_custom_call" | custom-call | flops 402653184 | bytes 4000000 | tf_op jit(solution)/shard_map/project_kv/pallas_call | solution.py:908
  113.1 7.3 %project_q.1 = (bf16[256,1536]{1,0:T(8,128)(2,1)}, bf16[1536,1536]{1,0:T(8,128)(2,1)}) custom-call(s32[32]{0:T(128)} %mul.70.starts.starts_a, s32[32]{0:T(128)} %mul.72.starts_b, bf16[256,1536]{1,0:T(8,128)(2,1)} %get-tuple-element.173.h_one, f32[8,1536]{1,0:T(8,128)} %get-tuple-element.174.vec, f32[256,128]{1,0:T(8,128)} %pad_maximum_fusion.11.cosine, ...), custom_call_target="tpu_custom_call" | custom-call | flops 1207959552 | bytes 7000000 | tf_op jit(solution)/shard_map/project_q/pallas_call | solution.py:927
  124.0 5.8 %attend.1 = (bf16[256,1536]{1,0:T(8,128)(2,1)S(1)}, f32[4,1,768]{2,1,0:T(1,128)S(1)}) custom-call(bf16[256,1536]{1,0:T(8,128)(2,1)S(1)} %copy-done.17, f32[2,1024,128]{2,1,0:T(8,128)S(1)} %or_select_fusion.barred, bf16[256,512]{1,0:T(8,128)(2,1)S(1)} %pad_maximum_fusion.9.refs_0_, bf16[256,512]{1,0:T(8,128)(2,1)S(1)} %collective-permute-done.19.refs_1_, ...), custom_call_target="tpu_custom_call" | custom-call | flops 1610612736 | bytes 4000000 | tf_op jit(solution)/shard_map/attend/pallas_call | solution.py:947
  134.7 8.1 %branch.1 = (f32[256,1536]{1,0:T(8,128)}, bf16[256,1536]{1,0:T(8,128)(2,1)}, bf16[1536,1536]{1,0:T(8,128)(2,1)}) custom-call(s32[32]{0:T(128)} %mul.70.starts.starts_a, s32[32]{0:T(128)} %mul.72.starts_b, bf16[256,1536]{1,0:T(8,128)(2,1)} %copy-done.5, bf16[256,1536]{1,0:T(8,128)(2,1)} %bitcast.107, f32[8,1536]{1,0:T(8,128)} %get-tuple-element.174.vec, ...), custom_call_target="tpu_custom_call" | custom-call | flops 1207959552 | bytes 8000000 | tf_op jit(solution)/shard_map/branch/pallas_call | solution.py:962
  149.6 5.8 %collective-permute-done.36 = bf16[128,1536]{1,0:T(8,128)(2,1)} collective-permute-done((bf16[128,1536]{1,0:T(8,128)(2,1)S(1)}, bf16[128,1536]{1,0:T(8,128)(2,1)}, u32[]{:S(2)}, u32[]{:S(2)}) %collective-permute-start.36) | collective-permute-done | bytes 393248 | tf_op jit(solution)/shard_map/ppermute | solution.py:297
  161.7 15.3 %collective-permute-done.38.refs_3_ = bf16[256,1536]{1,0:T(8,128)(2,1)S(1)} collective-permute-done((bf16[256,1536]{1,0:T(8,128)(2,1)S(1)}, bf16[256,1536]{1,0:T(8,128)(2,1)S(1)}, u32[]{:S(2)}, u32[]{:S(2)}) %collective-permute-start.38) | collective-permute-done | bytes 786464 | tf_op jit(solution)/shard_map/ppermute | solution.py:297
  182.5 36.9 %mlp_first.1 = (bf16[1920,2048]{1,0:T(8,128)(2,1)}, bf16[2048,1536]{1,0:T(8,128)(2,1)}, bf16[2048,1536]{1,0:T(8,128)(2,1)}, bf16[2048,1536]{1,0:T(8,128)(2,1)}) custom-call(bf16[2048,1536]{1,0:T(8,128)(2,1)} %constant_dynamic-update-slice_fusion.21.grad.right_grad, bf16[256,1536]{1,0:T(8,128)(2,1)} %copy-done.41, bf16[256,1536]{1,0:T(8,128)(2,1)} %copy-done.57, ...), custom_call_target="tpu_custom_call" | custom-call | flops 2013265920 | bytes 4000000 | tf_op jit(solution)/shard_map/mlp_first/pallas_call | solution.py:987
  219.4 19.2 %weight_grad.2 = bf16[4,1920,384]{2,1,0:T(8,128)(2,1)S(1)} custom-call(bf16[1920,2048]{1,0:T(8,128)(2,1)} %get-tuple-element.199.left_own.left_other, bf16[1920,2048]{1,0:T(8,128)(2,1)} %get-tuple-element.199.left_own.left_other, bf16[2048,1536]{1,0:T(8,128)(2,1)} %constant_dynamic-update-slice_fusion.21.grad.right_grad, ...), custom_call_target="tpu_custom_call" | custom-call | flops 1207959552 | bytes 2000000 | tf_op jit(solution)/shard_map/weight_grad/pallas_call | solution.py:1013
  241.4 5.2 %all-gather.8.cloned.1.call-done.weights = bf16[1440,1536]{1,0:T(8,128)(2,1)} async-done(((bf16[1440,384]{1,0:T(8,128)(2,1)}), bf16[1440,1536]{1,0:T(8,128)(2,1)}) %all-gather.8.cloned.1.call-update) | async-done | bytes 4423696 | tf_op jit(solution)/shard_map/all_gather | solution.py:978
  246.6 15.8 %mlp_second.2 = (bf16[1440,1024]{1,0:T(8,128)(2,1)S(1)}, bf16[1024,480]{1,0:T(8,128)(2,1)S(1)}, bf16[1024,1536]{1,0:T(8,128)(2,1)}) custom-call(bf16[2048,1536]{1,0:T(8,128)(2,1)} %constant_dynamic-update-slice_fusion.21.grad.right_grad, bf16[2048,1536]{1,0:T(8,128)(2,1)} %get-tuple-element.200.right_h.h, ...), custom_call_target="tpu_custom_call" | custom-call | flops 7549747200 | bytes 30000000 | tf_op jit(solution)/shard_map/mlp_second/pallas_call | solution.py:1049
  271.0 17.2 %mlp_second.3 = (bf16[1440,1024]{1,0:T(8,128)(2,1)}, bf16[1024,480]{1,0:T(8,128)(2,1)S(1)}, bf16[512,1536]{1,0:T(8,128)(2,1)}, bf16[256,1536]{1,0:T(8,128)(2,1)S(1)}, bf16[256,1536]{1,0:T(8,128)(2,1)S(1)}) custom-call(bf16[2048,1536]{1,0:T(8,128)(2,1)} %constant_dynamic-update-slice_fusion.21.grad.right_grad, ...), custom_call_target="tpu_custom_call" | custom-call | flops 7549747200 | bytes 30000000 | tf_op jit(solution)/shard_map/mlp_second/pallas_call | solution.py:1049
  294.0 15.9 %weight_grad.3 = bf16[4,1440,384]{2,1,0:T(8,128)(2,1)} custom-call(bf16[1440,1024]{1,0:T(8,128)(2,1)S(1)} %copy-done.32, bf16[1440,1024]{1,0:T(8,128)(2,1)S(1)} %copy-done.34, bf16[2048,1536]{1,0:T(8,128)(2,1)} %constant_dynamic-update-slice_fusion.21.grad.right_grad, bf16[2048,1536]{1,0:T(8,128)(2,1)} %get-tuple-element.200.right_h.h), custom_call_target="tpu_custom_call" | custom-call | flops 9059696640 | bytes 20000000 | tf_op jit(solution)/shard_map/weight_grad/pallas_call | solution.py:1013
  317.5 6.8 %mlp_down.3 = (bf16[512,1536]{1,0:T(8,128)(2,1)}, bf16[256,1536]{1,0:T(8,128)(2,1)}, bf16[256,1536]{1,0:T(8,128)(2,1)}) custom-call(bf16[1024,480]{1,0:T(8,128)(2,1)} %copy-done.11, bf16[1440,1536]{1,0:T(8,128)(2,1)} %all-gather.8.cloned.1.call-done.weights, bf16[2048,1536]{1,0:T(8,128)(2,1)} %get-tuple-element.206.refs_0_, ...), custom_call_target="tpu_custom_call" | custom-call | flops 1509949440 | bytes 10000000 | tf_op jit(solution)/shard_map/mlp_down/pallas_call | solution.py:1074
  325.9 12.1 %branch_back.1 = (f32[256,1536]{1,0:T(8,128)}, bf16[256,1536]{1,0:T(8,128)(2,1)}, f32[1,1536]{1,0:T(1,128)}, bf16[768,768]{1,0:T(8,128)(2,1)}, bf16[768,768]{1,0...) custom-call(s32[32]{0:T(128)} %mul.82.starts_a.starts, s32[32]{0:T(128)} %mul.84.starts_b, ...), custom_call_target="tpu_custom_call" | custom-call | flops 2415919104 | bytes 15000000 | tf_op jit(solution)/shard_map/branch_back/pallas_call | solution.py:1130
  344.5 5.6 %attend_back.2 = (bf16[128,1536]{1,0:T(8,128)(2,1)S(1)}, bf16[512,512]{1,0:T(8,128)(2,1)S(1)}, bf16[512,512]{1,0:T(8,128)(2,1)}) custom-call(bf16[256,1536]{1,0:T(8,128)(2,1)S(1)} %copy-done.18, bf16[256,1536]{1,0:T(8,128)(2,1)S(1)} %copy-done.19, f32[256,128]{1,0:T(8,128)S(1)} %copy-done.7, f32[256,128]{1,0:T(8,128)S(1)} %copy-done.6, ...), custom_call_target="tpu_custom_call" | custom-call | flops 2013265920 | bytes 5000000 | tf_op jit(solution)/shard_map/attend_back/pallas_call | solution.py:1149
  355.2 6.1 %attend_back.3 = (bf16[128,1536]{1,0:T(8,128)(2,1)S(1)}, bf16[512,512]{1,0:T(8,128)(2,1)S(1)}, bf16[512,512]{1,0:T(8,128)(2,1)}) custom-call(bf16[256,1536]{1,0:T(8,128)(2,1)S(1)} %copy-done.18, bf16[256,1536]{1,0:T(8,128)(2,1)S(1)} %copy-done.19, f32[256,128]{1,0:T(8,128)S(1)} %copy-done.7, f32[256,128]{1,0:T(8,128)S(1)} %copy-done.6, ...), custom_call_target="tpu_custom_call" | custom-call | flops 2013265920 | bytes 5000000 | tf_op jit(solution)/shard_map/attend_back/pallas_call | solution.py:1149
  365.2 10.3 %query_back.1 = (f32[256,1536]{1,0:T(8,128)}, f32[1,1536]{1,0:T(1,128)}, bf16[768,768]{1,0:T(8,128)(2,1)}, bf16[768,768]{1,0:T(8,128)(2,1)}, bf16[768,768]{1,0:T(8,128)(2,1)}, /*index=5*/bf16[768,768]{1,0:T(8,128)(2,1)}) custom-call(s32[32]{0:T(128)} %mul.82.starts_a.starts, s32[32]{0:T(128)} %mul.84.starts_b, bf16[128,1536]{1,0:T(8,128)(2,1)} %copy-done.35, ...), custom_call_target="tpu_custom_call" | custom-call | flops 2415919104 | bytes 12000000 | tf_op jit(solution)/shard_map/query_back/pallas_call | solution.py:1173
  391.1 5.9 %collective-permute-done.56.got_a = bf16[128,512]{1,0:T(8,128)(2,1)S(1)} collective-permute-done((bf16[128,512]{1,0:T(8,128)(2,1)S(1)}, bf16[128,512]{1,0:T(8,128)(2,1)S(1)}, u32[]{:S(2)}, u32[]{:S(2)}) %collective-permute-start.56) | collective-permute-done | bytes 131104 | tf_op jit(solution)/shard_map/ppermute | solution.py:297
  403.0 6.7 %kv_back.1 = (bf16[256,1536]{1,0:T(8,128)(2,1)}, bf16[768,640]{1,0:T(8,128)(2,1)S(1)}, bf16[768,640]{1,0:T(8,128)(2,1)S(1)}) custom-call(s32[32]{0:T(128)S(1)} %copy-done.16, bf16[128,512]{1,0:T(8,128)(2,1)S(1)} %get-tuple-element.260.keep_a, bf16[128,512]{1,0:T(8,128)(2,1)S(1)} %collective-permute-done.56.got_a, ...), custom_call_target="tpu_custom_call" | custom-call | flops 805306368 | bytes 10000000 | tf_op jit(solution)/shard_map/kv_back/pallas_call | solution.py:1195
  415.9 7.1 %collective-permute-done.61 = bf16[128,1536]{1,0:T(8,128)(2,1)S(1)} collective-permute-done((bf16[128,1536]{1,0:T(8,128)(2,1)S(1)}, bf16[128,1536]{1,0:T(8,128)(2,1)S(1)}, u32[]{:S(2)}, u32[]{:S(2)}) %collective-permute-start.61) | collective-permute-done | bytes 393248 | tf_op jit(solution)/shard_map/ppermute | solution.py:297
  441.7 5.4 %collective-permute-done.78 = bf16[48,1536]{1,0:T(8,128)(2,1)S(1)} collective-permute-done((bf16[48,1536]{1,0:T(8,128)(2,1)S(1)}, bf16[48,1536]{1,0:T(8,128)(2,1)S(1)}, u32[]{:S(2)}, u32[]{:S(2)}) %collective-permute-start.78) | collective-permute-done | bytes 147488 | tf_op jit(solution)/shard_map/ppermute | solution.py:328
  468.0 5.8 %collective-permute-done.75 = bf16[48,2176]{1,0:T(8,128)(2,1)S(1)} collective-permute-done((bf16[48,2176]{1,0:T(8,128)(2,1)S(1)}, bf16[48,2176]{1,0:T(8,128)(2,1)S(1)}, u32[]{:S(2)}, u32[]{:S(2)}) %collective-permute-start.75) | collective-permute-done | bytes 208928 | tf_op jit(solution)/shard_map/ppermute | solution.py:328
  (450 shorter events, 210.6 us)
Async XLA Ops:
  7.2 44.5 %all-gather.4.cloned.1.call-start = ((), (), s32[]{:S(2)}) async-start(), calls=%async_computation.2 | async-start | bytes 1781760 | tf_op jit(solution)/shard_map/all_gather | solution.py:853
  16.5 166.0 %all-gather.6.cloned.1.call-start = ((), (), s32[]{:S(2)}) async-start(), calls=%async_computation.3 | async-start | bytes 7372800 | tf_op jit(solution)/shard_map/all_gather | solution.py:889
  30.1 19.8 %collective-permute-start.6 = (bf16[256,1536]{1,0:T(8,128)(2,1)S(1)}, bf16[256,1536]{1,0:T(8,128)(2,1)}, u32[]{:S(2)}, u32[]{:S(2)}) collective-permute-start(bf16[256,1536]{1,0:T(8,128)(2,1)S(1)} %pad_maximum_fusion.5), channel_id=1, source_target_pairs={{0,2},{1,3},{2,0},{3,1},{4,6},{5,7},{6,4},{7,5},{8,10},{9,11},{10,... | collective-permute-start | bytes 2359304 | tf_op jit(solution)/shard_map/ppermute | solution.py:297
  30.6 19.5 %collective-permute-start.5 = (bf16[256,1536]{1,0:T(8,128)(2,1)S(1)}, bf16[256,1536]{1,0:T(8,128)(2,1)}, u32[]{:S(2)}, u32[]{:S(2)}) collective-permute-start(bf16[256,1536]{1,0:T(8,128)(2,1)S(1)} %pad_maximum_fusion.4), channel_id=1, source_target_pairs={{0,4},{1,5},{2,6},{3,7},{4,0},{5,1},{6,2},{7,3},{8,12},{9,13},{10,... | collective-permute-start | bytes 2359304 | tf_op jit(solution)/shard_map/ppermute | solution.py:297
  51.7 194.9 %all-gather.8.cloned.1.call-start = ((), (), s32[]{:S(2)}) async-start(), calls=%async_computation.4 | async-start | bytes 5529600 | tf_op jit(solution)/shard_map/all_gather | solution.py:978
  69.3 20.2 %collective-permute-start.9 = (bf16[384,1152]{1,0:T(8,128)(2,1)S(1)}, bf16[384,1152]{1,0:T(8,128)(2,1)S(1)}, u32[]{:S(2)}, u32[]{:S(2)}) collective-permute-start(bf16[384,1152]{1,0:T(8,128)(2,1)S(1)} %pad_maximum_fusion.2.refs_0_), channel_id=1, source_target_pairs={{0,4},{1,5},{2,6},{3,7},{4,0},{5,1},{6,2},{7,3},{8,12},{9,13},{10,... | collective-permute-start | bytes 2654216 | tf_op jit(solution)/shard_map/ppermute | solution.py:297
  70.7 22.4 %collective-permute-start.15 = (bf16[384,1152]{1,0:T(8,128)(2,1)S(1)}, bf16[384,1152]{1,0:T(8,128)(2,1)}, u32[]{:S(2)}, u32[]{:S(2)}) collective-permute-start(bf16[384,1152]{1,0:T(8,128)(2,1)S(1)} %pad_maximum_fusion.2.refs_0_), channel_id=1, source_target_pairs={{0,1},{1,0},{2,3},{3,2},{4,5},{5,4},{6,7},{7,6},{8,9},{9,8},{10,11... | collective-permute-start | bytes 2654216 | tf_op jit(solution)/shard_map/ppermute | solution.py:297
  91.4 19.4 %collective-permute-start.21 = (bf16[384,1024]{1,0:T(8,128)(2,1)}, bf16[384,1024]{1,0:T(8,128)(2,1)}, u32[]{:S(2)}, u32[]{:S(2)}) collective-permute-start(bf16[384,1024]{1,0:T(8,128)(2,1)} %copy-done.43), channel_id=1, source_target_pairs={{0,1},{1,0},{2,3},{3,2},{4,5},{5,4},{6,7},{7,6},{8,9},{9,8},{10,11... | collective-permute-start | bytes 2359304 | tf_op jit(solution)/shard_map/ppermute | solution.py:297
  110.8 20.0 %collective-permute-start.30 = (bf16[384,768]{1,0:T(8,128)(2,1)}, bf16[384,768]{1,0:T(8,128)(2,1)}, u32[]{:S(2)}, u32[]{:S(2)}) collective-permute-start(bf16[384,768]{1,0:T(8,128)(2,1)} %constant_dynamic-update-slice_fusion.33.refs_4_), channel_id=1, source_target_pairs={{0,2},{1,3},{2,0},{3,1},{4,6},{5,7},{6,4},{7,5},{8,10},{9,11},{10,... | collective-permute-start | bytes 1769480 | tf_op jit(solution)/shard_map/ppermute | solution.py:297
  111.3 19.5 %collective-permute-start.29 = (bf16[384,768]{1,0:T(8,128)(2,1)}, bf16[384,768]{1,0:T(8,128)(2,1)}, u32[]{:S(2)}, u32[]{:S(2)}) collective-permute-start(bf16[384,768]{1,0:T(8,128)(2,1)} %constant_dynamic-update-slice_fusion.31.refs_0_), channel_id=1, source_target_pairs={{0,4},{1,5},{2,6},{3,7},{4,0},{5,1},{6,2},{7,3},{8,12},{9,13},{10,... | collective-permute-start | bytes 1769480 | tf_op jit(solution)/shard_map/ppermute | solution.py:297
  155.9 207.4 %reduce-scatter.3.cloned.1.call-start = ((), (), s32[]{:S(2)}) async-start(), calls=%async_computation.5 | async-start | bytes 7372800 | tf_op jit(solution)/shard_map/reduce_scatter | solution.py:1027
  241.2 213.3 %reduce-scatter.5.cloned.1.call-start = ((), (), s32[]{:S(2)}) async-start(), calls=%async_computation.6 | async-start | bytes 5529600 | tf_op jit(solution)/shard_map/reduce_scatter | solution.py:1027
  270.2 47.3 %collective-permute-start.46 = (bf16[1024,1536]{1,0:T(8,128)(2,1)}, bf16[1024,1536]{1,0:T(8,128)(2,1)}, u32[]{:S(2)}, u32[]{:S(2)}) collective-permute-start(bf16[1024,1536]{1,0:T(8,128)(2,1)} %mlp_down.2), channel_id=1, source_target_pairs={{0,1},{1,0},{2,3},{3,2},{4,5},{5,4},{6,7},{7,6},{8,9},{9,8},{10,11... | collective-permute-start | bytes 9437192 | tf_op jit(solution)/shard_map/ppermute | solution.py:297
  289.2 20.7 %collective-permute-start.44 = (bf16[256,1536]{1,0:T(8,128)(2,1)S(1)}, bf16[256,1536]{1,0:T(8,128)(2,1)}, u32[]{:S(2)}, u32[]{:S(2)}) collective-permute-start(bf16[256,1536]{1,0:T(8,128)(2,1)S(1)} %get-tuple-element.212), channel_id=1, source_target_pairs={{0,4},{1,5},{2,6},{3,7},{4,0},{5,1},{6,2},{7,3},{8,12},{9,13},{10,... | collective-permute-start | bytes 2359304 | tf_op jit(solution)/shard_map/ppermute | solution.py:297
  290.7 19.5 %collective-permute-start.45 = (bf16[256,1536]{1,0:T(8,128)(2,1)S(1)}, bf16[256,1536]{1,0:T(8,128)(2,1)}, u32[]{:S(2)}, u32[]{:S(2)}) collective-permute-start(bf16[256,1536]{1,0:T(8,128)(2,1)S(1)} %get-tuple-element.213), channel_id=1, source_target_pairs={{0,2},{1,3},{2,0},{3,1},{4,6},{5,7},{6,4},{7,5},{8,10},{9,11},{10,... | collective-permute-start | bytes 2359304 | tf_op jit(solution)/shard_map/ppermute | solution.py:297
  338.8 36.8 %collective-permute-start.49 = (bf16[256,1536]{1,0:T(8,128)(2,1)}, bf16[256,1536]{1,0:T(8,128)(2,1)}, u32[]{:S(2)}, u32[]{:S(2)}) collective-permute-start(bf16[256,1536]{1,0:T(8,128)(2,1)} %get-tuple-element.224), channel_id=1, source_target_pairs={{0,4},{1,5},{2,6},{3,7},{4,0},{5,1},{6,2},{7,3},{8,12},{9,13},{10,... | collective-permute-start | bytes 2359304 | tf_op jit(solution)/shard_map/ppermute | solution.py:297
  340.2 35.4 %collective-permute-start.50 = (bf16[256,1536]{1,0:T(8,128)(2,1)}, bf16[256,1536]{1,0:T(8,128)(2,1)}, u32[]{:S(2)}, u32[]{:S(2)}) collective-permute-start(bf16[256,1536]{1,0:T(8,128)(2,1)} %get-tuple-element.225), channel_id=1, source_target_pairs={{0,2},{1,3},{2,0},{3,1},{4,6},{5,7},{6,4},{7,5},{8,10},{9,11},{10,... | collective-permute-start | bytes 2359304 | tf_op jit(solution)/shard_map/ppermute | solution.py:297
  353.0 23.1 %collective-permute-start.64 = (bf16[384,768]{1,0:T(8,128)(2,1)}, bf16[384,768]{1,0:T(8,128)(2,1)}, u32[]{:S(2)}, u32[]{:S(2)}) collective-permute-start(bf16[384,768]{1,0:T(8,128)(2,1)} %get-tuple-element.316), channel_id=1, source_target_pairs={{0,4},{1,5},{2,6},{3,7},{4,0},{5,1},{6,2},{7,3},{8,12},{9,13},{10,... | collective-permute-start | bytes 1769480 | tf_op jit(solution)/shard_map/ppermute | solution.py:297
  362.0 20.2 %collective-permute-start.54 = (bf16[512,512]{1,0:T(8,128)(2,1)}, bf16[512,512]{1,0:T(8,128)(2,1)}, u32[]{:S(2)}, u32[]{:S(2)}) collective-permute-start(bf16[512,512]{1,0:T(8,128)(2,1)} %get-tuple-element.258), channel_id=1, source_target_pairs={{0,1},{1,0},{2,3},{3,2},{4,5},{5,4},{6,7},{7,6},{8,9},{9,8},{10,11... | collective-permute-start | bytes 1572872 | tf_op jit(solution)/shard_map/ppermute | solution.py:297
  375.6 21.4 %collective-permute-start.57 = (bf16[768,768]{1,0:T(8,128)(2,1)}, bf16[768,768]{1,0:T(8,128)(2,1)S(1)}, u32[]{:S(2)}, u32[]{:S(2)}) collective-permute-start(bf16[768,768]{1,0:T(8,128)(2,1)} %get-tuple-element.264), channel_id=1, source_target_pairs={{0,1},{1,0},{2,3},{3,2},{4,5},{5,4},{6,7},{7,6},{8,9},{9,8},{10,11... | collective-permute-start | bytes 3538952 | tf_op jit(solution)/shard_map/ppermute | solution.py:297
  375.6 21.7 %collective-permute-start.58 = (bf16[768,768]{1,0:T(8,128)(2,1)}, bf16[768,768]{1,0:T(8,128)(2,1)S(1)}, u32[]{:S(2)}, u32[]{:S(2)}) collective-permute-start(bf16[768,768]{1,0:T(8,128)(2,1)} %get-tuple-element.266), channel_id=1, source_target_pairs={{0,1},{1,0},{2,3},{3,2},{4,5},{5,4},{6,7},{7,6},{8,9},{9,8},{10,11... | collective-permute-start | bytes 3538952 | tf_op jit(solution)/shard_map/ppermute | solution.py:297
  414.1 20.0 %collective-permute-start.68 = (bf16[384,768]{1,0:T(8,128)(2,1)S(1)}, bf16[384,768]{1,0:T(8,128)(2,1)S(1)}, u32[]{:S(2)}, u32[]{:S(2)}) collective-permute-start(bf16[384,768]{1,0:T(8,128)(2,1)S(1)} %get-tuple-element.312), channel_id=1, source_target_pairs={{0,4},{1,5},{2,6},{3,7},{4,0},{5,1},{6,2},{7,3},{8,12},{9,13},{10,... | collective-permute-start | bytes 1769480 | tf_op jit(solution)/shard_map/ppermute | solution.py:297
  414.7 21.1 %collective-permute-start.69 = (bf16[384,768]{1,0:T(8,128)(2,1)S(1)}, bf16[384,768]{1,0:T(8,128)(2,1)S(1)}, u32[]{:S(2)}, u32[]{:S(2)}) collective-permute-start(bf16[384,768]{1,0:T(8,128)(2,1)S(1)} %get-tuple-element.310), channel_id=1, source_target_pairs={{0,2},{1,3},{2,0},{3,1},{4,6},{5,7},{6,4},{7,5},{8,10},{9,11},{10,... | collective-permute-start | bytes 1769480 | tf_op jit(solution)/shard_map/ppermute | solution.py:297
  428.1 19.0 %collective-permute-start.78 = (bf16[48,1536]{1,0:T(8,128)(2,1)S(1)}, bf16[48,1536]{1,0:T(8,128)(2,1)S(1)}, u32[]{:S(2)}, u32[]{:S(2)}) collective-permute-start(bf16[48,1536]{1,0:T(8,128)(2,1)S(1)} %get-tuple-element.340), channel_id=1, source_target_pairs={{0,16},{8,24},{16,0},{24,8},{1,17},{9,25},{17,1},{25,9},{2,18},{10... | collective-permute-start | bytes 442376 | tf_op jit(solution)/shard_map/ppermute | solution.py:328
  (135 other events, 1102.6 us)
Sparse Core Ops, SparseCore 0:
  16.7 34.9 all-gather.3
  53.9 107.7 all-gather.5
  163.8 82.7 all-gather.7
  248.8 102.9 reduce-scatter.2
  354.0 88.0 reduce-scatter.4

commit v5 on v4

--- a/solution.py
+++ b/solution.py
@@ -431,7 +431,7 @@
     return value * cosine + pltpu.roll(value, HEAD // 2, 1) * sine
 
 
-def project_kv(starts, x, cosine, sine, pick_k, pick_v, *refs):
+def project_kv(starts, x, trig, picks, *refs):
     pieces, (kv_out, h_out, vec_out, whole, held, sems, out_sem) = refs[:4], refs[4:]
     copies = weight_copies(pieces, held, starts, sems, slice(0, KV_COLUMNS), slice(None))
     for copy in copies:
@@ -445,20 +445,20 @@
     vec = held[:, 2 * HK :].astype(F32).T[:8, :]
     vec_out[...] = vec
     low = vec.astype(BF16)
-    b_key = dot_nn(low, pick_k[...])[3:4, :]
-    b_value = dot_nn(low, pick_v[...])[3:4, :]
+    b_key = dot_nn(low, picks[:, :HK])[3:4, :]
+    b_value = dot_nn(low, picks[:, HK:])[3:4, :]
     h_one = (unit * vec[0:1, :]).astype(BF16)
     h_out[...] = h_one
     lin = dot_nn(h_one, held[:, : 2 * HK])
     for head in range(KV_HEADS):
         cut = slice(head * HEAD, (head + 1) * HEAD)
-        key = turn(lin[:, cut] + b_key[:, cut], cosine[...], sine[...])
+        key = turn(lin[:, cut] + b_key[:, cut], trig[:, :HEAD], trig[:, HEAD:])
         kv_out[:, cut] = key.astype(BF16)
     kv_out[:, HK:] = (lin[:, HK:] + b_value).astype(BF16)
     over.wait()
 
 
-def project_q(starts_a, starts_b, h_one, vec, cosine, sine, *refs):
+def project_q(starts_a, starts_b, h_one, vec, trig, *refs):
     pieces, (q_out, whole, held, sems, out_sem) = refs[:8], refs[8:]
     copies = query_copies(pieces, held, starts_a, starts_b, sems)
     for copy in copies:
@@ -470,7 +470,7 @@
     lin = dot_nn(h_one[...], held[...]) + vec[2:3, :]
     for head in range(Q_HEADS):
         cut = slice(head * HEAD, (head + 1) * HEAD)
-        q_out[:, cut] = turn(lin[:, cut], cosine[...], sine[...]).astype(BF16)
+        q_out[:, cut] = turn(lin[:, cut], trig[:, :HEAD], trig[:, HEAD:]).astype(BF16)
     over.wait()
 
 
@@ -702,7 +702,7 @@
         out_copy.wait()
 
 
-def attend_back(row, q, d_att, cosine, sine, barred, lse, *refs):
+def attend_back(row, q, d_att, trig, barred, lse, *refs):
     kv, (dq_out, own, other) = refs[:4], refs[4:]
     bar = jnp.concatenate([barred[row]] * GROUP, axis=1)
     at = slice(row * SEG, (row + 1) * SEG)
@@ -728,7 +728,7 @@
         d_query = dot_nn(flipped(keys), d_score)
         for g in range(GROUP):
             head = kv_head * GROUP + g
-            back = turn(d_query[:, g * SEG : (g + 1) * SEG].T, cosine[at, :], -sine[at, :])
+            back = turn(d_query[:, g * SEG : (g + 1) * SEG].T, trig[at, :HEAD], -trig[at, HEAD:])
             dq_out[:, head * HEAD : (head + 1) * HEAD] = back.astype(BF16)
 
 
@@ -750,8 +750,8 @@
 
 
 def kv_back(
-    starts, keep_a, got_a, keep_b, got_b, x, h_one, vec, cosine, sine, d_h_q, d_mid, d_gain, d_bias,
-    pick_k, pick_v, weight, *refs,
+    starts, keep_a, got_a, keep_b, got_b, x, h_one, vec, trig, d_h_q, d_mid, d_gain, d_bias,
+    picks, weight, *refs,
 ):
     grad_out, own, other, held_d, out_sems = refs
     d_kv = jnp.concatenate(
@@ -762,7 +762,7 @@
         axis=0,
     )
     parts = [
-        turn(d_kv[:, head * HEAD : (head + 1) * HEAD], cosine[...], -sine[...])
+        turn(d_kv[:, head * HEAD : (head + 1) * HEAD], trig[:, :HEAD], -trig[:, HEAD:])
         for head in range(KV_HEADS)
     ]
     d_lin = jnp.concatenate(parts + [d_kv[:, HK:]], axis=1).astype(BF16)
@@ -777,7 +777,7 @@
             jnp.sum(d_h * unit, axis=0, keepdims=True),
             d_gain[...],
             d_bias[...],
-            dot_nt(d_small[:, :HK], pick_k[...]) + dot_nt(d_small[:, HK:], pick_v[...]),
+            dot_nt(d_small[:, :HK], picks[:, :HK]) + dot_nt(d_small[:, HK:], picks[:, HK:]),
             jnp.zeros((124, HQ), F32),
         ],
         axis=0,
@@ -837,7 +837,7 @@
     pick_v = ((in_block >= small) & (in_block < 2 * small))[:, None] & (
         (head_lane - small)[:, None] == np.arange(HK)
     )
-    pick_k, pick_v = jnp.asarray(pick_k, BF16), jnp.asarray(pick_v, BF16)
+    picks = jnp.asarray(np.concatenate([pick_k, pick_v], axis=1), BF16)
 
     half = HQ // 2
     rows = range(ROWS)
@@ -850,6 +850,7 @@
     )
     vectors = jnp.pad(vectors, ((0, 0), (0, 124)))
     own = jnp.concatenate([w_key, w_value, vectors, w_query, w_out], axis=1)
+    own, (seg_ids, pad_mask) = tie(own, (seg_ids, pad_mask))
     w_rows = lax.all_gather(own, "wide", axis=0, tiled=True)
     parts = [(0, split), (split, units)]
     own_parts = [
@@ -877,14 +878,13 @@
     own_idx = me * SEG + jnp.arange(SEG, dtype=jnp.int32)
     begins = jnp.sum((ids_all[:, None, :] < seg_ids[:, :, None]).astype(jnp.int32), axis=-1)
     cosine, sine = angles((own_idx[None, :] - begins).reshape(TOKENS), HEAD)
-    cosine = jnp.concatenate([cosine, cosine], axis=-1)
-    sine = jnp.concatenate([-sine, sine], axis=-1)
+    trig = jnp.concatenate([cosine, cosine, -sine, sine], axis=-1)
     allowed = (ids_all[:, :, None] == seg_ids[:, None, :]) & (
         key_idx[:, :, None] < own_idx[None, None, :]
     ) & (pads_all[:, :, None] == 1) | (key_idx[:, :, None] == own_idx[None, None, :])
     barred = jnp.where(allowed, 0.0, -1e30).astype(F32)
 
-    w_rows, (cosine, sine, barred, grad_far) = tie(w_rows, (cosine, sine, barred, grad_far))
+    w_rows, (trig, barred, grad_far) = tie(w_rows, (trig, barred, grad_far))
     w_rows, own_parts[0] = tie(w_rows, own_parts[0])
     weights = [lax.all_gather(own_parts[0], "wide", axis=1, tiled=True)]
     bounds = (0, FIRST, KV_COLUMNS + HQ, KV_COLUMNS + HQ + half, KV_COLUMNS + HQ + width)
@@ -914,13 +914,13 @@
             shaped(width, KV_COLUMNS),
         ],
         [pltpu.VMEM((width, KV_COLUMNS), BF16), dma((32,)), dma],
-        in_smem(1) + in_vmem(5) + in_hbm(4),
+        in_smem(1) + in_vmem(3) + in_hbm(4),
         in_vmem(3) + in_hbm(1),
         2 * TOKENS * width * 2 * HK,
         4e6,
         60,
         name="project_kv",
-    )(starts[0], x, cosine, sine, pick_k, pick_v, *w_pieces[0])
+    )(starts[0], x, trig, picks, *w_pieces[0])
     kv_own = [kv[at_row[r]] for r in rows]
     kv_one = [links.first(kv_own[r], order[r]) for r in rows]
     kv_one = together(kv_one)
@@ -928,13 +928,13 @@
         project_q,
         [shaped(TOKENS, HQ), shaped(width, HQ)],
         [pltpu.VMEM((width, HQ), BF16), dma((2, 32)), dma],
-        in_smem(2) + in_vmem(4) + in_hbm(8),
+        in_smem(2) + in_vmem(3) + in_hbm(8),
         in_vmem(1) + in_hbm(1),
         2 * TOKENS * width * HQ,
         7e6,
         60,
         name="project_q",
-    )(*starts, h_one, vec, cosine, sine, *w_pieces[0], *w_pieces[1])
+    )(*starts, h_one, vec, trig, *w_pieces[0], *w_pieces[1])
     kv_near = [jnp.concatenate([kv_own[r], kv_one[r]], axis=0) for r in rows]
     kv_far = [links.second(kv_near[r], order[r]) for r in rows]
     kv_far = together(kv_far)
@@ -1018,7 +1018,7 @@
             pl.BlockSpec((2, block, cut), lambda k, m: (k, m, 0)),
             (2.0 if place == 0 else 0.2) * many * width * size,
             2e7 if place == 0 else 2e6,
-            48,
+            60,
             grid=(WIDE // 2, 3),
             name="weight_grad",
         )(left_own, left_other, grad_all, h_all)
@@ -1062,7 +1062,7 @@
             + specs,
             5 * many * width * rest,
             3e7,
-            50,
+            60,
             grid=(tiles,),
             name="mlp_second",
         )(grad_all, h_all, weights[1], d_h, *got)
@@ -1150,13 +1150,13 @@
             functools.partial(attend_back, row),
             [shaped(SEG, HQ)] + [shaped(ROW_LEN // 2, 2 * HK)] * 2,
             [],
-            in_vmem(6) + in_vmem(4),
+            in_vmem(5) + in_vmem(4),
             in_vmem(3),
             5 * TOKENS * ROW_LEN * HQ,
             5e6,
             48,
             name="attend_back",
-        )(q, d_att, cosine, sine, barred, lse, *kv_rows[4 * row : 4 * row + 4])
+        )(q, d_att, trig, barred, lse, *kv_rows[4 * row : 4 * row + 4])
 
     dq_a, own_a, other_a = back_of(0, d_att)
     got_a = links.core(other_a)
@@ -1196,20 +1196,21 @@
         kv_back,
         [shaped(TOKENS, width)] + [shaped(16 * SHARE, KV_COLUMNS)] * 2,
         [pltpu.VMEM((width, KV_COLUMNS), BF16), dma((32,))],
-        in_smem(1) + in_vmem(16),
+        in_smem(1) + in_vmem(14),
         in_vmem(1) + in_hbm(2),
         4 * TOKENS * width * 2 * HK,
         1e7,
         24,
         name="kv_back",
     )(
-        ends[0], *d_kv, x, h_one, vec, cosine, sine, d_h_q, d_mid, d_gain, d_bias,
-        pick_k, pick_v, w_kv,
+        ends[0], *d_kv, x, h_one, vec, trig, d_h_q, d_mid, d_gain, d_bias,
+        picks, w_kv,
     )
     got_w = links.core(other_w)
     keep_o, d_h_q = tie(keep_o, d_h_q)
     sum_o = last_sums([k + g for k, g in keep_o])
     got_w, sum_o = tie(got_w, sum_o)
+    got_w, keep_q = tie(got_w, keep_q)
     got_m, own_w = tie(got_m, own_w)
     mixed = first_rows(added(by_row(keep_m), got_m))
     keep_w, got_w = links.scatter_second(own_w + got_w, 0)

time: 488 us -> 487 us (level)
  waiting for transfers between devices: 133 us -> 140 us
  local copies, waits for them, and re-layouts: 56.1 us -> 49.2 us
    unnamed x170 -> x156, local copies, waits for them, and re-layouts: 31.4 us -> 24.5 us
  transfers between devices with their start and end apart: 85 -> 85, of which waited for: 40 -> 39; matrix products, arithmetic and copies ran while one was open for 13% -> 12% of each run, Pallas kernels for 38% -> 39%
where the time goes in v5:
time: 487 us; the launch traced here: 482 us
  Pallas kernels  188 us (39%)
  waiting for transfers between devices  140 us (29%)
  starting transfers between devices  61.2 us (13%)
  local copies, waits for them, and re-layouts  49.2 us (10%)
  other arithmetic  29.2 us (6%)
  between operations  15.3 us (3%)
    ppermute x74, waiting for transfers between devices, hop(): return lax.ppermute(value, 'narrow', [(i, i ^ bit) for i in range(PARTS)])  110 us
    ppermute x74, starting transfers between devices, hop(): return lax.ppermute(value, 'narrow', [(i, i ^ bit) for i in range(PARTS)])  54.7 us
    pallas_call x2, Pallas kernels, grad_of(): call(weight_grad, shaped(WIDE, size, cut), [], half_t + [right, right], p...  37.2 us
    pallas_call x1, Pallas kernels, fast_device(): call(mlp_first, [shaped(size, many), shaped(many, width), shaped(many, wi...  36.9 us
    pallas_call x2, Pallas kernels, half_of(): call(mlp_second, [shaped(3 * rest, many // 2), shaped(many // 2, rest)] +...  33.7 us
    unnamed x156, local copies, waits for them, and re-layouts  24.5 us
    ppermute x6, waiting for transfers between devices, over_wide(): lax.ppermute(value, 'wide', [(i, (i + step) % WIDE) for i in range(WIDE)])  22.4 us
    pallas_call x2, Pallas kernels, down_of(): call(mlp_down, shapes, [], [pl.BlockSpec((TILE, rest), lambda t: (t, 0)),...  12.1 us
  transfers between devices with their start and end apart: 85, of which 39 were waited for; matrix products, arithmetic and copies ran while one was open for 12% of the time, Pallas kernels for 39%

profile of v5, /device:TPU:0, one launch (start us, length us, event | category | flops | bytes accessed | tf_op | source)
XLA Modules:
  0.0 482.5 jit_solution(3878374061614500205)
XLA Ops:
  34.7 15.2 %collective-permute-done.6 = bf16[256,1536]{1,0:T(8,128)(2,1)} collective-permute-done((bf16[256,1536]{1,0:T(8,128)(2,1)S(1)}, bf16[256,1536]{1,0:T(8,128)(2,1)}, u32[]{:S(2)}, u32[]{:S(2)}) %collective-permute-start.6) | collective-permute-done | bytes 786464 | tf_op jit(solution)/shard_map/ppermute | solution.py:297
  72.4 12.6 %collective-permute-done.10.refs_5_ = bf16[384,1024]{1,0:T(8,128)(2,1)} collective-permute-done((bf16[384,1024]{1,0:T(8,128)(2,1)S(1)}, bf16[384,1024]{1,0:T(8,128)(2,1)}, u32[]{:S(2)}, u32[]{:S(2)}) %collective-permute-start.10) | collective-permute-done | bytes 786464 | tf_op jit(solution)/shard_map/ppermute | solution.py:297
  92.8 5.8 %project_kv.1 = (bf16[256,512]{1,0:T(8,128)(2,1)}, bf16[256,1536]{1,0:T(8,128)(2,1)}, f32[8,1536]{1,0:T(8,128)}, bf16[1536,640]{1,0:T(8,128)(2,1)}) custom-call(s32[32]{0:T(128)} %mul.70.starts.starts_a, bf16[256,1536]{1,0:T(8,128)(2,1)} %bitcast.106, f32[256,256]{1,0:T(8,128)} %pad_maximum_fusion.9.trig, bf16[1536,512]{1,0:T(8,128)(2,1)} %constant.54.clone.picks, ...), custom_call_target="tpu_custom_call" | custom-call | flops 402653184 | bytes 4000000 | tf_op jit(solution)/shard_map/project_kv/pallas_call | solution.py:908
  111.9 7.3 %project_q.1 = (bf16[256,1536]{1,0:T(8,128)(2,1)}, bf16[1536,1536]{1,0:T(8,128)(2,1)}) custom-call(s32[32]{0:T(128)} %mul.70.starts.starts_a, s32[32]{0:T(128)} %mul.72.starts_b, bf16[256,1536]{1,0:T(8,128)(2,1)} %get-tuple-element.182.h_one, f32[8,1536]{1,0:T(8,128)} %get-tuple-element.183.vec, f32[256,256]{1,0:T(8,128)} %pad_maximum_fusion.9.trig, ...), custom_call_target="tpu_custom_call" | custom-call | flops 1207959552 | bytes 7000000 | tf_op jit(solution)/shard_map/project_q/pallas_call | solution.py:927
  122.7 5.8 %attend.1 = (bf16[256,1536]{1,0:T(8,128)(2,1)S(1)}, f32[4,1,768]{2,1,0:T(1,128)S(1)}) custom-call(bf16[256,1536]{1,0:T(8,128)(2,1)S(1)} %copy-done.12, f32[2,1024,128]{2,1,0:T(8,128)S(1)} %or_select_fusion.barred, bf16[256,512]{1,0:T(8,128)(2,1)S(1)} %pad_maximum_fusion.10.refs_0_, bf16[256,512]{1,0:T(8,128)(2,1)S(1)} %collective-permute-done.19.refs_1_, ...), custom_call_target="tpu_custom_call" | custom-call | flops 1610612736 | bytes 4000000 | tf_op jit(solution)/shard_map/attend/pallas_call | solution.py:947
  133.4 8.0 %branch.1 = (f32[256,1536]{1,0:T(8,128)}, bf16[256,1536]{1,0:T(8,128)(2,1)}, bf16[1536,1536]{1,0:T(8,128)(2,1)}) custom-call(s32[32]{0:T(128)} %mul.70.starts.starts_a, s32[32]{0:T(128)} %mul.72.starts_b, bf16[256,1536]{1,0:T(8,128)(2,1)} %copy-done.4, bf16[256,1536]{1,0:T(8,128)(2,1)} %bitcast.107, f32[8,1536]{1,0:T(8,128)} %get-tuple-element.183.vec, ...), custom_call_target="tpu_custom_call" | custom-call | flops 1207959552 | bytes 8000000 | tf_op jit(solution)/shard_map/branch/pallas_call | solution.py:962
  148.2 5.8 %collective-permute-done.36 = bf16[128,1536]{1,0:T(8,128)(2,1)} collective-permute-done((bf16[128,1536]{1,0:T(8,128)(2,1)S(1)}, bf16[128,1536]{1,0:T(8,128)(2,1)}, u32[]{:S(2)}, u32[]{:S(2)}) %collective-permute-start.36) | collective-permute-done | bytes 393248 | tf_op jit(solution)/shard_map/ppermute | solution.py:297
  160.4 15.3 %collective-permute-done.38.refs_3_ = bf16[256,1536]{1,0:T(8,128)(2,1)S(1)} collective-permute-done((bf16[256,1536]{1,0:T(8,128)(2,1)S(1)}, bf16[256,1536]{1,0:T(8,128)(2,1)S(1)}, u32[]{:S(2)}, u32[]{:S(2)}) %collective-permute-start.38) | collective-permute-done | bytes 786464 | tf_op jit(solution)/shard_map/ppermute | solution.py:297
  181.1 36.9 %mlp_first.1 = (bf16[1920,2048]{1,0:T(8,128)(2,1)}, bf16[2048,1536]{1,0:T(8,128)(2,1)}, bf16[2048,1536]{1,0:T(8,128)(2,1)}, bf16[2048,1536]{1,0:T(8,128)(2,1)}) custom-call(bf16[2048,1536]{1,0:T(8,128)(2,1)} %constant_dynamic-update-slice_fusion.21.grad.right_grad, bf16[256,1536]{1,0:T(8,128)(2,1)} %copy-done.33, bf16[256,1536]{1,0:T(8,128)(2,1)} %copy-done.49, ...), custom_call_target="tpu_custom_call" | custom-call | flops 2013265920 | bytes 4000000 | tf_op jit(solution)/shard_map/mlp_first/pallas_call | solution.py:987
  218.0 20.2 %weight_grad.2 = bf16[4,1920,384]{2,1,0:T(8,128)(2,1)} custom-call(bf16[1920,2048]{1,0:T(8,128)(2,1)} %get-tuple-element.208.left_own.left_other, bf16[1920,2048]{1,0:T(8,128)(2,1)} %get-tuple-element.208.left_own.left_other, bf16[2048,1536]{1,0:T(8,128)(2,1)} %constant_dynamic-update-slice_fusion.21.grad.right_grad, ...), custom_call_target="tpu_custom_call" | custom-call | flops 1207959552 | bytes 2000000 | tf_op jit(solution)/shard_map/weight_grad/pallas_call | solution.py:1013
  238.5 7.1 %all-gather.8.cloned.1.call-done.weights = bf16[1440,1536]{1,0:T(8,128)(2,1)} async-done(((bf16[1440,384]{1,0:T(8,128)(2,1)}), bf16[1440,1536]{1,0:T(8,128)(2,1)}) %all-gather.8.cloned.1.call-update) | async-done | bytes 4423696 | tf_op jit(solution)/shard_map/all_gather | solution.py:978
  245.6 15.8 %mlp_second.2 = (bf16[1440,1024]{1,0:T(8,128)(2,1)}, bf16[1024,480]{1,0:T(8,128)(2,1)}, bf16[1024,1536]{1,0:T(8,128)(2,1)}) custom-call(bf16[2048,1536]{1,0:T(8,128)(2,1)} %constant_dynamic-update-slice_fusion.21.grad.right_grad, bf16[2048,1536]{1,0:T(8,128)(2,1)} %get-tuple-element.209.right_h.h, bf16[1440,1536]{1,0:T(8,128)(2,1)} %all-gather.8.cloned.1.call-done.weights, ...), custom_call_target="tpu_custom_call" | custom-call | flops 7549747200 | bytes 30000000 | tf_op jit(solution)/shard_map/mlp_second/pallas_call | solution.py:1049
  267.5 17.9 %mlp_second.3 = (bf16[1440,1024]{1,0:T(8,128)(2,1)}, bf16[1024,480]{1,0:T(8,128)(2,1)}, bf16[512,1536]{1,0:T(8,128)(2,1)}, bf16[256,1536]{1,0:T(8,128)(2,1)}, bf16[256,1536]{1,0:T(8,128)(2,1)}) custom-call(bf16[2048,1536]{1,0:T(8,128)(2,1)} %constant_dynamic-update-slice_fusion.21.grad.right_grad, bf16[2048,1536]{1,0:T(8,128)(2,1)} %get-tuple-element.209.right_h.h, ...), custom_call_target="tpu_custom_call" | custom-call | flops 7549747200 | bytes 30000000 | tf_op jit(solution)/shard_map/mlp_second/pallas_call | solution.py:1049
  288.4 17.0 %weight_grad.3 = bf16[4,1440,384]{2,1,0:T(8,128)(2,1)} custom-call(bf16[1440,1024]{1,0:T(8,128)(2,1)} %get-tuple-element.218.left_own, bf16[1440,1024]{1,0:T(8,128)(2,1)} %get-tuple-element.219.left_other, bf16[2048,1536]{1,0:T(8,128)(2,1)} %constant_dynamic-update-slice_fusion.21.grad.right_grad, bf16[2048,1536]{1,0:T(8,128)(2,1)} %get-tuple-element.209.right_h.h), custom_call_target="tpu_custom_call" | custom-call | flops 9059696640 | bytes 20000000 | tf_op jit(solution)/shard_map/weight_grad/pallas_call | solution.py:1013
  314.2 6.9 %mlp_down.3 = (bf16[512,1536]{1,0:T(8,128)(2,1)}, bf16[256,1536]{1,0:T(8,128)(2,1)}, bf16[256,1536]{1,0:T(8,128)(2,1)}) custom-call(bf16[1024,480]{1,0:T(8,128)(2,1)} %get-tuple-element.226.hid, bf16[1440,1536]{1,0:T(8,128)(2,1)} %all-gather.8.cloned.1.call-done.weights, bf16[2048,1536]{1,0:T(8,128)(2,1)} %get-tuple-element.215.refs_0_, ...), custom_call_target="tpu_custom_call" | custom-call | flops 1509949440 | bytes 10000000 | tf_op jit(solution)/shard_map/mlp_down/pallas_call | solution.py:1074
  322.7 12.1 %branch_back.1 = (f32[256,1536]{1,0:T(8,128)}, bf16[256,1536]{1,0:T(8,128)(2,1)}, f32[1,1536]{1,0:T(1,128)}, bf16[768,768]{1,0:T(8,128)(2,1)}, bf16[768,768]{1,0...) custom-call(s32[32]{0:T(128)} %mul.82.starts_a.starts, s32[32]{0:T(128)} %mul.84.starts_b, ...), custom_call_target="tpu_custom_call" | custom-call | flops 2415919104 | bytes 15000000 | tf_op jit(solution)/shard_map/branch_back/pallas_call | solution.py:1130
  340.6 5.7 %attend_back.2 = (bf16[128,1536]{1,0:T(8,128)(2,1)S(1)}, bf16[512,512]{1,0:T(8,128)(2,1)S(1)}, bf16[512,512]{1,0:T(8,128)(2,1)}) custom-call(bf16[256,1536]{1,0:T(8,128)(2,1)S(1)} %copy-done.13, bf16[256,1536]{1,0:T(8,128)(2,1)S(1)} %copy-done.14, f32[256,256]{1,0:T(8,128)S(1)} %copy-done.2, f32[2,1024,128]{2,1,0:T(8,128)S(1)} %or_select_fusion.barred, ...), custom_call_target="tpu_custom_call" | custom-call | flops 2013265920 | bytes 5000000 | tf_op jit(solution)/shard_map/attend_back/pallas_call | solution.py:1149
  352.2 6.1 %attend_back.3 = (bf16[128,1536]{1,0:T(8,128)(2,1)S(1)}, bf16[512,512]{1,0:T(8,128)(2,1)S(1)}, bf16[512,512]{1,0:T(8,128)(2,1)}) custom-call(bf16[256,1536]{1,0:T(8,128)(2,1)S(1)} %copy-done.13, bf16[256,1536]{1,0:T(8,128)(2,1)S(1)} %copy-done.14, f32[256,256]{1,0:T(8,128)S(1)} %copy-done.2, f32[2,1024,128]{2,1,0:T(8,128)S(1)} %or_select_fusion.barred, ...), custom_call_target="tpu_custom_call" | custom-call | flops 2013265920 | bytes 5000000 | tf_op jit(solution)/shard_map/attend_back/pallas_call | solution.py:1149
  361.9 10.2 %query_back.1 = (f32[256,1536]{1,0:T(8,128)}, f32[1,1536]{1,0:T(1,128)}, bf16[768,768]{1,0:T(8,128)(2,1)}, bf16[768,768]{1,0:T(8,128)(2,1)}, bf16[768,768]{1,0:T(8,128)(2,1)}, /*index=5*/bf16[768,768]{1,0:T(8,128)(2,1)}) custom-call(s32[32]{0:T(128)} %mul.82.starts_a.starts, s32[32]{0:T(128)} %mul.84.starts_b, bf16[128,1536]{1,0:T(8,128)(2,1)} %copy-done.27, ...), custom_call_target="tpu_custom_call" | custom-call | flops 2415919104 | bytes 12000000 | tf_op jit(solution)/shard_map/query_back/pallas_call | solution.py:1173
  387.9 6.4 %collective-permute-done.56.got_a = bf16[128,512]{1,0:T(8,128)(2,1)S(1)} collective-permute-done((bf16[128,512]{1,0:T(8,128)(2,1)S(1)}, bf16[128,512]{1,0:T(8,128)(2,1)S(1)}, u32[]{:S(2)}, u32[]{:S(2)}) %collective-permute-start.56) | collective-permute-done | bytes 131104 | tf_op jit(solution)/shard_map/ppermute | solution.py:297
  400.4 6.8 %kv_back.1 = (bf16[256,1536]{1,0:T(8,128)(2,1)}, bf16[768,640]{1,0:T(8,128)(2,1)S(1)}, bf16[768,640]{1,0:T(8,128)(2,1)S(1)}) custom-call(s32[32]{0:T(128)S(1)} %copy-done.11, bf16[128,512]{1,0:T(8,128)(2,1)S(1)} %get-tuple-element.269.keep_a, bf16[128,512]{1,0:T(8,128)(2,1)S(1)} %collective-permute-done.56.got_a, ...), custom_call_target="tpu_custom_call" | custom-call | flops 805306368 | bytes 10000000 | tf_op jit(solution)/shard_map/kv_back/pallas_call | solution.py:1195
  413.5 7.6 %collective-permute-done.61 = bf16[128,1536]{1,0:T(8,128)(2,1)S(1)} collective-permute-done((bf16[128,1536]{1,0:T(8,128)(2,1)S(1)}, bf16[128,1536]{1,0:T(8,128)(2,1)S(1)}, u32[]{:S(2)}, u32[]{:S(2)}) %collective-permute-start.61) | collective-permute-done | bytes 393248 | tf_op jit(solution)/shard_map/ppermute | solution.py:297
  439.0 7.0 %collective-permute-done.78 = bf16[48,1536]{1,0:T(8,128)(2,1)S(1)} collective-permute-done((bf16[48,1536]{1,0:T(8,128)(2,1)S(1)}, bf16[48,1536]{1,0:T(8,128)(2,1)S(1)}, u32[]{:S(2)}, u32[]{:S(2)}) %collective-permute-start.78) | collective-permute-done | bytes 147488 | tf_op jit(solution)/shard_map/ppermute | solution.py:328
  467.0 5.8 %collective-permute-done.75 = bf16[48,2176]{1,0:T(8,128)(2,1)S(1)} collective-permute-done((bf16[48,2176]{1,0:T(8,128)(2,1)S(1)}, bf16[48,2176]{1,0:T(8,128)(2,1)S(1)}, u32[]{:S(2)}, u32[]{:S(2)}) %collective-permute-start.75) | collective-permute-done | bytes 208928 | tf_op jit(solution)/shard_map/ppermute | solution.py:328
  (435 shorter events, 201.6 us)
Async XLA Ops:
  7.2 43.2 %all-gather.4.cloned.1.call-start = ((), (), s32[]{:S(2)}) async-start(), calls=%async_computation.2 | async-start | bytes 1781760 | tf_op jit(solution)/shard_map/all_gather | solution.py:854
  12.9 168.2 %all-gather.6.cloned.1.call-start = ((), (), s32[]{:S(2)}) async-start(), calls=%async_computation.3 | async-start | bytes 7372800 | tf_op jit(solution)/shard_map/all_gather | solution.py:889
  30.1 19.8 %collective-permute-start.6 = (bf16[256,1536]{1,0:T(8,128)(2,1)S(1)}, bf16[256,1536]{1,0:T(8,128)(2,1)}, u32[]{:S(2)}, u32[]{:S(2)}) collective-permute-start(bf16[256,1536]{1,0:T(8,128)(2,1)S(1)} %pad_maximum_fusion.5), channel_id=1, source_target_pairs={{0,2},{1,3},{2,0},{3,1},{4,6},{5,7},{6,4},{7,5},{8,10},{9,11},{10,... | collective-permute-start | bytes 2359304 | tf_op jit(solution)/shard_map/ppermute | solution.py:297
  30.6 19.5 %collective-permute-start.5 = (bf16[256,1536]{1,0:T(8,128)(2,1)S(1)}, bf16[256,1536]{1,0:T(8,128)(2,1)}, u32[]{:S(2)}, u32[]{:S(2)}) collective-permute-start(bf16[256,1536]{1,0:T(8,128)(2,1)S(1)} %pad_maximum_fusion.4), channel_id=1, source_target_pairs={{0,4},{1,5},{2,6},{3,7},{4,0},{5,1},{6,2},{7,3},{8,12},{9,13},{10,... | collective-permute-start | bytes 2359304 | tf_op jit(solution)/shard_map/ppermute | solution.py:297
  50.4 195.1 %all-gather.8.cloned.1.call-start = ((), (), s32[]{:S(2)}) async-start(), calls=%async_computation.4 | async-start | bytes 5529600 | tf_op jit(solution)/shard_map/all_gather | solution.py:978
  68.1 20.2 %collective-permute-start.9 = (bf16[384,1152]{1,0:T(8,128)(2,1)S(1)}, bf16[384,1152]{1,0:T(8,128)(2,1)S(1)}, u32[]{:S(2)}, u32[]{:S(2)}) collective-permute-start(bf16[384,1152]{1,0:T(8,128)(2,1)S(1)} %pad_maximum_fusion.2.refs_0_), channel_id=1, source_target_pairs={{0,4},{1,5},{2,6},{3,7},{4,0},{5,1},{6,2},{7,3},{8,12},{9,13},{10,... | collective-permute-start | bytes 2654216 | tf_op jit(solution)/shard_map/ppermute | solution.py:297
  69.6 22.4 %collective-permute-start.15 = (bf16[384,1152]{1,0:T(8,128)(2,1)S(1)}, bf16[384,1152]{1,0:T(8,128)(2,1)}, u32[]{:S(2)}, u32[]{:S(2)}) collective-permute-start(bf16[384,1152]{1,0:T(8,128)(2,1)S(1)} %pad_maximum_fusion.2.refs_0_), channel_id=1, source_target_pairs={{0,1},{1,0},{2,3},{3,2},{4,5},{5,4},{6,7},{7,6},{8,9},{9,8},{10,11... | collective-permute-start | bytes 2654216 | tf_op jit(solution)/shard_map/ppermute | solution.py:297
  90.2 19.3 %collective-permute-start.21 = (bf16[384,1024]{1,0:T(8,128)(2,1)}, bf16[384,1024]{1,0:T(8,128)(2,1)}, u32[]{:S(2)}, u32[]{:S(2)}) collective-permute-start(bf16[384,1024]{1,0:T(8,128)(2,1)} %copy-done.35), channel_id=1, source_target_pairs={{0,1},{1,0},{2,3},{3,2},{4,5},{5,4},{6,7},{7,6},{8,9},{9,8},{10,11... | collective-permute-start | bytes 2359304 | tf_op jit(solution)/shard_map/ppermute | solution.py:297
  109.5 20.0 %collective-permute-start.30 = (bf16[384,768]{1,0:T(8,128)(2,1)}, bf16[384,768]{1,0:T(8,128)(2,1)}, u32[]{:S(2)}, u32[]{:S(2)}) collective-permute-start(bf16[384,768]{1,0:T(8,128)(2,1)} %constant_dynamic-update-slice_fusion.33.refs_4_), channel_id=1, source_target_pairs={{0,2},{1,3},{2,0},{3,1},{4,6},{5,7},{6,4},{7,5},{8,10},{9,11},{10,... | collective-permute-start | bytes 1769480 | tf_op jit(solution)/shard_map/ppermute | solution.py:297
  110.1 19.4 %collective-permute-start.29 = (bf16[384,768]{1,0:T(8,128)(2,1)}, bf16[384,768]{1,0:T(8,128)(2,1)}, u32[]{:S(2)}, u32[]{:S(2)}) collective-permute-start(bf16[384,768]{1,0:T(8,128)(2,1)} %constant_dynamic-update-slice_fusion.31.refs_0_), channel_id=1, source_target_pairs={{0,4},{1,5},{2,6},{3,7},{4,0},{5,1},{6,2},{7,3},{8,12},{9,13},{10,... | collective-permute-start | bytes 1769480 | tf_op jit(solution)/shard_map/ppermute | solution.py:297
  154.6 205.5 %reduce-scatter.3.cloned.1.call-start = ((), (), s32[]{:S(2)}) async-start(), calls=%async_computation.5 | async-start | bytes 7372800 | tf_op jit(solution)/shard_map/reduce_scatter | solution.py:1027
  238.3 215.2 %reduce-scatter.5.cloned.1.call-start = ((), (), s32[]{:S(2)}) async-start(), calls=%async_computation.6 | async-start | bytes 5529600 | tf_op jit(solution)/shard_map/reduce_scatter | solution.py:1027
  266.8 47.4 %collective-permute-start.46 = (bf16[1024,1536]{1,0:T(8,128)(2,1)}, bf16[1024,1536]{1,0:T(8,128)(2,1)}, u32[]{:S(2)}, u32[]{:S(2)}) collective-permute-start(bf16[1024,1536]{1,0:T(8,128)(2,1)} %mlp_down.2), channel_id=1, source_target_pairs={{0,1},{1,0},{2,3},{3,2},{4,5},{5,4},{6,7},{7,6},{8,9},{9,8},{10,11... | collective-permute-start | bytes 9437192 | tf_op jit(solution)/shard_map/ppermute | solution.py:297
  285.4 20.0 %collective-permute-start.44 = (bf16[256,1536]{1,0:T(8,128)(2,1)}, bf16[256,1536]{1,0:T(8,128)(2,1)S(1)}, u32[]{:S(2)}, u32[]{:S(2)}) collective-permute-start(bf16[256,1536]{1,0:T(8,128)(2,1)} %get-tuple-element.221), channel_id=1, source_target_pairs={{0,4},{1,5},{2,6},{3,7},{4,0},{5,1},{6,2},{7,3},{8,12},{9,13},{10,... | collective-permute-start | bytes 2359304 | tf_op jit(solution)/shard_map/ppermute | solution.py:297
  286.9 19.6 %collective-permute-start.45 = (bf16[256,1536]{1,0:T(8,128)(2,1)}, bf16[256,1536]{1,0:T(8,128)(2,1)}, u32[]{:S(2)}, u32[]{:S(2)}) collective-permute-start(bf16[256,1536]{1,0:T(8,128)(2,1)} %get-tuple-element.222), channel_id=1, source_target_pairs={{0,2},{1,3},{2,0},{3,1},{4,6},{5,7},{6,4},{7,5},{8,10},{9,11},{10,... | collective-permute-start | bytes 2359304 | tf_op jit(solution)/shard_map/ppermute | solution.py:297
  335.4 36.7 %collective-permute-start.49 = (bf16[256,1536]{1,0:T(8,128)(2,1)}, bf16[256,1536]{1,0:T(8,128)(2,1)}, u32[]{:S(2)}, u32[]{:S(2)}) collective-permute-start(bf16[256,1536]{1,0:T(8,128)(2,1)} %get-tuple-element.233), channel_id=1, source_target_pairs={{0,4},{1,5},{2,6},{3,7},{4,0},{5,1},{6,2},{7,3},{8,12},{9,13},{10,... | collective-permute-start | bytes 2359304 | tf_op jit(solution)/shard_map/ppermute | solution.py:297
  336.3 36.1 %collective-permute-start.50 = (bf16[256,1536]{1,0:T(8,128)(2,1)}, bf16[256,1536]{1,0:T(8,128)(2,1)}, u32[]{:S(2)}, u32[]{:S(2)}) collective-permute-start(bf16[256,1536]{1,0:T(8,128)(2,1)} %get-tuple-element.234), channel_id=1, source_target_pairs={{0,2},{1,3},{2,0},{3,1},{4,6},{5,7},{6,4},{7,5},{8,10},{9,11},{10,... | collective-permute-start | bytes 2359304 | tf_op jit(solution)/shard_map/ppermute | solution.py:297
  349.1 23.6 %collective-permute-start.64 = (bf16[384,768]{1,0:T(8,128)(2,1)}, bf16[384,768]{1,0:T(8,128)(2,1)}, u32[]{:S(2)}, u32[]{:S(2)}) collective-permute-start(bf16[384,768]{1,0:T(8,128)(2,1)} %get-tuple-element.330), channel_id=1, source_target_pairs={{0,4},{1,5},{2,6},{3,7},{4,0},{5,1},{6,2},{7,3},{8,12},{9,13},{10,... | collective-permute-start | bytes 1769480 | tf_op jit(solution)/shard_map/ppermute | solution.py:297
  359.1 20.0 %collective-permute-start.54 = (bf16[512,512]{1,0:T(8,128)(2,1)}, bf16[512,512]{1,0:T(8,128)(2,1)}, u32[]{:S(2)}, u32[]{:S(2)}) collective-permute-start(bf16[512,512]{1,0:T(8,128)(2,1)} %get-tuple-element.267), channel_id=1, source_target_pairs={{0,1},{1,0},{2,3},{3,2},{4,5},{5,4},{6,7},{7,6},{8,9},{9,8},{10,11... | collective-permute-start | bytes 1572872 | tf_op jit(solution)/shard_map/ppermute | solution.py:297
  372.1 22.2 %collective-permute-start.57 = (bf16[768,768]{1,0:T(8,128)(2,1)}, bf16[768,768]{1,0:T(8,128)(2,1)S(1)}, u32[]{:S(2)}, u32[]{:S(2)}) collective-permute-start(bf16[768,768]{1,0:T(8,128)(2,1)} %get-tuple-element.273), channel_id=1, source_target_pairs={{0,1},{1,0},{2,3},{3,2},{4,5},{5,4},{6,7},{7,6},{8,9},{9,8},{10,11... | collective-permute-start | bytes 3538952 | tf_op jit(solution)/shard_map/ppermute | solution.py:297
  372.4 22.3 %collective-permute-start.58 = (bf16[768,768]{1,0:T(8,128)(2,1)}, bf16[768,768]{1,0:T(8,128)(2,1)S(1)}, u32[]{:S(2)}, u32[]{:S(2)}) collective-permute-start(bf16[768,768]{1,0:T(8,128)(2,1)} %get-tuple-element.275), channel_id=1, source_target_pairs={{0,1},{1,0},{2,3},{3,2},{4,5},{5,4},{6,7},{7,6},{8,9},{9,8},{10,11... | collective-permute-start | bytes 3538952 | tf_op jit(solution)/shard_map/ppermute | solution.py:297
  410.6 20.5 %collective-permute-start.68 = (bf16[384,768]{1,0:T(8,128)(2,1)S(1)}, bf16[384,768]{1,0:T(8,128)(2,1)S(1)}, u32[]{:S(2)}, u32[]{:S(2)}) collective-permute-start(bf16[384,768]{1,0:T(8,128)(2,1)S(1)} %get-tuple-element.326), channel_id=1, source_target_pairs={{0,4},{1,5},{2,6},{3,7},{4,0},{5,1},{6,2},{7,3},{8,12},{9,13},{10,... | collective-permute-start | bytes 1769480 | tf_op jit(solution)/shard_map/ppermute | solution.py:297
  411.9 19.2 %collective-permute-start.69 = (bf16[384,768]{1,0:T(8,128)(2,1)S(1)}, bf16[384,768]{1,0:T(8,128)(2,1)S(1)}, u32[]{:S(2)}, u32[]{:S(2)}) collective-permute-start(bf16[384,768]{1,0:T(8,128)(2,1)S(1)} %get-tuple-element.324), channel_id=1, source_target_pairs={{0,2},{1,3},{2,0},{3,1},{4,6},{5,7},{6,4},{7,5},{8,10},{9,11},{10,... | collective-permute-start | bytes 1769480 | tf_op jit(solution)/shard_map/ppermute | solution.py:297
  425.2 20.9 %collective-permute-start.78 = (bf16[48,1536]{1,0:T(8,128)(2,1)S(1)}, bf16[48,1536]{1,0:T(8,128)(2,1)S(1)}, u32[]{:S(2)}, u32[]{:S(2)}) collective-permute-start(bf16[48,1536]{1,0:T(8,128)(2,1)S(1)} %get-tuple-element.354), channel_id=1, source_target_pairs={{0,16},{8,24},{16,0},{24,8},{1,17},{9,25},{17,1},{25,9},{2,18},{10... | collective-permute-start | bytes 442376 | tf_op jit(solution)/shard_map/ppermute | solution.py:328
  (128 other events, 1068.1 us)
Sparse Core Ops, SparseCore 0:
  13.0 37.3 all-gather.3
  52.6 107.9 all-gather.5
  162.8 82.7 all-gather.7
  247.8 102.9 reduce-scatter.2
  352.9 88.9 reduce-scatter.4
